TPU v7x, 128 devices: a whole 4x4x4 slice. The times are simulated.
128 devices in a mesh: fsdp: 2 (over y_lo), ctx: 16 (over y_hi, x, core), tp: 4 (over z).
Axes of the slice: x: 4, y: 4 (y_hi: 2, y_lo: 2; y = y_hi * 2 + y_lo), z: 4, core: 2. Of those that a mesh axis runs over, the one named last changes fastest.
Arguments:
- tokens: bfloat16 [4096, 2048], P(('fsdp', 'ctx')), may hold values from -6 to 6
- lengths: int32 [2, 3], P('fsdp'), may hold values from 1 to 1920, as said below
- routes: int32 [4096, 6], P(('fsdp', 'ctx')), may hold values from 0 to 7, all different within a row
- cotangent: bfloat16 [4096, 2048], P(('fsdp', 'ctx')), may hold values from -6 to 6
- attn_gain: bfloat16 [2048], P(('fsdp', 'ctx')), may hold values from 0.5 to 1.5
- w_query: bfloat16 [2048, 3072], P(('fsdp', 'ctx'), 'tp'), may hold values from -0.125 to 0.125
- w_latent: bfloat16 [2048, 576], P(('fsdp', 'ctx')), may hold values from -0.125 to 0.125
- latent_gain: bfloat16 [512], P(('fsdp', 'ctx')), may hold values from 0.5 to 1.5
- w_expand: bfloat16 [512, 4096], P(('fsdp', 'ctx'), 'tp'), may hold values from -0.25 to 0.25
- w_out: bfloat16 [2048, 2048], P('tp', ('fsdp', 'ctx')), may hold values from -3 to 3
- moe_gain: bfloat16 [2048], P(('fsdp', 'ctx')), may hold values from 0.5 to 1.5
- w_router: bfloat16 [2048, 8], P(('fsdp', 'ctx')), may hold values from -0.0625 to 0.0625
- w_gate: bfloat16 [8, 2048, 1408], P(None, ('fsdp', 'ctx'), 'tp'), may hold values from -0.125 to 0.125
- w_up: bfloat16 [8, 2048, 1408], P(None, ('fsdp', 'ctx'), 'tp'), may hold values from -0.125 to 0.125
- w_down: bfloat16 [8, 1408, 2048], P(None, 'tp', ('fsdp', 'ctx')), may hold values from -0.15625 to 0.15625
- shared_gate: bfloat16 [2048, 2816], P(('fsdp', 'ctx'), 'tp'), may hold values from -0.125 to 0.125
- shared_up: bfloat16 [2048, 2816], P(('fsdp', 'ctx'), 'tp'), may hold values from -0.125 to 0.125
- shared_down: bfloat16 [2816, 2048], P('tp', ('fsdp', 'ctx')), may hold values from -0.109375 to 0.109375
Outputs:
- output: bfloat16 [4096, 2048], P(('fsdp', 'ctx'))
- d_tokens: float32 [4096, 2048], P(('fsdp', 'ctx'))
- d_attn_gain: float32 [2048], P(('fsdp', 'ctx'))
- d_w_query: float32 [2048, 3072], P(('fsdp', 'ctx'), 'tp')
- d_w_latent: float32 [2048, 576], P(('fsdp', 'ctx'))
- d_latent_gain: float32 [512], P(('fsdp', 'ctx'))
- d_w_expand: float32 [512, 4096], P(('fsdp', 'ctx'), 'tp')
- d_w_out: float32 [2048, 2048], P('tp', ('fsdp', 'ctx'))
- d_moe_gain: float32 [2048], P(('fsdp', 'ctx'))
- d_w_router: float32 [2048, 8], P(('fsdp', 'ctx'))
- d_w_gate: float32 [8, 2048, 1408], P(None, ('fsdp', 'ctx'), 'tp')
- d_w_up: float32 [8, 2048, 1408], P(None, ('fsdp', 'ctx'), 'tp')
- d_w_down: float32 [8, 1408, 2048], P(None, 'tp', ('fsdp', 'ctx'))
- d_shared_gate: float32 [2048, 2816], P(('fsdp', 'ctx'), 'tp')
- d_shared_up: float32 [2048, 2816], P(('fsdp', 'ctx'), 'tp')
- d_shared_down: float32 [2816, 2048], P('tp', ('fsdp', 'ctx'))
Inputs may be any that keep to these rules, and one draw needn't show every extreme that they name: `lengths`: in each row the first and the last document are shorter than 128 and the middle one has 1920 positions; a row sums to 2048. `routes`: each row names 6 different experts.
All inputs are finite; a program needn't handle non-finite values.
Results may differ from a plain program's by a relative error of at most 0.035.
Values may be sent and summed in bfloat16 or wider, within the bound.
No kernel may reach another device: no remote copies, remote signals or barrier semaphores. Data moves between devices by JAX's collectives and lax.ppermute only.
A program may use at most 192 MiB of HBM per device.

v0:
```python
import jax
import jax.numpy as jnp
from jax import lax
from jax.sharding import PartitionSpec as P

NOPE = 128
ROPE = 64
VD = 128
R = 512
E = 8


epsilon = 1e-06
rope_base = 50000.0
route_scale = 2.446
highest = lax.Precision.HIGHEST


def rms_parts(values):
    inverse = lax.rsqrt(jnp.mean(values * values, axis=-1, keepdims=True) + epsilon)
    return (values * inverse, inverse)


def norm_back(grad_normed, unit_rows, inverse, gain_vec):
    scaled = grad_normed * gain_vec
    grad_gain = jnp.sum(grad_normed * unit_rows, axis=0)
    grad_in = inverse * (scaled - unit_rows * jnp.mean(scaled * unit_rows, axis=-1, keepdims=True))
    return (grad_in, grad_gain)


def rotary(values, cosine, sine_part):
    half_width = values.shape[-1] // 2
    front_half = values[..., :half_width]
    back_half = values[..., half_width:]
    return jnp.concatenate(
        [front_half * cosine - back_half * sine_part, back_half * cosine + front_half * sine_part],
        axis=-1,
    )


def angle_tables(within, half_width):
    frequency = rope_base ** (-jnp.arange(half_width, dtype=jnp.float32) / half_width)
    angles = within.astype(jnp.float32)[:, None] * frequency[None, :]
    return (jnp.cos(angles), jnp.sin(angles))


def doc_layout(doc_lengths, pack_len):
    doc_ends = jnp.cumsum(doc_lengths)
    positions = jnp.arange(pack_len, dtype=jnp.int32)
    doc_ids = jnp.sum((positions[:, None] >= doc_ends[None, :-1]).astype(jnp.int32), axis=1)
    doc_starts = doc_ends - doc_lengths
    belongs = doc_ids[:, None] == jnp.arange(doc_lengths.shape[0], dtype=jnp.int32)[None, :]
    doc_first = jnp.sum(jnp.where(belongs, doc_starts[None, :], 0), axis=1)
    return (doc_ids, positions, positions - doc_first)


def swiglu_back(gate_pre, up_pre, grad_act):
    sigmoid_gate = jax.nn.sigmoid(gate_pre)
    slope = sigmoid_gate * (1.0 + gate_pre * (1.0 - sigmoid_gate))
    grad_gate = (grad_act * up_pre * slope).astype(jnp.bfloat16)
    grad_up = (grad_act * gate_pre * sigmoid_gate).astype(jnp.bfloat16)
    return (grad_gate, grad_up)


def shards(
    tokens,
    lengths,
    routes,
    cotangent,
    attn_gain,
    w_query,
    w_latent,
    latent_gain,
    w_expand,
    w_out,
    moe_gain,
    w_router,
    w_gate,
    w_up,
    w_down,
    shared_gate,
    shared_up,
    shared_down,
):
    row_count = tokens.shape[0]
    pack_len = row_count * lax.axis_size("ctx")
    doc_ids, positions, within_all = doc_layout(lengths[0], pack_len)
    offset = lax.axis_index("ctx") * row_count
    own_docs = lax.dynamic_slice_in_dim(doc_ids, offset, row_count, 0)
    own_places = lax.dynamic_slice_in_dim(positions, offset, row_count, 0)
    own_within = lax.dynamic_slice_in_dim(within_all, offset, row_count, 0)
    cosine, sine_part = angle_tables(own_within, ROPE // 2)
    gathered_set = (
        lax.all_gather(attn_gain, ("fsdp", "ctx"), axis=0, tiled=True),
        lax.all_gather(w_query, ("fsdp", "ctx"), axis=0, tiled=True),
        lax.all_gather(w_latent, ("fsdp", "ctx"), axis=0, tiled=True),
        lax.all_gather(latent_gain, ("fsdp", "ctx"), axis=0, tiled=True),
        lax.all_gather(w_expand, ("fsdp", "ctx"), axis=0, tiled=True),
        lax.all_gather(w_out, ("fsdp", "ctx"), axis=1, tiled=True),
        lax.all_gather(moe_gain, ("fsdp", "ctx"), axis=0, tiled=True),
        lax.all_gather(w_router, ("fsdp", "ctx"), axis=0, tiled=True),
        lax.all_gather(shared_gate, ("fsdp", "ctx"), axis=0, tiled=True),
        lax.all_gather(shared_up, ("fsdp", "ctx"), axis=0, tiled=True),
        lax.all_gather(shared_down, ("fsdp", "ctx"), axis=1, tiled=True),
        lax.all_gather(w_gate, ("fsdp", "ctx"), axis=1, tiled=True),
        lax.all_gather(w_up, ("fsdp", "ctx"), axis=1, tiled=True),
        lax.all_gather(w_down, ("fsdp", "ctx"), axis=2, tiled=True),
    )
    gate_weight, up_weight, down_weight = (gathered_set[11], gathered_set[12], gathered_set[13])
    gain_attn, query_weight, latent_weight, gain_latent, expand_weight, out_weight = gathered_set[
        :6
    ]
    gain_moe, router_weight, shared_gate_w, shared_up_w, shared_down_w = gathered_set[6:11]
    residual_in = tokens.astype(jnp.float32)
    unit_attn, scale_attn = rms_parts(residual_in)
    hidden = (unit_attn * gain_attn.astype(jnp.float32)).astype(jnp.bfloat16)
    local_heads = query_weight.shape[1] // (NOPE + ROPE)
    query_raw = jnp.dot(hidden, query_weight, preferred_element_type=jnp.float32).reshape(
        row_count, local_heads, NOPE + ROPE
    )
    queries = jnp.concatenate(
        [query_raw[..., :NOPE], rotary(query_raw[..., NOPE:], cosine[:, None], sine_part[:, None])],
        axis=-1,
    ).astype(jnp.bfloat16)
    latent = jnp.dot(hidden, latent_weight, preferred_element_type=jnp.float32)
    unit_latent, scale_latent = rms_parts(latent[:, :R])
    compact = unit_latent * gain_latent.astype(jnp.float32)
    key_rot = rotary(latent[:, R:], cosine, sine_part)
    own_keys = jnp.concatenate([compact, key_rot], axis=-1).astype(jnp.bfloat16)
    key_rows = lax.all_gather(own_keys, "ctx", axis=0, tiled=True)
    expand = expand_weight.reshape(R, local_heads, NOPE + VD)
    key_weight = expand[..., :NOPE]
    value_weight = expand[..., NOPE:]
    absorbed = jnp.einsum(
        "thn,rhn->thr", queries[..., :NOPE], key_weight, preferred_element_type=jnp.float32
    ).astype(jnp.bfloat16)
    query_cat = jnp.concatenate([absorbed, queries[..., NOPE:]], axis=-1)
    score_scale = (NOPE + ROPE) ** (-0.5)
    allowed = (own_docs[:, None] == doc_ids[None, :]) & (positions[None, :] <= own_places[:, None])

    def masked_scores():
        scores = score_scale * jnp.einsum(
            "thc,kc->htk", query_cat, key_rows, preferred_element_type=jnp.float32
        )
        return jnp.where(allowed[None], scores, -1e30)

    scores = masked_scores()
    row_max = jnp.max(scores, axis=-1, keepdims=True)
    log_total = row_max + jnp.log(jnp.sum(jnp.exp(scores - row_max), axis=-1, keepdims=True))
    probs_low = jnp.exp(scores - log_total).astype(jnp.bfloat16)
    mixture = jnp.einsum(
        "htk,kr->thr", probs_low, key_rows[:, :R], preferred_element_type=jnp.float32
    ).astype(jnp.bfloat16)
    head_out = (
        jnp.einsum("thr,rhv->thv", mixture, value_weight, preferred_element_type=jnp.float32)
        .astype(jnp.bfloat16)
        .reshape(row_count, local_heads * VD)
    )
    attention = lax.psum(jnp.dot(head_out, out_weight, preferred_element_type=jnp.float32), "tp")
    middle = residual_in + attention
    unit_moe, scale_moe = rms_parts(middle)
    normed = (unit_moe * gain_moe.astype(jnp.float32)).astype(jnp.bfloat16)
    router_sig = jax.nn.sigmoid(jnp.dot(normed, router_weight, preferred_element_type=jnp.float32))
    picked = jnp.sum(
        (routes[:, :, None] == jnp.arange(E, dtype=jnp.int32)[None, None, :]).astype(jnp.float32),
        axis=1,
    )
    weighted = router_sig * picked
    gate_total = jnp.sum(weighted, axis=1, keepdims=True)
    gate_values = route_scale * weighted / gate_total
    grad_out = cotangent.astype(jnp.float32)
    grad_expert = (gate_values.T[:, :, None] * grad_out[None]).astype(jnp.bfloat16)
    gate_pre = jnp.einsum("td,edf->etf", normed, gate_weight, preferred_element_type=jnp.float32)
    up_pre = jnp.einsum("td,edf->etf", normed, up_weight, preferred_element_type=jnp.float32)
    hidden_act = (jax.nn.silu(gate_pre) * up_pre).astype(jnp.bfloat16)
    expert_rows = jnp.einsum(
        "etf,efd->etd", hidden_act, down_weight, preferred_element_type=jnp.float32
    )
    d_down = jnp.einsum("etf,etd->efd", hidden_act, grad_expert, preferred_element_type=jnp.float32)
    grad_act = jnp.einsum(
        "etd,efd->etf", grad_expert, down_weight, preferred_element_type=jnp.float32
    )
    grad_gate_pre, grad_up_pre = swiglu_back(gate_pre, up_pre, grad_act)
    d_gate = jnp.einsum("td,etf->edf", normed, grad_gate_pre, preferred_element_type=jnp.float32)
    d_up = jnp.einsum("td,etf->edf", normed, grad_up_pre, preferred_element_type=jnp.float32)
    grad_normed = jnp.einsum(
        "etf,edf->td", grad_gate_pre, gate_weight, preferred_element_type=jnp.float32
    )
    grad_normed = grad_normed + jnp.einsum(
        "etf,edf->td", grad_up_pre, up_weight, preferred_element_type=jnp.float32
    )
    shared_gate_pre = jnp.dot(normed, shared_gate_w, preferred_element_type=jnp.float32)
    shared_up_pre = jnp.dot(normed, shared_up_w, preferred_element_type=jnp.float32)
    shared_act = (jax.nn.silu(shared_gate_pre) * shared_up_pre).astype(jnp.bfloat16)
    shared_row = jnp.dot(shared_act, shared_down_w, preferred_element_type=jnp.float32)
    expert_part = jnp.sum(gate_values.T[:, :, None] * expert_rows, axis=0) + shared_row
    expert_sum = lax.psum(expert_part.astype(jnp.bfloat16), "tp").astype(jnp.float32)
    output = (middle + expert_sum).astype(jnp.bfloat16)
    grad_gates_part = jnp.sum(grad_out[None] * expert_rows, axis=-1).T
    grad_shared = grad_out.astype(jnp.bfloat16)
    d_shared_down = jnp.dot(shared_act.T, grad_shared, preferred_element_type=jnp.float32)
    grad_shared_act = jnp.dot(grad_shared, shared_down_w.T, preferred_element_type=jnp.float32)
    grad_shared_gate, grad_shared_up = swiglu_back(shared_gate_pre, shared_up_pre, grad_shared_act)
    d_shared_gate = jnp.dot(normed.T, grad_shared_gate, preferred_element_type=jnp.float32)
    d_shared_up = jnp.dot(normed.T, grad_shared_up, preferred_element_type=jnp.float32)
    grad_normed = grad_normed + jnp.dot(
        grad_shared_gate, shared_gate_w.T, preferred_element_type=jnp.float32
    )
    grad_normed = grad_normed + jnp.dot(
        grad_shared_up, shared_up_w.T, preferred_element_type=jnp.float32
    )
    grad_normed, grad_gates = lax.psum((grad_normed, grad_gates_part), "tp")
    grad_weighted = (
        route_scale * grad_gates - jnp.sum(grad_gates * gate_values, axis=1, keepdims=True)
    ) / gate_total
    grad_logits = grad_weighted * picked * router_sig * (1.0 - router_sig)
    d_router = jnp.dot(normed.astype(jnp.float32).T, grad_logits, precision=highest)
    grad_normed = grad_normed + jnp.dot(
        grad_logits, router_weight.astype(jnp.float32).T, precision=highest
    )
    grad_middle_norm, d_gain_moe = norm_back(
        grad_normed, unit_moe, scale_moe, gain_moe.astype(jnp.float32)
    )
    grad_middle = grad_out + grad_middle_norm
    attn_set = (
        lax.all_gather(attn_gain, ("fsdp", "ctx"), axis=0, tiled=True),
        lax.all_gather(w_query, ("fsdp", "ctx"), axis=0, tiled=True),
        lax.all_gather(w_latent, ("fsdp", "ctx"), axis=0, tiled=True),
        lax.all_gather(latent_gain, ("fsdp", "ctx"), axis=0, tiled=True),
        lax.all_gather(w_expand, ("fsdp", "ctx"), axis=0, tiled=True),
        lax.all_gather(w_out, ("fsdp", "ctx"), axis=1, tiled=True),
    )
    gain_attn, query_weight, latent_weight, gain_latent, expand_weight, out_weight = attn_set
    expand = expand_weight.reshape(R, local_heads, NOPE + VD)
    key_weight = expand[..., :NOPE]
    value_weight = expand[..., NOPE:]
    grad_attention = grad_middle.astype(jnp.bfloat16)
    d_out = jnp.dot(head_out.T, grad_attention, preferred_element_type=jnp.float32)
    grad_heads = (
        jnp.dot(grad_attention, out_weight.T, preferred_element_type=jnp.float32)
        .astype(jnp.bfloat16)
        .reshape(row_count, local_heads, VD)
    )
    d_value = jnp.einsum("thr,thv->rhv", mixture, grad_heads, preferred_element_type=jnp.float32)
    grad_mixture = jnp.einsum(
        "thv,rhv->thr", grad_heads, value_weight, preferred_element_type=jnp.float32
    ).astype(jnp.bfloat16)
    probs = jnp.exp(masked_scores() - log_total)
    grad_probs = jnp.einsum(
        "thr,kr->htk", grad_mixture, key_rows[:, :R], preferred_element_type=jnp.float32
    )
    grad_scores = (
        probs * (grad_probs - jnp.sum(probs * grad_probs, axis=-1, keepdims=True))
    ).astype(jnp.bfloat16)
    grad_keys_latent = jnp.einsum(
        "htk,thr->kr", probs_low, grad_mixture, preferred_element_type=jnp.float32
    )
    grad_query_cat = score_scale * jnp.einsum(
        "htk,kc->thc", grad_scores, key_rows, preferred_element_type=jnp.float32
    )
    grad_keys = score_scale * jnp.einsum(
        "htk,thc->kc", grad_scores, query_cat, preferred_element_type=jnp.float32
    )
    grad_keys = grad_keys + jnp.concatenate(
        [grad_keys_latent, jnp.zeros((pack_len, ROPE), jnp.float32)], axis=-1
    )
    grad_absorbed = grad_query_cat[..., :R].astype(jnp.bfloat16)
    d_key = jnp.einsum(
        "thn,thr->rhn", queries[..., :NOPE], grad_absorbed, preferred_element_type=jnp.float32
    )
    grad_nope = jnp.einsum(
        "thr,rhn->thn", grad_absorbed, key_weight, preferred_element_type=jnp.float32
    )
    grad_rope = rotary(grad_query_cat[..., R:], cosine[:, None], -sine_part[:, None])
    grad_queries = (
        jnp.concatenate([grad_nope, grad_rope], axis=-1)
        .astype(jnp.bfloat16)
        .reshape(row_count, local_heads * (NOPE + ROPE))
    )
    d_query = jnp.dot(hidden.T, grad_queries, preferred_element_type=jnp.float32)
    grad_hidden_part = jnp.dot(grad_queries, query_weight.T, preferred_element_type=jnp.float32)
    own_key_grads = lax.psum_scatter(
        grad_keys.astype(jnp.bfloat16), "ctx", scatter_dimension=0, tiled=True
    ).astype(jnp.float32)
    own_key_grads, grad_hidden_part = (
        lax.psum(own_key_grads.astype(jnp.bfloat16), "tp").astype(jnp.float32),
        lax.psum(grad_hidden_part.astype(jnp.bfloat16), "tp").astype(jnp.float32),
    )
    grad_compact_in, d_gain_latent = norm_back(
        own_key_grads[:, :R], unit_latent, scale_latent, gain_latent.astype(jnp.float32)
    )
    grad_key_rot = rotary(own_key_grads[:, R:], cosine, -sine_part)
    grad_latent = jnp.concatenate([grad_compact_in, grad_key_rot], axis=-1).astype(jnp.bfloat16)
    d_latent = jnp.dot(hidden.T, grad_latent, preferred_element_type=jnp.float32)
    grad_hidden = grad_hidden_part + jnp.dot(
        grad_latent, latent_weight.T, preferred_element_type=jnp.float32
    )
    grad_input_norm, d_gain_attn = norm_back(
        grad_hidden, unit_attn, scale_attn, gain_attn.astype(jnp.float32)
    )
    grad_tokens = grad_middle + grad_input_norm
    d_expand = jnp.concatenate([d_key, d_value], axis=-1).reshape(R, local_heads * (NOPE + VD))
    owned = (
        lax.psum_scatter(
            d_gain_attn.astype(jnp.bfloat16), ("fsdp", "ctx"), scatter_dimension=0, tiled=True
        ).astype(jnp.float32),
        lax.psum_scatter(
            d_query.astype(jnp.bfloat16), ("fsdp", "ctx"), scatter_dimension=0, tiled=True
        ).astype(jnp.float32),
        lax.psum_scatter(
            d_latent.astype(jnp.bfloat16), ("fsdp", "ctx"), scatter_dimension=0, tiled=True
        ).astype(jnp.float32),
        lax.psum_scatter(
            d_gain_latent.astype(jnp.bfloat16), ("fsdp", "ctx"), scatter_dimension=0, tiled=True
        ).astype(jnp.float32),
        lax.psum_scatter(
            d_expand.astype(jnp.bfloat16), ("fsdp", "ctx"), scatter_dimension=0, tiled=True
        ).astype(jnp.float32),
        lax.psum_scatter(
            d_out.astype(jnp.bfloat16), ("fsdp", "ctx"), scatter_dimension=1, tiled=True
        ).astype(jnp.float32),
        lax.psum_scatter(
            d_gain_moe.astype(jnp.bfloat16), ("fsdp", "ctx"), scatter_dimension=0, tiled=True
        ).astype(jnp.float32),
        lax.psum_scatter(
            d_router.astype(jnp.bfloat16), ("fsdp", "ctx"), scatter_dimension=0, tiled=True
        ).astype(jnp.float32),
        lax.psum_scatter(
            d_shared_gate.astype(jnp.bfloat16), ("fsdp", "ctx"), scatter_dimension=0, tiled=True
        ).astype(jnp.float32),
        lax.psum_scatter(
            d_shared_up.astype(jnp.bfloat16), ("fsdp", "ctx"), scatter_dimension=0, tiled=True
        ).astype(jnp.float32),
        lax.psum_scatter(
            d_shared_down.astype(jnp.bfloat16), ("fsdp", "ctx"), scatter_dimension=1, tiled=True
        ).astype(jnp.float32),
        lax.psum_scatter(
            d_gate.astype(jnp.bfloat16), ("fsdp", "ctx"), scatter_dimension=1, tiled=True
        ).astype(jnp.float32),
        lax.psum_scatter(
            d_up.astype(jnp.bfloat16), ("fsdp", "ctx"), scatter_dimension=1, tiled=True
        ).astype(jnp.float32),
        lax.psum_scatter(
            d_down.astype(jnp.bfloat16), ("fsdp", "ctx"), scatter_dimension=2, tiled=True
        ).astype(jnp.float32),
    )
    d_gate, d_up, d_down = (owned[11], owned[12], owned[13])
    return (
        output,
        grad_tokens,
        owned[0],
        owned[1],
        owned[2],
        owned[3],
        owned[4],
        owned[5],
        owned[6],
        owned[7],
        d_gate,
        d_up,
        d_down,
        owned[8],
        owned[9],
        owned[10],
    )


def solution(mesh):
    placed = (
        P(("fsdp", "ctx"), None),
        P("fsdp", None),
        P(("fsdp", "ctx"), None),
        P(("fsdp", "ctx"), None),
        P(("fsdp", "ctx")),
        P(("fsdp", "ctx"), "tp"),
        P(("fsdp", "ctx"), None),
        P(("fsdp", "ctx")),
        P(("fsdp", "ctx"), "tp"),
        P("tp", ("fsdp", "ctx")),
        P(("fsdp", "ctx")),
        P(("fsdp", "ctx"), None),
        P(None, ("fsdp", "ctx"), "tp"),
        P(None, ("fsdp", "ctx"), "tp"),
        P(None, "tp", ("fsdp", "ctx")),
        P(("fsdp", "ctx"), "tp"),
        P(("fsdp", "ctx"), "tp"),
        P("tp", ("fsdp", "ctx")),
    )
    return jax.shard_map(
        shards,
        mesh=mesh,
        in_specs=placed,
        out_specs=(
            P(("fsdp", "ctx"), None),
            P(("fsdp", "ctx"), None),
            P(("fsdp", "ctx")),
            P(("fsdp", "ctx"), "tp"),
            P(("fsdp", "ctx"), None),
            P(("fsdp", "ctx")),
            P(("fsdp", "ctx"), "tp"),
            P("tp", ("fsdp", "ctx")),
            P(("fsdp", "ctx")),
            P(("fsdp", "ctx"), None),
            P(None, ("fsdp", "ctx"), "tp"),
            P(None, ("fsdp", "ctx"), "tp"),
            P(None, "tp", ("fsdp", "ctx")),
            P(("fsdp", "ctx"), "tp"),
            P(("fsdp", "ctx"), "tp"),
            P("tp", ("fsdp", "ctx")),
        ),
        check_vma=False,
    )
```

profile of v0, /device:TPU:0, one launch (start us, length us, event | category | flops | bytes accessed | tf_op | source)
XLA Modules:
  0.0 2583.4 jit_solution(13386291911186159419)
XLA Ops:
  14.6 70.0 %all-reduce.8 = (bf16[2048]{0:T(1024)(128)(2,1)S(1)}, bf16[512]{0:T(512)(128)(2,1)S(1)}, bf16[2048]{0:T(1024)(128)(2,1)}) all-reduce(bf16[2048]{0:T(1024)(128)(2,1)S(1)} %dynamic-update-slice, bf16[512]{0:T(512)(128)(2,1)S(1)} %dynamic-update-slice.1, ...), channel_id=1, replica_groups=mesh['fsdp'=2,'ctx'=16,'tp'=4] {'fsdp','ctx'}, use_global_device_ids=true, to_apply=%add.1 | all-reduce | flops 4608 | bytes 18432
  87.7 3.1 fusion.84
  92.9 34.3 %all-gather.19.cloned.1.call-done = bf16[512,1024]{1,0:T(8,128)(2,1)} async-done(((bf16[16,1024]{1,0:T(8,128)(2,1)}), bf16[512,1024]{1,0:T(8,128)(2,1)}) %all-gather.19.cloned.1.call-update) | async-done | bytes 1048592 | tf_op jit(solution)/shard_map/all_gather | solution.py:98
  128.8 58.3 %all-gather.17.cloned.1.call-done = bf16[2048,768]{1,0:T(8,128)(2,1)} async-done(((bf16[64,768]{1,0:T(8,128)(2,1)}), bf16[2048,768]{1,0:T(8,128)(2,1)}) %all-gather.17.cloned.1.call-update) | async-done | bytes 3145744 | tf_op jit(solution)/shard_map/all_gather | solution.py:95
  187.1 3.3 fusion.82
  191.0 48.7 %all-gather.15.cloned.1.call-done = bf16[2048,576]{0,1:T(8,128)(2,1)} async-done(((bf16[128,576]{0,1:T(8,128)(2,1)}), bf16[2048,576]{0,1:T(8,128)(2,1)}) %all-gather.15.cloned.1.call-update) | async-done | bytes 2359312 | tf_op jit(solution)/shard_map/all_gather | solution.py:130
  239.8 3.7 fusion.87
  244.2 2.6 copy-done.42
  248.4 48.9 %all-gather.21.cloned.1.call-done = bf16[512,2048]{0,1:T(8,128)(2,1)} async-done(((bf16[512,64]{0,1:T(8,128)(2,1)}), bf16[512,2048]{0,1:T(8,128)(2,1)}) %all-gather.21.cloned.1.call-update) | async-done | bytes 2097168 | tf_op jit(solution)/shard_map/all_gather | solution.py:99
  297.3 3.4 fusion.88
  305.0 38.2 %all-gather = bf16[32,64,8]{1,2,0:T(8,128)(2,1)S(1)} all-gather(bf16[1,64,8]{1,2,0:T(8,128)(2,1)S(1)} %bitcast.173), channel_id=1, replica_groups=mesh['fsdp'=2,'ctx'=16,'tp'=4] {'fsdp','ctx'}, dimensions={0}, use_global_device_ids=true | all-gather | bytes 33792 | tf_op jit(solution)/shard_map/all_gather | solution.py:101
  343.5 2.9 all-reduce.14.cloned.1.call-done
  348.4 59.1 %all-gather.29.cloned.1.call-done = bf16[2048,704]{1,0:T(8,128)(2,1)} async-done(((bf16[64,704]{1,0:T(8,128)(2,1)}), bf16[2048,704]{1,0:T(8,128)(2,1)}) %all-gather.29.cloned.1.call-update) | async-done | bytes 2883600 | tf_op jit(solution)/shard_map/all_gather | solution.py:102
  407.4 3.9 fusion.89
  411.4 55.9 %all-gather.31.cloned.1.call-done = bf16[2048,704]{1,0:T(8,128)(2,1)} async-done(((bf16[64,704]{1,0:T(8,128)(2,1)}), bf16[2048,704]{1,0:T(8,128)(2,1)}) %all-gather.31.cloned.1.call-update) | async-done | bytes 2883600 | tf_op jit(solution)/shard_map/all_gather | solution.py:103
  467.3 3.9 fusion.90
  471.2 55.9 %all-gather.33.cloned.1.call-done = bf16[704,2048]{0,1:T(8,128)(2,1)} async-done(((bf16[704,64]{0,1:T(8,128)(2,1)}), bf16[704,2048]{0,1:T(8,128)(2,1)}) %all-gather.33.cloned.1.call-update) | async-done | bytes 2883600 | tf_op jit(solution)/shard_map/all_gather | solution.py:104
  527.2 4.3 multiply_convert_fusion.7
  531.5 72.9 %all-gather.25.cloned.1.call-done = bf16[8,2048,352]{2,1,0:T(8,128)(2,1)} async-done(((bf16[8,64,352]{2,1,0:T(8,128)(2,1)}), bf16[8,2048,352]{2,1,0:T(8,128)(2,1)}) %all-gather.25.cloned.1.call-update) | async-done | bytes 11534352 | tf_op jit(solution)/shard_map/all_gather | solution.py:106
  604.4 9.3 convolution_bitcast_fusion.3
  613.7 69.4 %all-gather.27.cloned.1.call-done = bf16[8,352,2048]{1,2,0:T(8,128)(2,1)} async-done(((bf16[8,352,64]{1,2,0:T(8,128)(2,1)}), bf16[8,352,2048]{1,2,0:T(8,128)(2,1)}) %all-gather.27.cloned.1.call-update) | async-done | bytes 11534352 | tf_op jit(solution)/shard_map/all_gather | solution.py:107
  683.1 9.6 fusion
  692.7 68.9 %all-gather.23.cloned.1.call-done = bf16[8,2048,352]{2,1,0:T(8,128)(2,1)} async-done(((bf16[8,64,352]{2,1,0:T(8,128)(2,1)}), bf16[8,2048,352]{2,1,0:T(8,128)(2,1)}) %all-gather.23.cloned.1.call-update) | async-done | bytes 11534352 | tf_op jit(solution)/shard_map/all_gather | solution.py:105
  761.7 11.9 multiply_convert_fusion.4
  773.6 10.1 convolution_bitcast_fusion.1
  783.7 6.9 fusion.11
  790.5 3.5 convolution_add_fusion.2
  794.1 2.1 convolution_add_fusion.1
  796.3 9.7 multiply_reduce_fusion
  806.0 11.0 psum.45
  817.7 25.6 all-reduce.16.cloned.1.call-done
  843.3 2.3 multiply_reduce_fusion.2
  851.9 3.7 convolution_bitcast_fusion
  860.1 2.9 fusion.2
  863.0 4.4 copy.200
  867.5 4.3 fusion.12
  876.9 64.3 %reduce-scatter.37.cloned.1.call-done = bf16[128,576]{1,0:T(8,128)(2,1)} async-done(((bf16[2048,576]{1,0:T(8,128)(2,1)}), bf16[128,576]{1,0:T(8,128)(2,1)}) %reduce-scatter.37.cloned.1.call-update) | async-done | bytes 147472
  943.0 3.5 convolution_convert_fusion.3
  946.9 3.6 convolution_convert_fusion.2
  950.5 3.9 convolution_convert_fusion.1
  960.1 2.3 copy.178
  962.4 3.4 convolution_convert_fusion.6
  965.9 3.7 convolution_convert_fusion.4
  969.7 21.3 all-reduce.18.cloned.1.call-done
  993.1 2.4 convolution_convert_fusion.5
  995.6 7.0 convert_bitcast_fusion.1
  1002.6 16.4 copy.179
  1019.1 7.1 convert_bitcast_fusion
  1026.3 16.5 copy.180
  1043.8 6.6 convolution_convert_fusion
  1051.9 78.5 %reduce-scatter.31.cloned.1.call-done = bf16[64,704]{1,0:T(8,128)(2,1)} async-done(((bf16[2048,704]{1,0:T(8,128)(2,1)}), bf16[64,704]{1,0:T(8,128)(2,1)}) %reduce-scatter.31.cloned.1.call-update) | async-done | bytes 90128 | tf_op jit(solution)/shard_map/reduce_scatter | solution.py:328
  1132.0 138.9 %reduce-scatter.33.cloned.1.call-done = bf16[64,704]{1,0:T(8,128)(2,1)} async-done(((bf16[2048,704]{1,0:T(8,128)(2,1)}), bf16[64,704]{1,0:T(8,128)(2,1)}) %reduce-scatter.33.cloned.1.call-update) | async-done | bytes 90128 | tf_op jit(solution)/shard_map/reduce_scatter | solution.py:331
  1272.5 138.7 %reduce-scatter.35.cloned.1.call-done = bf16[704,64]{0,1:T(8,128)(2,1)} async-done(((bf16[704,2048]{0,1:T(8,128)(2,1)}), bf16[704,64]{0,1:T(8,128)(2,1)}) %reduce-scatter.35.cloned.1.call-update) | async-done | bytes 90128 | tf_op jit(solution)/shard_map/reduce_scatter | solution.py:334
  1412.8 134.9 %reduce-scatter.39.cloned.1.call-done = bf16[64,8]{1,0:T(8,128)(2,1)} async-done(((bf16[2048,8]{1,0:T(8,128)(2,1)}), bf16[64,8]{1,0:T(8,128)(2,1)}) %reduce-scatter.39.cloned.1.call-update) | async-done | bytes 1040
  1549.0 135.1 %reduce-scatter.21.cloned.1.call-done = bf16[16,1024]{1,0:T(8,128)(2,1)} async-done(((bf16[512,1024]{1,0:T(8,128)(2,1)}), bf16[16,1024]{1,0:T(8,128)(2,1)}) %reduce-scatter.21.cloned.1.call-update) | async-done | bytes 32784 | tf_op jit(solution)/shard_map/reduce_scatter | solution.py:316
  1685.6 137.7 %reduce-scatter.23.cloned.1.call-done = bf16[512,64]{0,1:T(8,128)(2,1)} async-done(((bf16[512,2048]{0,1:T(8,128)(2,1)}), bf16[512,64]{0,1:T(8,128)(2,1)}) %reduce-scatter.23.cloned.1.call-update) | async-done | bytes 65552 | tf_op jit(solution)/shard_map/reduce_scatter | solution.py:319
  1824.7 3.9 fusion.42
  1828.6 64.9 %all-reduce.7 = (bf16[2048]{0:T(1024)(128)(2,1)S(1)}, bf16[512]{0:T(512)(128)(2,1)S(1)}, bf16[2048]{0:T(1024)(128)(2,1)S(1)}) all-reduce(bf16[2048]{0:T(1024)(128)(2,1)S(1)} %get-tuple-element.100, bf16[512]{0:T(512)(128)(2,1)S(1)} %get-tuple-element.102, ...), channel_id=3, replica_groups=mesh['fsdp'=2,'ctx'=16,'tp'=4] {'fsdp','ctx'}, use_global_device_ids=true, to_apply=%region_25.26.clone | all-reduce | flops 4608 | bytes 18432
  1894.8 2.7 fusion.41
  1897.5 65.8 %reduce-scatter.17.cloned.1.call-done = bf16[64,768]{1,0:T(8,128)(2,1)} async-done(((bf16[2048,768]{1,0:T(8,128)(2,1)}), bf16[64,768]{1,0:T(8,128)(2,1)}) %reduce-scatter.17.cloned.1.call-update) | async-done | bytes 98320 | tf_op jit(solution)/shard_map/reduce_scatter | solution.py:307
  1964.9 138.7 %reduce-scatter.19.cloned.1.call-done = bf16[64,576]{1,0:T(8,128)(2,1)} async-done(((bf16[2048,576]{1,0:T(8,128)(2,1)}), bf16[64,576]{1,0:T(8,128)(2,1)}) %reduce-scatter.19.cloned.1.call-update) | async-done | bytes 73744 | tf_op jit(solution)/shard_map/reduce_scatter | solution.py:310
  2105.1 155.1 %reduce-scatter.25.cloned.1.call-done = bf16[8,64,352]{2,0,1:T(8,128)(2,1)} async-done(((bf16[8,2048,352]{2,0,1:T(8,128)(2,1)}), bf16[8,64,352]{2,0,1:T(8,128)(2,1)}) %reduce-scatter.25.cloned.1.call-update) | async-done | bytes 360464 | tf_op jit(solution)/shard_map/reduce_scatter | solution.py:337
  2262.2 155.4 %reduce-scatter.27.cloned.1.call-done = bf16[8,64,352]{2,0,1:T(8,128)(2,1)} async-done(((bf16[8,2048,352]{2,0,1:T(8,128)(2,1)}), bf16[8,64,352]{2,0,1:T(8,128)(2,1)}) %reduce-scatter.27.cloned.1.call-update) | async-done | bytes 360464 | tf_op jit(solution)/shard_map/reduce_scatter | solution.py:340
  2419.5 155.0 %reduce-scatter.29.cloned.1.call-done = bf16[8,352,64]{1,2,0:T(8,128)(2,1)} async-done(((bf16[8,352,2048]{1,2,0:T(8,128)(2,1)}), bf16[8,352,64]{1,2,0:T(8,128)(2,1)}) %reduce-scatter.29.cloned.1.call-update) | async-done | bytes 360464 | tf_op jit(solution)/shard_map/reduce_scatter | solution.py:343
  (227 shorter events, 68.8 us)
Async XLA Ops:
  7.2 80.5 %all-gather.13.cloned.1.call-start = ((), (), s32[]{:S(2)}) async-start(), calls=%async_computation.12 | async-start | bytes 2703360 | tf_op jit(solution)/shard_map/all_gather | solution.py:96
  7.9 119.4 %all-gather.19.cloned.1.call-start = ((), (), s32[]{:S(2)}) async-start(), calls=%async_computation.15 | async-start | bytes 1081344 | tf_op jit(solution)/shard_map/all_gather | solution.py:98
  8.7 178.4 %all-gather.17.cloned.1.call-start = ((), (), s32[]{:S(2)}) async-start(), calls=%async_computation.14 | async-start | bytes 3244032 | tf_op jit(solution)/shard_map/all_gather | solution.py:95
  9.4 230.4 %all-gather.15.cloned.1.call-start = ((), (), s32[]{:S(2)}) async-start(), calls=%async_computation.13 | async-start | bytes 2506752 | tf_op jit(solution)/shard_map/all_gather | solution.py:130
  85.4 43.3 %copy-start.39 = (f32[32]{0:T(128)}, f32[32]{0:T(128)S(1)}, u32[]{:S(2)}) copy-start(f32[32]{0:T(128)S(1)} %multiply_power_fusion) | copy-start | bytes 388
  86.4 42.4 %copy-start.33 = (f32[128]{0:T(128)}, f32[128]{0:T(128)S(1)}, u32[]{:S(2)}) copy-start(f32[128]{0:T(128)S(1)} %fusion.73) | copy-start | bytes 1540
  87.6 99.4 %copy-start = (bf16[128,2048]{1,0:T(8,128)(2,1)S(1)}, bf16[128,2048]{1,0:T(8,128)(2,1)}, u32[]{:S(2)}) copy-start(bf16[128,2048]{1,0:T(8,128)(2,1)} %param.18) | copy-start | bytes 1572868
  90.9 99.5 %copy-start.35 = (f32[128]{0:T(128)}, f32[128]{0:T(128)S(1)}, u32[]{:S(2)}) copy-start(f32[128]{0:T(128)S(1)} %add_rsqrt_fusion.1) | copy-start | bytes 1540
  91.9 205.4 %all-gather.21.cloned.1.call-start = ((), (), s32[]{:S(2)}) async-start(), calls=%async_computation.16 | async-start | bytes 2162688 | tf_op jit(solution)/shard_map/all_gather | solution.py:99
  92.5 253.9 %all-reduce.14.cloned.1.call-start = ((), (), s32[]{:S(2)}) async-start(), calls=%async_computation.17 | async-start | bytes 2097152 | tf_op jit(solution)/shard_map/psum | solution.py:159
  128.8 119.3 %copy-start.9 = (bf16[512,1024]{0,1:T(8,128)(2,1)}, bf16[512,1024]{0,1:T(8,128)(2,1)S(1)}, u32[]{:S(2)}) copy-start(bf16[512,1024]{0,1:T(8,128)(2,1)S(1)} %copy.158) | copy-start | bytes 3145732
  190.3 53.2 %copy-start.14 = (f32[128,768]{0,1:T(8,128)}, f32[128,768]{0,1:T(8,128)S(1)}, u32[]{:S(2)}) copy-start(f32[128,768]{0,1:T(8,128)S(1)} %fusion.82) | copy-start | bytes 1179652
  190.5 53.0 %copy-start.27 = (bf16[128,4,32]{2,0,1:T(8,128)(2,1)}, bf16[128,4,32]{2,0,1:T(8,128)(2,1)S(1)}, u32[]{:S(2)}) copy-start(bf16[128,4,32]{2,0,1:T(8,128)(2,1)S(1)} %copy.161) | copy-start | bytes 98308
  190.7 52.9 %copy-start.29 = (bf16[128,4,32]{2,0,1:T(8,128)(2,1)}, bf16[128,4,32]{2,0,1:T(8,128)(2,1)S(1)}, u32[]{:S(2)}) copy-start(bf16[128,4,32]{2,0,1:T(8,128)(2,1)S(1)} %copy.162) | copy-start | bytes 98308
  191.0 52.5 %copy-start.25 = (bf16[128,4,512]{2,0,1:T(8,128)(2,1)}, bf16[128,4,512]{2,0,1:T(8,128)(2,1)S(1)}, u32[]{:S(2)}) copy-start(bf16[128,4,512]{2,0,1:T(8,128)(2,1)S(1)} %fusion.29) | copy-start | bytes 1572868
  243.6 4.5 copy-start.1
  243.6 3.2 copy-start.42
  248.1 55.5 %copy-start.24 = (bf16[512,4,128]{2,0,1:T(8,128)(2,1)}, bf16[512,4,128]{2,0,1:T(8,128)(2,1)S(1)}, u32[]{:S(2)}) copy-start(bf16[512,4,128]{2,0,1:T(8,128)(2,1)S(1)} %fusion.28) | copy-start | bytes 1572868
  248.4 94.8 %copy-start.23 = (bf16[4,128,128]{1,2,0:T(8,128)(2,1)}, bf16[4,128,128]{1,2,0:T(8,128)(2,1)S(1)}, u32[]{:S(2)}) copy-start(bf16[4,128,128]{1,2,0:T(8,128)(2,1)S(1)} %convolution_convert_fusion.14) | copy-start | bytes 393220
  248.4 56.5 %copy-start.37 = (bf16[2048]{0:T(1024)(128)(2,1)S(1)}, bf16[2048]{0:T(1024)(128)(2,1)}, u32[]{:S(2)}) copy-start(bf16[2048]{0:T(1024)(128)(2,1)} %get-tuple-element.109) | copy-start | bytes 12292
  248.4 56.5 %copy-start.41 = (bf16[64,8]{0,1:T(8,128)(2,1)S(1)}, bf16[64,8]{0,1:T(8,128)(2,1)}, u32[]{:S(2)}) copy-start(bf16[64,8]{0,1:T(8,128)(2,1)} %param.29) | copy-start | bytes 3076
  248.4 94.9 %copy-start.11 = (bf16[128,2048]{1,0:T(8,128)(2,1)S(1)}, bf16[128,2048]{1,0:T(8,128)(2,1)}, u32[]{:S(2)}) copy-start(bf16[128,2048]{1,0:T(8,128)(2,1)} %param.21) | copy-start | bytes 1572868
  297.3 46.1 %copy-start.38 = (s32[128,6]{0,1:T(8,128)S(1)}, s32[128,6]{0,1:T(8,128)}, u32[]{:S(2)}) copy-start(s32[128,6]{0,1:T(8,128)} %param.20) | copy-start | bytes 9220
  300.7 106.7 %all-gather.29.cloned.1.call-start = ((), (), s32[]{:S(2)}) async-start(), calls=%async_computation.21 | async-start | bytes 3244032 | tf_op jit(solution)/shard_map/all_gather | solution.py:102
  301.5 165.8 %all-gather.31.cloned.1.call-start = ((), (), s32[]{:S(2)}) async-start(), calls=%async_computation.22 | async-start | bytes 3244032 | tf_op jit(solution)/shard_map/all_gather | solution.py:103
  302.2 224.9 %all-gather.33.cloned.1.call-start = ((), (), s32[]{:S(2)}) async-start(), calls=%async_computation.23 | async-start | bytes 3244032 | tf_op jit(solution)/shard_map/all_gather | solution.py:104
  303.0 301.4 %all-gather.25.cloned.1.call-start = ((), (), s32[]{:S(2)}) async-start(), calls=%async_computation.19 | async-start | bytes 12976128 | tf_op jit(solution)/shard_map/all_gather | solution.py:106
  303.6 379.5 %all-gather.27.cloned.1.call-start = ((), (), s32[]{:S(2)}) async-start(), calls=%async_computation.20 | async-start | bytes 12976128 | tf_op jit(solution)/shard_map/all_gather | solution.py:107
  304.3 457.4 %all-gather.23.cloned.1.call-start = ((), (), s32[]{:S(2)}) async-start(), calls=%async_computation.18 | async-start | bytes 12976128 | tf_op jit(solution)/shard_map/all_gather | solution.py:105
  304.9 538.4 %all-reduce.16.cloned.1.call-start = ((), (), s32[]{:S(2)}) async-start(), calls=%async_computation.24 | async-start | bytes 2097152 | tf_op jit(solution)/shard_map/psum | solution.py:212
  348.3 468.7 %copy-start.31 = (f32[128]{0:T(128)}, f32[128]{0:T(128)S(1)}, u32[]{:S(2)}) copy-start(f32[128]{0:T(128)S(1)} %get-tuple-element.138) | copy-start | bytes 1540
  773.6 10.1 copy-start.5
  790.5 3.5 copy-start.7
  790.5 3.6 copy-start.21
  796.3 145.0 %reduce-scatter.37.cloned.1.call-start = ((), (), s32[]{:S(2)}) async-start(), calls=%async_computation.35 | async-start | bytes 2785280
  843.3 2.3 copy-start.12
  843.3 4.3 copy-start.8
  851.8 3.7 copy-start.2
  851.9 4.2 copy-start.43
  857.8 2.2 copy-start.26
  857.9 2.2 copy-start.28
  857.9 2.2 copy-start.30
  867.4 123.6 %all-reduce.18.cloned.1.call-start = ((), (), s32[]{:S(2)}) async-start(), calls=%async_computation.37 | async-start | bytes 2392064 | tf_op jit(solution)/shard_map/psum | solution.py:197
  867.4 4.4 copy-start.16
  867.5 4.3 copy-start.44
  871.8 1.4 copy-start.10
  871.8 3.2 copy-start.6
  942.9 187.5 %reduce-scatter.31.cloned.1.call-start = ((), (), s32[]{:S(2)}) async-start(), calls=%async_computation.32 | async-start | bytes 3244032 | tf_op jit(solution)/shard_map/reduce_scatter | solution.py:328
  946.6 324.3 %reduce-scatter.33.cloned.1.call-start = ((), (), s32[]{:S(2)}) async-start(), calls=%async_computation.33 | async-start | bytes 3244032 | tf_op jit(solution)/shard_map/reduce_scatter | solution.py:331
  950.5 460.7 %reduce-scatter.35.cloned.1.call-start = ((), (), s32[]{:S(2)}) async-start(), calls=%async_computation.34 | async-start | bytes 3244032 | tf_op jit(solution)/shard_map/reduce_scatter | solution.py:334
  954.5 593.1 %reduce-scatter.39.cloned.1.call-start = ((), (), s32[]{:S(2)}) async-start(), calls=%async_computation.36 | async-start | bytes 540672
  956.0 728.2 %reduce-scatter.21.cloned.1.call-start = ((), (), s32[]{:S(2)}) async-start(), calls=%async_computation.27 | async-start | bytes 1081344 | tf_op jit(solution)/shard_map/reduce_scatter | solution.py:316
  962.4 860.9 %reduce-scatter.23.cloned.1.call-start = ((), (), s32[]{:S(2)}) async-start(), calls=%async_computation.28 | async-start | bytes 2162688 | tf_op jit(solution)/shard_map/reduce_scatter | solution.py:319
  965.9 26.0 %copy-start.36 = (f32[128]{0:T(128)S(1)}, f32[128]{0:T(128)}, u32[]{:S(2)}) copy-start(f32[128]{0:T(128)} %copy-done.35) | copy-start | bytes 1540
  965.9 26.3 %copy-start.34 = (f32[128]{0:T(128)S(1)}, f32[128]{0:T(128)}, u32[]{:S(2)}) copy-start(f32[128]{0:T(128)} %copy-done.33) | copy-start | bytes 1540
  965.9 26.3 %copy-start.40 = (f32[32]{0:T(128)S(1)}, f32[32]{0:T(128)}, u32[]{:S(2)}) copy-start(f32[32]{0:T(128)} %copy-done.39) | copy-start | bytes 388
  965.9 997.4 %reduce-scatter.17.cloned.1.call-start = ((), (), s32[]{:S(2)}) async-start(), calls=%async_computation.25 | async-start | bytes 3244032 | tf_op jit(solution)/shard_map/reduce_scatter | solution.py:307
  969.6 1134.0 %reduce-scatter.19.cloned.1.call-start = ((), (), s32[]{:S(2)}) async-start(), calls=%async_computation.26 | async-start | bytes 2703360 | tf_op jit(solution)/shard_map/reduce_scatter | solution.py:310
  995.6 1264.7 %reduce-scatter.25.cloned.1.call-start = ((), (), s32[]{:S(2)}) async-start(), calls=%async_computation.29 | async-start | bytes 12976128 | tf_op jit(solution)/shard_map/reduce_scatter | solution.py:337
  1019.1 1398.5 %reduce-scatter.27.cloned.1.call-start = ((), (), s32[]{:S(2)}) async-start(), calls=%async_computation.30 | async-start | bytes 12976128 | tf_op jit(solution)/shard_map/reduce_scatter | solution.py:340
  1042.7 1531.7 %reduce-scatter.29.cloned.1.call-start = ((), (), s32[]{:S(2)}) async-start(), calls=%async_computation.31 | async-start | bytes 12976128 | tf_op jit(solution)/shard_map/reduce_scatter | solution.py:343
  1050.4 774.3 %copy-start.20 = (bf16[128,512]{0,1:T(8,128)(2,1)S(1)}, bf16[128,512]{0,1:T(8,128)(2,1)}, u32[]{:S(2)}) copy-start(bf16[128,512]{0,1:T(8,128)(2,1)} %copy-done.19) | copy-start | bytes 393220
  1050.5 844.3 %copy-start.4 = (f32[128,2048]{1,0:T(8,128)S(1)}, f32[128,2048]{1,0:T(8,128)}, u32[]{:S(2)}) copy-start(f32[128,2048]{1,0:T(8,128)} %copy-done.3) | copy-start | bytes 3145732
  1050.5 844.3 %copy-start.22 = (bf16[128,2048]{1,0:T(8,128)(2,1)S(1)}, bf16[128,2048]{1,0:T(8,128)(2,1)}, u32[]{:S(2)}) copy-start(bf16[128,2048]{1,0:T(8,128)(2,1)} %get-tuple-element.110) | copy-start | bytes 1572868
  (7 other events, 6.4 us)
Sparse Core Ops, SparseCore 0:
  9.7 60.8 all-gather.12
  72.3 54.9 all-gather.18
  129.0 58.0 all-gather.16
  189.8 49.9 all-gather.14
  241.3 55.9 all-gather.20
  300.9 45.4 all-reduce.13
  348.2 59.1 all-gather.28
  409.3 57.9 all-gather.30
  469.1 57.9 all-gather.32
  528.8 75.5 all-gather.24
  606.1 76.9 all-gather.26
  684.7 76.9 all-gather.22
  796.4 46.8 all-reduce.15
  867.5 73.6 reduce-scatter.36
  944.4 46.4 all-reduce.17
  993.2 137.1 reduce-scatter.30
  1132.8 138.0 reduce-scatter.32
  1273.1 138.0 reduce-scatter.34
  1413.6 133.9 reduce-scatter.38
  1549.8 134.2 reduce-scatter.20
  1686.7 136.5 reduce-scatter.22
  1825.6 137.6 reduce-scatter.16
  1965.8 137.7 reduce-scatter.18
  2106.0 154.2 reduce-scatter.24
  2262.8 154.6 reduce-scatter.26
  2419.9 154.5 reduce-scatter.28
where the time goes:
time: 2600 us; the launch traced here: 2580 us
  waiting for transfers between devices  2130 us (82%)
  blocking collectives  184 us (7%)
  matrix products  161 us (6%)
  local copies, waits for them, and re-layouts  62.8 us (2%)
  other arithmetic  29 us (1%)
    unnamed x28, waiting for transfers between devices  206 us
    reduce_scatter x1, waiting for transfers between devices, shards(): lax.psum_scatter(d_up.astype(jnp.bfloat16), ('fsdp', 'ctx'), scatter_dime...  155 us
    reduce_scatter x1, waiting for transfers between devices, shards(): lax.psum_scatter(d_gate.astype(jnp.bfloat16), ('fsdp', 'ctx'), scatter_di...  155 us
    reduce_scatter x1, waiting for transfers between devices, shards(): lax.psum_scatter(d_down.astype(jnp.bfloat16), ('fsdp', 'ctx'), scatter_di...  155 us
    reduce_scatter x1, waiting for transfers between devices, shards(): lax.psum_scatter(d_shared_up.astype(jnp.bfloat16), ('fsdp', 'ctx'), scatt...  139 us
    reduce_scatter x1, waiting for transfers between devices, shards(): lax.psum_scatter(d_shared_down.astype(jnp.bfloat16), ('fsdp', 'ctx'), sca...  139 us
    reduce_scatter x1, waiting for transfers between devices, shards(): lax.psum_scatter(d_latent.astype(jnp.bfloat16), ('fsdp', 'ctx'), scatter_...  139 us
    reduce_scatter x1, waiting for transfers between devices, shards(): lax.psum_scatter(d_out.astype(jnp.bfloat16), ('fsdp', 'ctx'), scatter_dim...  138 us
  transfers between devices with their start and end apart: 26, of which 25 were waited for; matrix products, arithmetic and copies ran while one was open for 7% of the time, Pallas kernels for 0%

commit v1 on v0

v1 whole, which is shorter than its diff:
```python
import jax
import jax.numpy as jnp
from jax import lax
from jax.experimental import pallas as pl
from jax.experimental.pallas import tpu as pltpu
from jax.sharding import PartitionSpec as P

NOPE = 128
ROPE = 64
VD = 128
R = 512
E = 8
FF_PAD = 384
SH_PAD = 128

epsilon = 1e-06
rope_base = 50000.0
route_scale = 2.446
highest = lax.Precision.HIGHEST
bf16 = jnp.bfloat16
f32 = jnp.float32

PLANE = ("fsdp", "ctx")


def mask(ky=0, kx=0, kc=0):
    return (ky & 1) * 16 + (ky >> 1) * 8 + kx * 2 + kc


def swap(values, ky=0, kx=0, kc=0):
    bits = mask(ky, kx, kc)
    return lax.ppermute(values, PLANE, [(i, i ^ bits) for i in range(32)])


def swap_z(values, k):
    return lax.ppermute(values, "tp", [(i, i ^ k) for i in range(4)])


def arrange(parts, places, count, rows, me):
    width = parts[0].shape[-1]

    def kernel(me_ref, *refs):
        ins, out, sem = refs[: len(parts)], refs[len(parts)], refs[len(parts) + 1]
        copies = []
        for n, (part, index, row, bits) in enumerate(places):
            height = parts[part].shape[1]
            copies.append(
                pltpu.make_async_copy(
                    ins[part].at[index],
                    out.at[me_ref[0] ^ bits, pl.ds(row, height)],
                    sem.at[n],
                )
            )
        for copy in copies:
            copy.start()
        for copy in copies:
            copy.wait()

    return pl.pallas_call(
        kernel,
        out_shape=jax.ShapeDtypeStruct((count, rows, width), parts[0].dtype),
        in_specs=[pl.BlockSpec(memory_space=pltpu.SMEM)]
        + [pl.BlockSpec(memory_space=pl.ANY)] * len(parts),
        out_specs=pl.BlockSpec(memory_space=pl.ANY),
        scratch_shapes=[pltpu.SemaphoreType.DMA((len(places),))],
    )(me.reshape(1), *parts)


def pick(source, order, me):
    def kernel(me_ref, src, out, sem):
        copies = [
            pltpu.make_async_copy(src.at[me_ref[0] ^ bits], out.at[n], sem.at[n])
            for n, bits in enumerate(order)
        ]
        for copy in copies:
            copy.start()
        for copy in copies:
            copy.wait()

    return pl.pallas_call(
        kernel,
        out_shape=jax.ShapeDtypeStruct((len(order),) + source.shape[1:], source.dtype),
        in_specs=[
            pl.BlockSpec(memory_space=pltpu.SMEM),
            pl.BlockSpec(memory_space=pl.ANY),
        ],
        out_specs=pl.BlockSpec(memory_space=pl.ANY),
        scratch_shapes=[pltpu.SemaphoreType.DMA((len(order),))],
    )(me.reshape(1), source)


def total(parts, dtype=bf16):
    out = parts[0].astype(f32)
    for part in parts[1:]:
        out = out + part.astype(f32)
    return out.astype(dtype)


def gather_plane(block, me):
    half = block.shape[0] // 2
    along_x = jnp.stack([block[:half]] + [swap(block[:half], kx=k) for k in (1, 2, 3)])
    along_y = jnp.stack([block[half:]] + [swap(block[half:], ky=k) for k in (1, 2, 3)])
    first = [along_x] + [swap(along_x, ky=k) for k in (1, 2, 3)]
    second = [along_y] + [swap(along_y, kx=k) for k in (1, 2, 3)]
    parts, places = [], []
    for kc in (0, 1):
        for major in range(4):
            for row, halves in ((0, first), (half, second)):
                part = halves[major] if kc == 0 else swap(halves[major], kc=1)
                for minor in range(4):
                    ky, kx = (major, minor) if row == 0 else (minor, major)
                    places.append((len(parts), minor, row, mask(ky, kx, kc)))
                parts.append(part)
    return arrange(parts, places, 32, block.shape[0], me)


def scatter_plane(blocks, me):
    order = [mask(ky, kx, 0) for ky in range(4) for kx in range(4)]
    keep = pick(blocks, order, me)
    send = pick(blocks, [bits + 1 for bits in order], me)
    both = total([keep, swap(send, kc=1)])
    both = both.reshape((4, 4) + both.shape[1:])
    half = blocks.shape[1] // 2
    first, second = both[:, :, :half], both[:, :, half:]
    first = total([first[:, 0]] + [swap(first[:, k], kx=k) for k in (1, 2, 3)])
    second = total([second[0]] + [swap(second[k], ky=k) for k in (1, 2, 3)])
    first = total([first[0]] + [swap(first[k], ky=k) for k in (1, 2, 3)], f32)
    second = total([second[0]] + [swap(second[k], kx=k) for k in (1, 2, 3)], f32)
    return jnp.concatenate([first, second], axis=0)


def part_z(values, k, z):
    rows = values.shape[0] // 4
    return lax.dynamic_slice_in_dim(values, (z ^ k) * rows, rows, 0)


def scatter_z(values, z, dtype=bf16):
    return total([part_z(values, 0, z)] + [swap_z(part_z(values, k, z), k) for k in (1, 2, 3)], dtype)


def gather_z(values, z):
    rows = values.shape[0]
    out = jnp.zeros((4 * rows,) + values.shape[1:], values.dtype)
    for k in range(4):
        piece = values if k == 0 else swap_z(values, k)
        out = lax.dynamic_update_slice_in_dim(out, piece, (z ^ k) * rows, 0)
    return out


def gather_rows(values):
    own = [values] + [swap(values, kx=k) for k in (1, 2, 3)]
    other = [swap(part, kc=1) for part in own]
    return jnp.concatenate(own + other, axis=0)


def rms_parts(values):
    inverse = lax.rsqrt(jnp.mean(values * values, axis=-1, keepdims=True) + epsilon)
    return (values * inverse, inverse)


def norm_back(grad_normed, unit_rows, inverse, gain_vec):
    scaled = grad_normed * gain_vec
    grad_gain = jnp.sum(grad_normed * unit_rows, axis=0)
    grad_in = inverse * (scaled - unit_rows * jnp.mean(scaled * unit_rows, axis=-1, keepdims=True))
    return (grad_in, grad_gain)


def rotary(values, cosine, sine_part):
    half_width = values.shape[-1] // 2
    front_half = values[..., :half_width]
    back_half = values[..., half_width:]
    return jnp.concatenate(
        [front_half * cosine - back_half * sine_part, back_half * cosine + front_half * sine_part],
        axis=-1,
    )


def angle_tables(within, half_width):
    frequency = rope_base ** (-jnp.arange(half_width, dtype=jnp.float32) / half_width)
    angles = within.astype(jnp.float32)[:, None] * frequency[None, :]
    return (jnp.cos(angles), jnp.sin(angles))


def doc_layout(doc_lengths, pack_len):
    doc_ends = jnp.cumsum(doc_lengths)
    positions = jnp.arange(pack_len, dtype=jnp.int32)
    doc_ids = jnp.sum((positions[:, None] >= doc_ends[None, :-1]).astype(jnp.int32), axis=1)
    doc_starts = doc_ends - doc_lengths
    belongs = doc_ids[:, None] == jnp.arange(doc_lengths.shape[0], dtype=jnp.int32)[None, :]
    doc_first = jnp.sum(jnp.where(belongs, doc_starts[None, :], 0), axis=1)
    return (doc_ids, positions, positions - doc_first)


def pad_to(values, width):
    return jnp.pad(values, [(0, 0)] * (values.ndim - 1) + [(0, width - values.shape[-1])])


def dot(left, right):
    return jnp.dot(left, right, preferred_element_type=f32)


def shards(
    tokens,
    lengths,
    routes,
    cotangent,
    attn_gain,
    w_query,
    w_latent,
    latent_gain,
    w_expand,
    w_out,
    moe_gain,
    w_router,
    w_gate,
    w_up,
    w_down,
    shared_gate,
    shared_up,
    shared_down,
):
    me = lax.axis_index("fsdp") * 16 + lax.axis_index("ctx")
    place = lax.axis_index("ctx")
    member = place % 8
    z = lax.axis_index("tp")
    row_count, width = tokens.shape
    db = width // 32
    pack_len = row_count * 16
    rb = R // 32
    local_heads = w_query.shape[1] // (NOPE + ROPE)
    ff, sh = w_gate.shape[2], shared_gate.shape[1] // 8

    aux = jnp.concatenate(
        [attn_gain[None], moe_gain[None], pad_to(latent_gain[None], db), jnp.zeros((5, db), bf16), w_router.T],
        axis=0,
    )
    aux = jnp.pad(aux, ((0, db - 16), (0, 0)))
    expand_rows = jnp.concatenate(jnp.split(w_expand, local_heads, axis=1), axis=0)
    packed = jnp.concatenate([w_query, w_latent, aux, w_out.T, expand_rows], axis=1)
    gathered = gather_plane(packed, me)
    cuts, edge = [], 0
    for piece in (w_query, w_latent, aux, w_out.T, expand_rows):
        cuts.append(gathered[:, :, edge : edge + piece.shape[1]])
        edge += piece.shape[1]
    query_weight = cuts[0].reshape(width, -1)
    latent_weight = cuts[1].reshape(width, -1)
    gain_attn = cuts[2][:, 0].reshape(width).astype(f32)
    gain_moe = cuts[2][:, 1].reshape(width).astype(f32)
    gain_latent = cuts[2][:, 2, :rb].reshape(R).astype(f32)
    router_weight = jnp.swapaxes(cuts[2][:, 8:16], 0, 1).reshape(E, width).T
    out_weight_t = cuts[3].reshape(width, -1)
    expand = jnp.swapaxes(cuts[4].reshape(32, local_heads, rb, NOPE + VD), 0, 1).reshape(
        local_heads, R, NOPE + VD
    )
    key_weight = expand[..., :NOPE]
    value_weight = expand[..., NOPE:]

    def with_shared(routed, shared):
        shared = jnp.stack(jnp.split(shared, 8, axis=1))
        return jnp.concatenate([pad_to(routed, FF_PAD), pad_to(shared, SH_PAD)], axis=-1)

    experts = jnp.stack(
        [
            with_shared(w_gate, shared_gate),
            with_shared(w_up, shared_up),
            with_shared(jnp.swapaxes(w_down, 1, 2), shared_down.T),
        ],
        axis=1,
    )
    wide = experts.shape[-1]
    experts = pick(experts.reshape(8, 3 * db, wide), [mask(0, kx, kc) for kc in (0, 1) for kx in range(4)], member)
    other = swap(experts[4:], kc=1)
    by_x = jnp.stack([experts[:4], other], axis=1)
    mine = [by_x[0]] + [swap(by_x[k], kx=k) for k in (1, 2, 3)]
    mine = jnp.stack(mine)
    from_y = [mine] + [swap(mine, ky=k) for k in (1, 2, 3)]
    parts = [part.reshape(8, 3 * db, wide) for part in from_y]
    places = [
        (ky, kx * 2 + kc, 0, mask(ky, kx, kc)) for ky in range(4) for kx in range(4) for kc in (0, 1)
    ]
    mine = arrange(parts, places, 32, 3 * db, me).reshape(32, 3, db, wide)
    gate_weight = mine[:, 0].reshape(width, wide)
    up_weight = mine[:, 1].reshape(width, wide)
    down_weight_t = mine[:, 2].reshape(width, wide)

    picked = jnp.sum(
        (routes[:, :, None] == jnp.arange(E, dtype=jnp.int32)[None, None, :]).astype(f32), axis=1
    )
    group_in = gather_rows(jnp.concatenate([cotangent, pad_to(picked.astype(bf16), 128)], axis=1))
    group_cot = group_in[:, :width]
    group_picked = group_in[:, width : width + E].astype(f32)

    doc_ids, positions, within_all = doc_layout(lengths[0], pack_len)
    offset = place * row_count
    own_docs = lax.dynamic_slice_in_dim(doc_ids, offset, row_count, 0)
    own_places = lax.dynamic_slice_in_dim(positions, offset, row_count, 0)
    own_within = lax.dynamic_slice_in_dim(within_all, offset, row_count, 0)
    cosine, sine_part = angle_tables(own_within, ROPE // 2)
    residual_in = tokens.astype(f32)
    unit_attn, scale_attn = rms_parts(residual_in)
    hidden = (unit_attn * gain_attn).astype(bf16)
    query_raw = dot(hidden, query_weight).reshape(row_count, local_heads, NOPE + ROPE)
    queries = jnp.concatenate(
        [query_raw[..., :NOPE], rotary(query_raw[..., NOPE:], cosine[:, None], sine_part[:, None])],
        axis=-1,
    ).astype(bf16)
    latent = dot(hidden, latent_weight)
    unit_latent, scale_latent = rms_parts(latent[:, :R])
    compact = unit_latent * gain_latent
    key_rot = rotary(latent[:, R:], cosine, sine_part)
    own_keys = jnp.concatenate([compact, key_rot], axis=-1).astype(bf16)

    along_x = jnp.stack([own_keys] + [swap(own_keys, kx=k) for k in (1, 2, 3)])
    along_y = [along_x, swap(along_x, ky=2)]
    key_parts = along_y + [swap(part, kc=1) for part in along_y]
    key_places = [
        (kc * 2 + yh, kx, 0, yh * 8 + kx * 2 + kc) for kc in (0, 1) for yh in (0, 1) for kx in range(4)
    ]
    key_rows = arrange(key_parts, key_places, 16, row_count, place).reshape(pack_len, R + ROPE)

    absorbed = jnp.einsum(
        "thn,hrn->thr", queries[..., :NOPE], key_weight, preferred_element_type=f32
    ).astype(bf16)
    query_cat = jnp.concatenate([absorbed, queries[..., NOPE:]], axis=-1)
    score_scale = (NOPE + ROPE) ** (-0.5)
    allowed = (own_docs[:, None] == doc_ids[None, :]) & (positions[None, :] <= own_places[:, None])
    scores = score_scale * jnp.einsum("thc,kc->htk", query_cat, key_rows, preferred_element_type=f32)
    scores = jnp.where(allowed[None], scores, -1e30)
    row_max = jnp.max(scores, axis=-1, keepdims=True)
    weights = jnp.exp(scores - row_max)
    probs_low = (weights / jnp.sum(weights, axis=-1, keepdims=True)).astype(bf16)
    mixture = jnp.einsum("htk,kr->thr", probs_low, key_rows[:, :R], preferred_element_type=f32).astype(bf16)
    head_out = (
        jnp.einsum("thr,hrv->thv", mixture, value_weight, preferred_element_type=f32)
        .astype(bf16)
        .reshape(row_count, local_heads * VD)
    )
    attention = jnp.einsum("tv,dv->td", head_out, out_weight_t, preferred_element_type=f32)
    attention = gather_z(scatter_z(attention.astype(bf16), z), z)
    middle = residual_in + attention.astype(f32)
    unit_moe, scale_moe = rms_parts(middle)
    normed = (unit_moe * gain_moe).astype(bf16)
    router_sig = jax.nn.sigmoid(dot(normed, router_weight))
    weighted = router_sig * picked
    gate_total = jnp.sum(weighted, axis=1, keepdims=True)
    gate_values = route_scale * weighted / gate_total
    grad_out = cotangent.astype(f32)

    group = gather_rows(normed)
    group_weighted = jax.nn.sigmoid(dot(group, router_weight)) * group_picked
    group_gates = route_scale * group_weighted / jnp.sum(group_weighted, axis=1, keepdims=True)
    gate_own = jnp.sum(
        jnp.where(jnp.arange(E)[None, :] == member, group_gates, 0.0), axis=1, keepdims=True
    )
    gate_row = jnp.concatenate(
        [jnp.broadcast_to(gate_own, (gate_own.shape[0], FF_PAD)), jnp.ones((gate_own.shape[0], SH_PAD), f32)],
        axis=1,
    )
    gate_pre = dot(group, gate_weight)
    up_pre = dot(group, up_weight)
    sig = jax.nn.sigmoid(gate_pre)
    silu = gate_pre * sig
    act = silu * up_pre
    act_low = (gate_row * act).astype(bf16)
    grad_act_bare = dot(group_cot, down_weight_t)
    grad_gate_own = jnp.sum((act * grad_act_bare)[:, :FF_PAD], axis=1, keepdims=True)
    grad_act = grad_act_bare * gate_row
    grad_gate_pre = (grad_act * up_pre * (sig * (1.0 + gate_pre * (1.0 - sig)))).astype(bf16)
    grad_up_pre = (grad_act * silu).astype(bf16)
    expert_part = jnp.einsum("tf,df->td", act_low, down_weight_t, preferred_element_type=f32).astype(bf16)
    grad_part = (
        jnp.einsum("tf,df->td", grad_gate_pre, gate_weight, preferred_element_type=f32)
        + jnp.einsum("tf,df->td", grad_up_pre, up_weight, preferred_element_type=f32)
    ).astype(bf16)
    d_down_t = jnp.einsum("td,tf->df", group_cot, act_low, preferred_element_type=f32).astype(bf16)
    d_gate = jnp.einsum("td,tf->df", group, grad_gate_pre, preferred_element_type=f32).astype(bf16)
    d_up = jnp.einsum("td,tf->df", group, grad_up_pre, preferred_element_type=f32).astype(bf16)
    lane = jnp.arange(128)[None, :]
    high = grad_gate_own.astype(bf16).astype(f32)
    gates_part = (
        jnp.where(lane == member, high, 0.0) + jnp.where(lane == member + E, grad_gate_own - high, 0.0)
    ).astype(bf16)
    first = expert_part.reshape(2, 4, row_count, -1)
    second = jnp.concatenate([grad_part, gates_part], axis=1).reshape(2, 4, row_count, -1)
    first = total([first[0], swap(first[1], kc=1)])
    second = total([second[0], swap(second[1], kc=1)])
    first = total([first[0]] + [swap(first[k], kx=k) for k in (1, 2, 3)])
    quarter = row_count // 4

    def z_rows(values, k):
        return lax.dynamic_slice_in_dim(values, (z ^ k) * quarter, quarter, 1)

    second = total([z_rows(second, 0)] + [swap_z(z_rows(second, k), k) for k in (1, 2, 3)])
    first = scatter_z(first, z)
    second = total([second[0]] + [swap(second[k], kx=k) for k in (1, 2, 3)])
    expert_sum = gather_z(first, z)
    second = gather_z(second, z)
    output = (middle + expert_sum.astype(f32)).astype(bf16)
    grad_normed = second[:, :width].astype(f32)
    grad_gates = second[:, width : width + E].astype(f32) + second[:, width + E : width + 2 * E].astype(f32)

    d_experts = jnp.stack(
        [d_gate.reshape(32, db, wide), d_up.reshape(32, db, wide), d_down_t.reshape(32, db, wide)], axis=1
    ).reshape(32, 3 * db, wide)
    d_experts = pick(
        d_experts, [mask(ky, kx, kc) for ky in range(4) for kx in range(4) for kc in (0, 1)], me
    ).reshape(4, 4, 2, 3 * db, wide)
    d_experts = total([d_experts[0]] + [swap(d_experts[k], ky=k) for k in (1, 2, 3)])
    d_experts = jnp.stack([d_experts[0]] + [swap(d_experts[k], kx=k) for k in (1, 2, 3)])
    d_parts = [d_experts[:, 0], swap(d_experts[:, 1], kc=1)]
    d_experts = arrange(
        d_parts, [(kc, kx, 0, kx * 2 + kc) for kc in (0, 1) for kx in range(4)], 8, 3 * db, member
    )
    d_experts = d_experts.reshape(8, 3, db, wide).astype(f32)
    d_routed = [d_experts[:, i, :, :ff] for i in range(3)]
    d_shared = [
        jnp.concatenate([d_experts[e, i, :, FF_PAD : FF_PAD + sh] for e in range(8)], axis=1) for i in range(3)
    ]

    grad_weighted = (
        route_scale * grad_gates - jnp.sum(grad_gates * gate_values, axis=1, keepdims=True)
    ) / gate_total
    grad_logits = grad_weighted * picked * router_sig * (1.0 - router_sig)
    d_router = jnp.dot(normed.astype(f32).T, grad_logits, precision=highest)
    grad_normed = grad_normed + jnp.dot(grad_logits, router_weight.astype(f32).T, precision=highest)
    grad_middle_norm, d_gain_moe = norm_back(grad_normed, unit_moe, scale_moe, gain_moe)
    grad_middle = grad_out + grad_middle_norm
    grad_attention = grad_middle.astype(bf16)
    d_out_t = jnp.einsum("td,tv->dv", grad_attention, head_out, preferred_element_type=f32)
    grad_heads = dot(grad_attention, out_weight_t).astype(bf16).reshape(row_count, local_heads, VD)
    d_value = jnp.einsum("thr,thv->hrv", mixture, grad_heads, preferred_element_type=f32)
    grad_mixture = jnp.einsum("thv,hrv->thr", grad_heads, value_weight, preferred_element_type=f32).astype(bf16)
    probs = probs_low.astype(f32)
    grad_probs = jnp.einsum("thr,kr->htk", grad_mixture, key_rows[:, :R], preferred_element_type=f32)
    grad_scores = (probs * (grad_probs - jnp.sum(probs * grad_probs, axis=-1, keepdims=True))).astype(bf16)
    grad_keys_latent = jnp.einsum("htk,thr->kr", probs_low, grad_mixture, preferred_element_type=f32)
    grad_query_cat = score_scale * jnp.einsum("htk,kc->thc", grad_scores, key_rows, preferred_element_type=f32)
    grad_keys = score_scale * jnp.einsum("htk,thc->kc", grad_scores, query_cat, preferred_element_type=f32)
    grad_keys = (grad_keys + pad_to(grad_keys_latent, R + ROPE)).astype(bf16)
    grad_absorbed = grad_query_cat[..., :R].astype(bf16)
    d_key = jnp.einsum("thn,thr->hrn", queries[..., :NOPE], grad_absorbed, preferred_element_type=f32)
    grad_nope = jnp.einsum("thr,hrn->thn", grad_absorbed, key_weight, preferred_element_type=f32)
    grad_rope = rotary(grad_query_cat[..., R:], cosine[:, None], -sine_part[:, None])
    grad_queries = (
        jnp.concatenate([grad_nope, grad_rope], axis=-1)
        .astype(bf16)
        .reshape(row_count, local_heads * (NOPE + ROPE))
    )
    d_query = jnp.einsum("td,tq->dq", hidden, grad_queries, preferred_element_type=f32)
    grad_hidden_part = jnp.einsum("tq,dq->td", grad_queries, query_weight, preferred_element_type=f32)

    grad_keys = pick(
        grad_keys.reshape(16, row_count, R + ROPE),
        [yh * 8 + kx * 2 + kc for kc in (0, 1) for kx in range(4) for yh in (0, 1)],
        place,
    ).reshape(2, 4, 2, row_count, R + ROPE)
    grad_keys = total([grad_keys[0], swap(grad_keys[1], kc=1)])
    grad_keys = total([grad_keys[0]] + [swap(grad_keys[k], kx=k) for k in (1, 2, 3)])
    grad_keys = total([grad_keys[0], swap(grad_keys[1], ky=2)])
    own_key_grads = total([grad_keys] + [swap_z(grad_keys, k) for k in (1, 2, 3)], f32)
    grad_hidden = gather_z(scatter_z(grad_hidden_part.astype(bf16), z), z).astype(f32)

    grad_compact_in, d_gain_latent = norm_back(own_key_grads[:, :R], unit_latent, scale_latent, gain_latent)
    grad_key_rot = rotary(own_key_grads[:, R:], cosine, -sine_part)
    grad_latent = jnp.concatenate([grad_compact_in, grad_key_rot], axis=-1).astype(bf16)
    d_latent = jnp.einsum("td,tq->dq", hidden, grad_latent, preferred_element_type=f32)
    grad_hidden = grad_hidden + jnp.einsum("tq,dq->td", grad_latent, latent_weight, preferred_element_type=f32)
    grad_input_norm, d_gain_attn = norm_back(grad_hidden, unit_attn, scale_attn, gain_attn)
    grad_tokens = grad_middle + grad_input_norm

    d_aux = jnp.concatenate(
        [
            d_gain_attn.reshape(32, 1, db),
            d_gain_moe.reshape(32, 1, db),
            pad_to(d_gain_latent.reshape(32, 1, rb), db),
            jnp.zeros((32, 5, db), f32),
            jnp.swapaxes(d_router.reshape(32, db, E), 1, 2),
        ],
        axis=1,
    )
    d_aux = jnp.pad(d_aux, ((0, 0), (0, db - 16), (0, 0)))
    d_expand = jnp.concatenate([d_key, d_value], axis=-1).reshape(local_heads, 32, rb, NOPE + VD)
    d_expand = jnp.swapaxes(d_expand, 0, 1).reshape(32, db, NOPE + VD)
    grads = jnp.concatenate(
        [
            piece.astype(bf16)
            for piece in (
                d_query.reshape(32, db, -1),
                d_latent.reshape(32, db, -1),
                d_aux,
                d_out_t.reshape(32, db, -1),
                d_expand,
            )
        ],
        axis=2,
    )
    owned = scatter_plane(grads, me)
    cuts, edge = [], 0
    for piece in (w_query, w_latent, aux, w_out.T, expand_rows):
        cuts.append(owned[:, edge : edge + piece.shape[1]])
        edge += piece.shape[1]
    return (
        output,
        grad_tokens,
        cuts[2][0],
        cuts[0],
        cuts[1],
        cuts[2][2, :rb],
        jnp.concatenate(jnp.split(cuts[4], local_heads, axis=0), axis=1),
        cuts[3].T,
        cuts[2][1],
        cuts[2][8:16].T,
        d_routed[0],
        d_routed[1],
        jnp.swapaxes(d_routed[2], 1, 2),
        d_shared[0],
        d_shared[1],
        d_shared[2].T,
    )


def solution(mesh):
    rows = P(PLANE, None)
    split = P(PLANE, "tp")
    vector = P(PLANE)
    turned = P("tp", PLANE)
    expert_rows = P(None, PLANE, "tp")
    expert_columns = P(None, "tp", PLANE)
    return jax.shard_map(
        shards,
        mesh=mesh,
        in_specs=(
            rows,
            P("fsdp", None),
            rows,
            rows,
            vector,
            split,
            rows,
            vector,
            split,
            turned,
            vector,
            rows,
            expert_rows,
            expert_rows,
            expert_columns,
            split,
            split,
            turned,
        ),
        out_specs=(
            rows,
            rows,
            vector,
            split,
            rows,
            vector,
            split,
            turned,
            vector,
            rows,
            expert_rows,
            expert_rows,
            expert_columns,
            split,
            split,
            turned,
        ),
        check_vma=False,
    )
```

time: 2600 us -> 1980 us (0.76)
  waiting for transfers between devices: 2130 us -> 229 us
  Pallas kernels: 0 us -> 1190 us
  local copies, waits for them, and re-layouts: 62.8 us -> 259 us
  blocking collectives: 184 us -> 0 us
  starting transfers between devices: 1.59 us -> 142 us
  matrix products: 161 us -> 82.8 us
  other arithmetic: 29 us -> 60.5 us
    reduce_scatter x10 -> x0, waiting for transfers between devices: 1300 us -> none  [the longest x1 155 us: shards(): lax.psum_scatter(d_up.astype(jnp.bfloat16), ('fsdp', 'ctx'), scatter_dime...]
    pallas_call x0 -> x9, Pallas kernels: none -> 1190 us  [the longest x5 594 us: pick(): pl.pallas_call(kernel, out_shape=jax.ShapeDtypeStruct((len(order),) + sou...]
    all_gather x11 -> x0, waiting for transfers between devices: 572 us -> none  [the longest x1 72.9 us: shards(): lax.all_gather(w_up, ('fsdp', 'ctx'), axis=1, tiled=True)]
    ppermute x0 -> x107, waiting for transfers between devices: none -> 229 us  [the longest x80 145 us: swap(): return lax.ppermute(values, PLANE, [(i, i ^ bits) for i in range(32)])]
    unnamed x28 -> x0, waiting for transfers between devices: 206 us -> none
    ppermute x0 -> x107, starting transfers between devices: none -> 142 us  [the longest x80 95 us: swap(): return lax.ppermute(values, PLANE, [(i, i ^ bits) for i in range(32)])]
    unnamed x2 -> x0, blocking collectives: 135 us -> none
    dynamic_update_slice x0 -> x16, local copies, waits for them, and re-layouts: none -> 92.2 us  [gather_z(): out = lax.dynamic_update_slice_in_dim(out, piece, (z ^ k) * rows, 0)]
  transfers between devices with their start and end apart: 26 -> 107, of which waited for: 25 -> 45; matrix products, arithmetic and copies ran while one was open for 7% -> 17% of each run, Pallas kernels for 0% -> 60%
where the time goes in v1:
time: 1980 us; the launch traced here: 1960 us
  Pallas kernels  1190 us (60%)
  local copies, waits for them, and re-layouts  259 us (13%)
  waiting for transfers between devices  229 us (12%)
  starting transfers between devices  142 us (7%)
  matrix products  82.8 us (4%)
  other arithmetic  60.5 us (3%)
    pallas_call x5, Pallas kernels, pick(): pl.pallas_call(kernel, out_shape=jax.ShapeDtypeStruct((len(order),) + sou...  594 us
    pallas_call x4, Pallas kernels, arrange(): pl.pallas_call(kernel, out_shape=jax.ShapeDtypeStruct((count, rows, width...  593 us
    ppermute x80, waiting for transfers between devices, swap(): return lax.ppermute(values, PLANE, [(i, i ^ bits) for i in range(32)])  145 us
    ppermute x80, starting transfers between devices, swap(): return lax.ppermute(values, PLANE, [(i, i ^ bits) for i in range(32)])  95 us
    dynamic_update_slice x16, local copies, waits for them, and re-layouts, gather_z(): out = lax.dynamic_update_slice_in_dim(out, piece, (z ^ k) * rows, 0)  92.2 us
    ppermute x27, waiting for transfers between devices, swap_z(): return lax.ppermute(values, 'tp', [(i, i ^ k) for i in range(4)])  83.7 us
    ppermute x27, starting transfers between devices, swap_z(): return lax.ppermute(values, 'tp', [(i, i ^ k) for i in range(4)])  46.6 us
  transfers between devices with their start and end apart: 107, of which 45 were waited for; matrix products, arithmetic and copies ran while one was open for 17% of the time, Pallas kernels for 60%

profile of v1, /device:TPU:0, one launch (start us, length us, event | category | flops | bytes accessed | tf_op | source)
XLA Modules:
  0.0 1962.4 jit_solution(7721622970557967922)
XLA Ops:
  29.9 48.8 %shard_map.299 = bf16[8,192,512]{2,1,0:T(8,128)(2,1)} custom-call(s32[1]{0:T(128)} %bitcast.42.me_ref, bf16[8,192,512]{2,1,0:T(8,128)(2,1)} %bitcast.490), custom_call_target="tpu_custom_call" | custom-call | tf_op jit(solution)/shard_map/pallas_call | solution.py:80
  79.8 3.9 collective-permute-start.9
  85.7 4.1 collective-permute-start.8
  90.8 4.2 collective-permute-done.7.refs_3_
  97.8 8.8 collective-permute-done.9.refs_5_
  112.9 10.5 collective-permute-done.10.refs_6_
  132.4 271.7 %shard_map.297 = bf16[32,64,2176]{2,1,0:T(8,128)(2,1)} custom-call(s32[1]{0:T(128)} %bitcast.me_ref, bf16[4,32,2176]{2,1,0:T(8,128)(2,1)} %copy-done.39, bf16[4,32,2176]{2,1,0:T(8,128)(2,1)} %copy-done.38, bf16[4,32,2176]{2,1,0:T(8,128)(2,1)} %collective-permute-done.6.refs_2_, bf16[4,32,2176]{2,1,0:T(8,128)(2,1)} %copy-done.56, ...), custom_call_target="tpu_custom_call" | custom-call | tf_op jit(solution)/shard_map/pallas_call | solution.py:59
  427.5 5.2 collective-permute-done.49
  464.7 80.7 %shard_map.298 = bf16[16,128,576]{2,1,0:T(8,128)(2,1)} custom-call(s32[1]{0:T(128)} %bitcast.17.me_ref, bf16[4,128,576]{2,1,0:T(8,128)(2,1)} %copy-done.21, bf16[4,128,576]{2,1,0:T(8,128)(2,1)} %copy.345.refs_1_, bf16[4,128,576]{2,1,0:T(8,128)(2,1)} %copy.346.refs_2_, bf16[4,128,576]{2,1,0:T(8,128)(2,1)} %copy.347.refs_3_), custom_call_target="tpu_custom_call" | custom-call | tf_op jit(solution)/shard_map/pallas_call | solution.py:59
  545.4 7.0 fusion.144
  582.6 5.3 dynamic_update_slice.48
  589.9 192.0 %shard_map.300 = bf16[32,192,512]{2,1,0:T(8,128)(2,1)} custom-call(s32[1]{0:T(128)} %bitcast.me_ref, bf16[8,192,512]{2,1,0:T(8,128)(2,1)} %bitcast.81.refs_0_, bf16[8,192,512]{2,1,0:T(8,128)(2,1)} %bitcast.82.refs_1_, bf16[8,192,512]{2,1,0:T(8,128)(2,1)} %bitcast.83.refs_2_, bf16[8,192,512]{2,1,0:T(8,128)(2,1)} %bitcast.84.refs_3_), custom_call_target="tpu_custom_call" | custom-call | tf_op jit(solution)/shard_map/pallas_call | solution.py:59
  781.9 5.9 fusion.138
  789.6 6.1 dynamic_update_slice.49
  797.6 6.1 dynamic_update_slice.50
  805.6 6.1 dynamic_update_slice.51
  820.6 9.2 collective-permute-done.32
  831.3 11.1 collective-permute-done.33
  845.0 8.0 collective-permute-done.39
  853.2 10.1 collective-permute-done.40
  878.4 5.8 fusion.148
  884.5 6.1 add_convert_fusion.1
  904.9 4.4 convolution_convert_fusion
  909.3 3.8 collective-permute-done.64
  913.1 11.4 collective-permute-done.65
  937.0 192.0 %shard_map.304 = bf16[32,192,512]{2,1,0:T(8,128)(2,1)} custom-call(s32[1]{0:T(128)} %bitcast.me_ref, bf16[32,192,512]{2,1,0:T(8,128)(2,1)} %bitcast.471), custom_call_target="tpu_custom_call" | custom-call | tf_op jit(solution)/shard_map/pallas_call | solution.py:80
  1130.9 3.8 collective-permute-start.71
  1135.6 5.5 fusion.137
  1146.1 6.2 dynamic_update_slice.56
  1154.2 7.2 dynamic_update_slice.57
  1163.4 7.2 dynamic_update_slice.58
  1172.6 7.2 dynamic_update_slice.59
  1200.9 4.4 copy.386
  1205.2 80.7 %shard_map.301 = bf16[16,128,576]{2,1,0:T(8,128)(2,1)} custom-call(s32[1]{0:T(128)} %bitcast.17.me_ref, bf16[16,128,576]{2,1,0:T(8,128)(2,1)} %bitcast.482), custom_call_target="tpu_custom_call" | custom-call | tf_op jit(solution)/shard_map/pallas_call | solution.py:80
  1292.0 4.8 fusion.139
  1296.8 3.9 copy.367
  1300.7 4.2 copy.368
  1307.0 3.8 fusion.31
  1374.5 7.3 collective-permute-done.73
  1384.7 4.0 collective-permute-done.74
  1392.4 12.0 collective-permute-done.76
  1407.6 10.4 collective-permute-done.77
  1424.9 5.4 dynamic_update_slice.60
  1430.3 6.1 dynamic_update_slice.61
  1436.4 6.1 dynamic_update_slice.62
  1442.5 6.1 dynamic_update_slice.63
  1452.0 13.9 concatenate.115.src
  1465.9 136.2 %shard_map.303 = bf16[16,64,2176]{2,1,0:T(8,128)(2,1)} custom-call(s32[1]{0:T(128)} %bitcast.me_ref, bf16[32,64,2176]{2,1,0:T(8,128)(2,1)} %concatenate.115.src), custom_call_target="tpu_custom_call" | custom-call | tf_op jit(solution)/shard_map/pallas_call | solution.py:80
  1612.8 4.9 collective-permute-done.103
  1619.2 8.4 collective-permute-done.104
  1630.9 6.5 collective-permute-done.54
  1637.5 12.2 collective-permute-done.55
  1658.7 10.2 collective-permute-done.57
  1668.8 8.9 collective-permute-done.58
  1680.8 3.8 collective-permute-start.61
  1686.6 48.8 %shard_map.305 = bf16[8,192,512]{2,1,0:T(8,128)(2,1)} custom-call(s32[1]{0:T(128)} %bitcast.42.me_ref, bf16[4,192,512]{2,1,0:T(8,128)(2,1)} %get-tuple-element.164.refs_0_, bf16[4,192,512]{2,1,0:T(8,128)(2,1)} %copy-done.55), custom_call_target="tpu_custom_call" | custom-call | tf_op jit(solution)/shard_map/pallas_call | solution.py:59
  1748.4 5.8 dynamic_update_slice.53
  1754.2 5.8 dynamic_update_slice.54
  1763.6 136.2 %shard_map.302 = bf16[16,64,2176]{2,1,0:T(8,128)(2,1)} custom-call(s32[1]{0:T(128)} %bitcast.me_ref, bf16[32,64,2176]{2,1,0:T(8,128)(2,1)} %concatenate.115.src), custom_call_target="tpu_custom_call" | custom-call | tf_op jit(solution)/shard_map/pallas_call | solution.py:80
  1899.9 4.9 add_convert_fusion
  1916.3 4.1 collective-permute-done.88
  1929.9 4.4 collective-permute-done.95
  1946.8 4.3 collective-permute-start.92
  1951.2 4.4 collective-permute-done.92
  (637 shorter events, 411.0 us)
Async XLA Ops:
  4.7 74.1 %collective-permute-start.3 = (bf16[32,2176]{1,0:T(8,128)(2,1)S(1)}, bf16[32,2176]{1,0:T(8,128)(2,1)S(1)}, u32[]{:S(2)}, u32[]{:S(2)}) collective-permute-start(bf16[32,2176]{1,0:T(8,128)(2,1)S(1)} %get-tuple-element.216), channel_id=1, source_target_pairs={{0,64},{4,68},{8,72},{12,76},{16,80},{20,84},{24,88},{28,92},{32,9... | collective-permute-start | bytes 417800 | tf_op jit(solution)/shard_map/ppermute | solution.py:32
  6.4 72.8 %collective-permute-start.4 = (bf16[32,2176]{1,0:T(8,128)(2,1)S(1)}, bf16[32,2176]{1,0:T(8,128)(2,1)S(1)}, u32[]{:S(2)}, u32[]{:S(2)}) collective-permute-start(bf16[32,2176]{1,0:T(8,128)(2,1)S(1)} %get-tuple-element.216), channel_id=1, source_target_pairs={{0,32},{4,36},{8,40},{12,44},{16,48},{20,52},{24,56},{28,60},{32,0... | collective-permute-start | bytes 417800 | tf_op jit(solution)/shard_map/ppermute | solution.py:32
  9.3 70.0 %collective-permute-start.5 = (bf16[32,2176]{1,0:T(8,128)(2,1)S(1)}, bf16[32,2176]{1,0:T(8,128)(2,1)S(1)}, u32[]{:S(2)}, u32[]{:S(2)}) collective-permute-start(bf16[32,2176]{1,0:T(8,128)(2,1)S(1)} %get-tuple-element.216), channel_id=1, source_target_pairs={{0,96},{4,100},{8,104},{12,108},{16,112},{20,116},{24,120},{28,124... | collective-permute-start | bytes 417800 | tf_op jit(solution)/shard_map/ppermute | solution.py:32
  9.5 74.3 %collective-permute-start = (bf16[32,2176]{1,0:T(8,128)(2,1)S(1)}, bf16[32,2176]{1,0:T(8,128)(2,1)S(1)}, u32[]{:S(2)}, u32[]{:S(2)}) collective-permute-start(bf16[32,2176]{1,0:T(8,128)(2,1)S(1)} %get-tuple-element.217), channel_id=1, source_target_pairs={{0,8},{4,12},{8,0},{12,4},{16,24},{20,28},{24,16},{28,20},{32,40},... | collective-permute-start | bytes 417800 | tf_op jit(solution)/shard_map/ppermute | solution.py:32
  11.0 73.1 %collective-permute-start.1 = (bf16[32,2176]{1,0:T(8,128)(2,1)S(1)}, bf16[32,2176]{1,0:T(8,128)(2,1)S(1)}, u32[]{:S(2)}, u32[]{:S(2)}) collective-permute-start(bf16[32,2176]{1,0:T(8,128)(2,1)S(1)} %get-tuple-element.217), channel_id=1, source_target_pairs={{0,16},{4,20},{8,24},{12,28},{16,0},{20,4},{24,8},{28,12},{32,48},... | collective-permute-start | bytes 417800 | tf_op jit(solution)/shard_map/ppermute | solution.py:32
  79.8 26.8 %collective-permute-start.9 = (bf16[4,32,2176]{2,1,0:T(8,128)(2,1)S(1)}, bf16[4,32,2176]{2,1,0:T(8,128)(2,1)}, u32[]{:S(2)}, u32[]{:S(2)}) collective-permute-start(bf16[4,32,2176]{2,1,0:T(8,128)(2,1)S(1)} %pad_maximum_fusion.9.refs_1_), channel_id=1, source_target_pairs={{0,16},{4,20},{8,24},{12,28},{16,0},{20,4},{24,8},{28,12},{32,48},... | collective-permute-start | bytes 1671176 | tf_op jit(solution)/shard_map/ppermute | solution.py:32
  83.8 25.8 %collective-permute-start.11 = (bf16[4,32,2176]{2,1,0:T(8,128)(2,1)S(1)}, bf16[4,32,2176]{2,1,0:T(8,128)(2,1)}, u32[]{:S(2)}, u32[]{:S(2)}) collective-permute-start(bf16[4,32,2176]{2,1,0:T(8,128)(2,1)S(1)} %pad_maximum_fusion.9.refs_1_), channel_id=1, source_target_pairs={{0,24},{4,28},{8,16},{12,20},{16,8},{20,12},{24,0},{28,4},{32,56},... | collective-permute-start | bytes 1671176 | tf_op jit(solution)/shard_map/ppermute | solution.py:32
  85.2 24.3 %collective-permute-start.6 = (bf16[4,32,2176]{2,1,0:T(8,128)(2,1)S(1)}, bf16[4,32,2176]{2,1,0:T(8,128)(2,1)}, u32[]{:S(2)}, u32[]{:S(2)}) collective-permute-start(bf16[4,32,2176]{2,1,0:T(8,128)(2,1)S(1)} %pad_maximum_fusion.8.refs_0_), channel_id=1, source_target_pairs={{0,64},{4,68},{8,72},{12,76},{16,80},{20,84},{24,88},{28,92},{32,9... | collective-permute-start | bytes 1671176 | tf_op jit(solution)/shard_map/ppermute | solution.py:32
  85.7 26.0 %collective-permute-start.8 = (bf16[4,32,2176]{2,1,0:T(8,128)(2,1)S(1)}, bf16[4,32,2176]{2,1,0:T(8,128)(2,1)}, u32[]{:S(2)}, u32[]{:S(2)}) collective-permute-start(bf16[4,32,2176]{2,1,0:T(8,128)(2,1)S(1)} %pad_maximum_fusion.8.refs_0_), channel_id=1, source_target_pairs={{0,32},{4,36},{8,40},{12,44},{16,48},{20,52},{24,56},{28,60},{32,0... | collective-permute-start | bytes 1671176 | tf_op jit(solution)/shard_map/ppermute | solution.py:32
  95.8 28.3 %collective-permute-start.46 = (bf16[4,192,512]{2,1,0:T(8,128)(2,1)}, bf16[4,192,512]{2,1,0:T(8,128)(2,1)S(1)}, u32[]{:S(2)}, u32[]{:S(2)}) collective-permute-start(bf16[4,192,512]{2,1,0:T(8,128)(2,1)} %get-tuple-element.174), channel_id=1, source_target_pairs={{0,4},{4,0},{8,12},{12,8},{16,20},{20,16},{24,28},{28,24},{32,36},... | collective-permute-start | bytes 2359304 | tf_op jit(solution)/shard_map/ppermute | solution.py:32
  106.6 16.8 collective-permute-start.10
  127.1 300.3 %collective-permute-start.47 = (bf16[2,192,512]{2,1,0:T(8,128)(2,1)}, bf16[2,192,512]{2,1,0:T(8,128)(2,1)}, u32[]{:S(2)}, u32[]{:S(2)}) collective-permute-start(bf16[2,192,512]{2,1,0:T(8,128)(2,1)} %get-tuple-element.170), channel_id=1, source_target_pairs={{0,8},{4,12},{8,0},{12,4},{16,24},{20,28},{24,16},{28,20},{32,40},... | collective-permute-start | bytes 1179656 | tf_op jit(solution)/shard_map/ppermute | solution.py:32
  127.3 300.2 %collective-permute-start.48 = (bf16[2,192,512]{2,1,0:T(8,128)(2,1)}, bf16[2,192,512]{2,1,0:T(8,128)(2,1)}, u32[]{:S(2)}, u32[]{:S(2)}) collective-permute-start(bf16[2,192,512]{2,1,0:T(8,128)(2,1)} %get-tuple-element.172), channel_id=1, source_target_pairs={{0,16},{4,20},{8,24},{12,28},{16,0},{20,4},{24,8},{28,12},{32,48},... | collective-permute-start | bytes 1179656 | tf_op jit(solution)/shard_map/ppermute | solution.py:32
  426.4 18.5 collective-permute-start.23
  435.1 152.7 %collective-permute-start.50 = (bf16[4,2,192,512]{3,2,1,0:T(8,128)(2,1)}, bf16[4,2,192,512]{3,2,1,0:T(8,128)(2,1)}, u32[]{:S(2)}, u32[]{:S(2)}) collective-permute-start(bf16[4,2,192,512]{3,2,1,0:T(8,128)(2,1)} %pad_maximum_fusion.3), channel_id=1, source_target_pairs={{0,64},{4,68},{8,72},{12,76},{16,80},{20,84},{24,88},{28,92},{32,9... | collective-permute-start | bytes 4718600 | tf_op jit(solution)/shard_map/ppermute | solution.py:32
  435.1 154.7 %collective-permute-start.51 = (bf16[4,2,192,512]{3,2,1,0:T(8,128)(2,1)}, bf16[4,2,192,512]{3,2,1,0:T(8,128)(2,1)}, u32[]{:S(2)}, u32[]{:S(2)}) collective-permute-start(bf16[4,2,192,512]{3,2,1,0:T(8,128)(2,1)} %pad_maximum_fusion.3), channel_id=1, source_target_pairs={{0,32},{4,36},{8,40},{12,44},{16,48},{20,52},{24,56},{28,60},{32,0... | collective-permute-start | bytes 4718600 | tf_op jit(solution)/shard_map/ppermute | solution.py:32
  436.9 153.0 %collective-permute-start.52 = (bf16[4,2,192,512]{3,2,1,0:T(8,128)(2,1)}, bf16[4,2,192,512]{3,2,1,0:T(8,128)(2,1)}, u32[]{:S(2)}, u32[]{:S(2)}) collective-permute-start(bf16[4,2,192,512]{3,2,1,0:T(8,128)(2,1)} %pad_maximum_fusion.3), channel_id=1, source_target_pairs={{0,96},{4,100},{8,104},{12,108},{16,112},{20,116},{24,120},{28,124... | collective-permute-start | bytes 4718600 | tf_op jit(solution)/shard_map/ppermute | solution.py:32
  444.9 17.6 collective-permute-start.25
  578.0 209.7 %collective-permute-start.29 = (bf16[32,2048]{1,0:T(8,128)(2,1)}, bf16[32,2048]{1,0:T(8,128)(2,1)}, u32[]{:S(2)}, u32[]{:S(2)}) collective-permute-start(bf16[32,2048]{1,0:T(8,128)(2,1)} %add_convert_fusion.8), channel_id=1, source_target_pairs={{0,1},{1,0},{2,3},{3,2},{4,5},{5,4},{6,7},{7,6},{8,9},{9,8},{10,11... | collective-permute-start | bytes 393224 | tf_op jit(solution)/shard_map/ppermute | solution.py:36
  578.0 217.7 %collective-permute-start.30 = (bf16[32,2048]{1,0:T(8,128)(2,1)}, bf16[32,2048]{1,0:T(8,128)(2,1)}, u32[]{:S(2)}, u32[]{:S(2)}) collective-permute-start(bf16[32,2048]{1,0:T(8,128)(2,1)} %add_convert_fusion.8), channel_id=1, source_target_pairs={{0,2},{1,3},{2,0},{3,1},{4,6},{5,7},{6,4},{7,5},{8,10},{9,11},{10,... | collective-permute-start | bytes 393224 | tf_op jit(solution)/shard_map/ppermute | solution.py:36
  587.9 215.9 %collective-permute-start.31 = (bf16[32,2048]{1,0:T(8,128)(2,1)}, bf16[32,2048]{1,0:T(8,128)(2,1)}, u32[]{:S(2)}, u32[]{:S(2)}) collective-permute-start(bf16[32,2048]{1,0:T(8,128)(2,1)} %add_convert_fusion.8), channel_id=1, source_target_pairs={{0,3},{1,2},{2,1},{3,0},{4,7},{5,6},{6,5},{7,4},{8,11},{9,10},{10,... | collective-permute-start | bytes 393224 | tf_op jit(solution)/shard_map/ppermute | solution.py:36
  814.9 27.5 %collective-permute-start.33 = (bf16[128,2048]{0,1:T(8,128)(2,1)S(1)}, bf16[128,2048]{0,1:T(8,128)(2,1)S(1)}, u32[]{:S(2)}, u32[]{:S(2)}) collective-permute-start(bf16[128,2048]{0,1:T(8,128)(2,1)S(1)} %get-tuple-element.105), channel_id=1, source_target_pairs={{0,16},{4,20},{8,24},{12,28},{16,0},{20,4},{24,8},{28,12},{32,48},... | collective-permute-start | bytes 1572872 | tf_op jit(solution)/shard_map/ppermute | solution.py:32
  818.3 25.6 %collective-permute-start.34 = (bf16[128,2048]{0,1:T(8,128)(2,1)S(1)}, bf16[128,2048]{0,1:T(8,128)(2,1)S(1)}, u32[]{:S(2)}, u32[]{:S(2)}) collective-permute-start(bf16[128,2048]{0,1:T(8,128)(2,1)S(1)} %get-tuple-element.105), channel_id=1, source_target_pairs={{0,24},{4,28},{8,16},{12,20},{16,8},{20,12},{24,0},{28,4},{32,56},... | collective-permute-start | bytes 1572872 | tf_op jit(solution)/shard_map/ppermute | solution.py:32
  819.6 24.6 %collective-permute-start.35 = (bf16[128,2048]{0,1:T(8,128)(2,1)S(1)}, bf16[128,2048]{0,1:T(8,128)(2,1)S(1)}, u32[]{:S(2)}, u32[]{:S(2)}) collective-permute-start(bf16[128,2048]{0,1:T(8,128)(2,1)S(1)} %get-tuple-element.105), channel_id=1, source_target_pairs={{0,4},{4,0},{8,12},{12,8},{16,20},{20,16},{24,28},{28,24},{32,36},... | collective-permute-start | bytes 1572872 | tf_op jit(solution)/shard_map/ppermute | solution.py:32
  820.5 32.5 %collective-permute-start.39 = (bf16[128,2176]{0,1:T(8,128)(2,1)S(1)}, bf16[128,2176]{0,1:T(8,128)(2,1)S(1)}, u32[]{:S(2)}, u32[]{:S(2)}) collective-permute-start(bf16[128,2176]{0,1:T(8,128)(2,1)S(1)} %get-tuple-element.191), channel_id=1, source_target_pairs={{0,8},{4,12},{8,0},{12,4},{16,24},{20,28},{24,16},{28,20},{32,40},... | collective-permute-start | bytes 1671176 | tf_op jit(solution)/shard_map/ppermute | solution.py:32
  829.8 33.5 %collective-permute-start.40 = (bf16[128,2176]{0,1:T(8,128)(2,1)S(1)}, bf16[128,2176]{0,1:T(8,128)(2,1)S(1)}, u32[]{:S(2)}, u32[]{:S(2)}) collective-permute-start(bf16[128,2176]{0,1:T(8,128)(2,1)S(1)} %get-tuple-element.191), channel_id=1, source_target_pairs={{0,16},{4,20},{8,24},{12,28},{16,0},{20,4},{24,8},{28,12},{32,48},... | collective-permute-start | bytes 1671176 | tf_op jit(solution)/shard_map/ppermute | solution.py:32
  842.4 23.4 %collective-permute-start.41 = (bf16[128,2176]{0,1:T(8,128)(2,1)S(1)}, bf16[128,2176]{0,1:T(8,128)(2,1)S(1)}, u32[]{:S(2)}, u32[]{:S(2)}) collective-permute-start(bf16[128,2176]{0,1:T(8,128)(2,1)S(1)} %get-tuple-element.191), channel_id=1, source_target_pairs={{0,24},{4,28},{8,16},{12,20},{16,8},{20,12},{24,0},{28,4},{32,56},... | collective-permute-start | bytes 1671176 | tf_op jit(solution)/shard_map/ppermute | solution.py:32
  843.9 22.1 %collective-permute-start.42 = (bf16[128,2176]{0,1:T(8,128)(2,1)S(1)}, bf16[128,2176]{0,1:T(8,128)(2,1)S(1)}, u32[]{:S(2)}, u32[]{:S(2)}) collective-permute-start(bf16[128,2176]{0,1:T(8,128)(2,1)S(1)} %get-tuple-element.191), channel_id=1, source_target_pairs={{0,4},{4,0},{8,12},{12,8},{16,20},{20,16},{24,28},{28,24},{32,36},... | collective-permute-start | bytes 1671176 | tf_op jit(solution)/shard_map/ppermute | solution.py:32
  844.2 22.6 %collective-permute-start.36 = (bf16[128,2048]{0,1:T(8,128)(2,1)S(1)}, bf16[128,2048]{0,1:T(8,128)(2,1)S(1)}, u32[]{:S(2)}, u32[]{:S(2)}) collective-permute-start(bf16[128,2048]{0,1:T(8,128)(2,1)S(1)} %collective-permute-done.32), channel_id=1, source_target_pairs={{0,4},{4,0},{8,12},{12,8},{16,20},{20,16},{24,28},{28,24},{32,36},... | collective-permute-start | bytes 1572872 | tf_op jit(solution)/shard_map/ppermute | solution.py:32
  897.6 26.9 %collective-permute-start.65 = (bf16[4,32,2176]{2,1,0:T(8,128)(2,1)S(1)}, bf16[4,32,2176]{2,1,0:T(8,128)(2,1)S(1)}, u32[]{:S(2)}, u32[]{:S(2)}) collective-permute-start(bf16[4,32,2176]{2,1,0:T(8,128)(2,1)S(1)} %get-tuple-element.159), channel_id=1, source_target_pairs={{0,2},{1,3},{2,0},{3,1},{4,6},{5,7},{6,4},{7,5},{8,10},{9,11},{10,... | collective-permute-start | bytes 1671176 | tf_op jit(solution)/shard_map/ppermute | solution.py:36
  900.0 27.3 %collective-permute-start.66 = (bf16[4,32,2176]{2,1,0:T(8,128)(2,1)S(1)}, bf16[4,32,2176]{2,1,0:T(8,128)(2,1)S(1)}, u32[]{:S(2)}, u32[]{:S(2)}) collective-permute-start(bf16[4,32,2176]{2,1,0:T(8,128)(2,1)S(1)} %get-tuple-element.158), channel_id=1, source_target_pairs={{0,3},{1,2},{2,1},{3,0},{4,7},{5,6},{6,5},{7,4},{8,11},{9,10},{10,... | collective-permute-start | bytes 1671176 | tf_op jit(solution)/shard_map/ppermute | solution.py:36
  929.2 199.8 %collective-permute-start.67 = (bf16[32,2176]{1,0:T(8,128)(2,1)}, bf16[32,2176]{1,0:T(8,128)(2,1)}, u32[]{:S(2)}, u32[]{:S(2)}) collective-permute-start(bf16[32,2176]{1,0:T(8,128)(2,1)} %get-tuple-element.188), channel_id=1, source_target_pairs={{0,8},{4,12},{8,0},{12,4},{16,24},{20,28},{24,16},{28,20},{32,40},... | collective-permute-start | bytes 417800 | tf_op jit(solution)/shard_map/ppermute | solution.py:32
  929.2 199.8 %collective-permute-start.68 = (bf16[32,2176]{1,0:T(8,128)(2,1)}, bf16[32,2176]{1,0:T(8,128)(2,1)}, u32[]{:S(2)}, u32[]{:S(2)}) collective-permute-start(bf16[32,2176]{1,0:T(8,128)(2,1)} %get-tuple-element.190), channel_id=1, source_target_pairs={{0,16},{4,20},{8,24},{12,28},{16,0},{20,4},{24,8},{28,12},{32,48},... | collective-permute-start | bytes 417800 | tf_op jit(solution)/shard_map/ppermute | solution.py:32
  932.0 197.0 %collective-permute-start.69 = (bf16[32,2176]{1,0:T(8,128)(2,1)}, bf16[32,2176]{1,0:T(8,128)(2,1)}, u32[]{:S(2)}, u32[]{:S(2)}) collective-permute-start(bf16[32,2176]{1,0:T(8,128)(2,1)} %get-tuple-element.189), channel_id=1, source_target_pairs={{0,24},{4,28},{8,16},{12,20},{16,8},{20,12},{24,0},{28,4},{32,56},... | collective-permute-start | bytes 417800 | tf_op jit(solution)/shard_map/ppermute | solution.py:32
  1130.9 21.4 %collective-permute-start.70 = (bf16[32,2176]{1,0:T(8,128)(2,1)}, bf16[32,2176]{1,0:T(8,128)(2,1)}, u32[]{:S(2)}, u32[]{:S(2)}) collective-permute-start(bf16[32,2176]{1,0:T(8,128)(2,1)} %fusion.99), channel_id=1, source_target_pairs={{0,1},{1,0},{2,3},{3,2},{4,5},{5,4},{6,7},{7,6},{8,9},{9,8},{10,11... | collective-permute-start | bytes 417800 | tf_op jit(solution)/shard_map/ppermute | solution.py:36
  1130.9 30.6 %collective-permute-start.71 = (bf16[32,2176]{1,0:T(8,128)(2,1)}, bf16[32,2176]{1,0:T(8,128)(2,1)}, u32[]{:S(2)}, u32[]{:S(2)}) collective-permute-start(bf16[32,2176]{1,0:T(8,128)(2,1)} %fusion.99), channel_id=1, source_target_pairs={{0,2},{1,3},{2,0},{3,1},{4,6},{5,7},{6,4},{7,5},{8,10},{9,11},{10,... | collective-permute-start | bytes 417800 | tf_op jit(solution)/shard_map/ppermute | solution.py:36
  1134.7 36.0 %collective-permute-start.72 = (bf16[32,2176]{1,0:T(8,128)(2,1)}, bf16[32,2176]{1,0:T(8,128)(2,1)}, u32[]{:S(2)}, u32[]{:S(2)}) collective-permute-start(bf16[32,2176]{1,0:T(8,128)(2,1)} %fusion.99), channel_id=1, source_target_pairs={{0,3},{1,2},{2,1},{3,0},{4,7},{5,6},{6,5},{7,4},{8,11},{9,10},{10,... | collective-permute-start | bytes 417800 | tf_op jit(solution)/shard_map/ppermute | solution.py:36
  1141.1 461.1 %collective-permute-start.100 = (bf16[4,2,192,512]{3,2,1,0:T(8,128)(2,1)}, bf16[4,2,192,512]{3,2,1,0:T(8,128)(2,1)}, u32[]{:S(2)}, u32[]{:S(2)}) collective-permute-start(bf16[4,2,192,512]{3,2,1,0:T(8,128)(2,1)} %bitcast.161), channel_id=1, source_target_pairs={{0,64},{4,68},{8,72},{12,76},{16,80},{20,84},{24,88},{28,92},{32,9... | collective-permute-start | bytes 4718600 | tf_op jit(solution)/shard_map/ppermute | solution.py:32
  1141.1 461.1 %collective-permute-start.101 = (bf16[4,2,192,512]{3,2,1,0:T(8,128)(2,1)}, bf16[4,2,192,512]{3,2,1,0:T(8,128)(2,1)}, u32[]{:S(2)}, u32[]{:S(2)}) collective-permute-start(bf16[4,2,192,512]{3,2,1,0:T(8,128)(2,1)} %bitcast.162), channel_id=1, source_target_pairs={{0,32},{4,36},{8,40},{12,44},{16,48},{20,52},{24,56},{28,60},{32,0... | collective-permute-start | bytes 4718600 | tf_op jit(solution)/shard_map/ppermute | solution.py:32
  1291.8 21.3 %collective-permute-start.79 = (bf16[4,2,128,576]{2,3,1,0:T(8,128)(2,1)}, bf16[4,2,128,576]{2,3,1,0:T(8,128)(2,1)}, u32[]{:S(2)}, u32[]{:S(2)}) collective-permute-start(bf16[4,2,128,576]{2,3,1,0:T(8,128)(2,1)} %copy.387), channel_id=1, source_target_pairs={{0,4},{4,0},{8,12},{12,8},{16,20},{20,16},{24,28},{28,24},{32,36},... | collective-permute-start | bytes 3538952 | tf_op jit(solution)/shard_map/ppermute | solution.py:32
  1319.7 18.3 collective-permute-start.81
  1322.5 18.1 collective-permute-start.82
  1366.9 21.8 %collective-permute-start.74 = (bf16[32,2048]{0,1:T(8,128)(2,1)S(1)}, bf16[32,2048]{0,1:T(8,128)(2,1)S(1)}, u32[]{:S(2)}, u32[]{:S(2)}) collective-permute-start(bf16[32,2048]{0,1:T(8,128)(2,1)S(1)} %get-tuple-element.195), channel_id=1, source_target_pairs={{0,2},{1,3},{2,0},{3,1},{4,6},{5,7},{6,4},{7,5},{8,10},{9,11},{10,... | collective-permute-start | bytes 393224 | tf_op jit(solution)/shard_map/ppermute | solution.py:36
  1369.2 22.0 %collective-permute-start.75 = (bf16[32,2048]{0,1:T(8,128)(2,1)S(1)}, bf16[32,2048]{0,1:T(8,128)(2,1)S(1)}, u32[]{:S(2)}, u32[]{:S(2)}) collective-permute-start(bf16[32,2048]{0,1:T(8,128)(2,1)S(1)} %get-tuple-element.194), channel_id=1, source_target_pairs={{0,3},{1,2},{2,1},{3,0},{4,7},{5,6},{6,5},{7,4},{8,11},{9,10},{10,... | collective-permute-start | bytes 393224 | tf_op jit(solution)/shard_map/ppermute | solution.py:36
  1381.8 220.5 %collective-permute-start.102 = (bf16[4,2,192,512]{3,2,1,0:T(8,128)(2,1)}, bf16[4,2,192,512]{3,2,1,0:T(8,128)(2,1)}, u32[]{:S(2)}, u32[]{:S(2)}) collective-permute-start(bf16[4,2,192,512]{3,2,1,0:T(8,128)(2,1)} %bitcast.163), channel_id=1, source_target_pairs={{0,96},{4,100},{8,104},{12,108},{16,112},{20,116},{24,120},{28,124... | collective-permute-start | bytes 4718600 | tf_op jit(solution)/shard_map/ppermute | solution.py:32
  1388.7 221.9 %collective-permute-start.53 = (bf16[4,128,2048]{1,2,0:T(8,128)(2,1)}, bf16[4,128,2048]{1,2,0:T(8,128)(2,1)}, u32[]{:S(2)}, u32[]{:S(2)}) collective-permute-start(bf16[4,128,2048]{1,2,0:T(8,128)(2,1)} %copy.367), channel_id=1, source_target_pairs={{0,4},{4,0},{8,12},{12,8},{16,20},{20,16},{24,28},{28,24},{32,36},... | collective-permute-start | bytes 6291464 | tf_op jit(solution)/shard_map/ppermute | solution.py:32
  1418.0 24.4 %collective-permute-start.78 = (bf16[32,2048]{0,1:T(8,128)(2,1)}, bf16[32,2048]{0,1:T(8,128)(2,1)}, u32[]{:S(2)}, u32[]{:S(2)}) collective-permute-start(bf16[32,2048]{0,1:T(8,128)(2,1)} %add_convert_fusion.4), channel_id=1, source_target_pairs={{0,3},{1,2},{2,1},{3,0},{4,7},{5,6},{6,5},{7,4},{8,11},{9,10},{10,... | collective-permute-start | bytes 393224 | tf_op jit(solution)/shard_map/ppermute | solution.py:36
  1602.1 297.8 %collective-permute-start.87 = (bf16[16,64,2176]{2,1,0:T(8,128)(2,1)}, bf16[16,64,2176]{2,1,0:T(8,128)(2,1)}, u32[]{:S(2)}, u32[]{:S(2)}) collective-permute-start(bf16[16,64,2176]{2,1,0:T(8,128)(2,1)} %shard_map.303), channel_id=1, source_target_pairs={{0,4},{4,0},{8,12},{12,8},{16,20},{20,16},{24,28},{28,24},{32,36},... | collective-permute-start | bytes 13369352 | tf_op jit(solution)/shard_map/ppermute | solution.py:32
  1605.9 21.7 %collective-permute-start.104 = (bf16[2,192,512]{2,1,0:T(8,128)(2,1)S(1)}, bf16[2,192,512]{2,1,0:T(8,128)(2,1)S(1)}, u32[]{:S(2)}, u32[]{:S(2)}) collective-permute-start(bf16[2,192,512]{2,1,0:T(8,128)(2,1)S(1)} %get-tuple-element.167), channel_id=1, source_target_pairs={{0,16},{4,20},{8,24},{12,28},{16,0},{20,4},{24,8},{28,12},{32,48},... | collective-permute-start | bytes 1179656 | tf_op jit(solution)/shard_map/ppermute | solution.py:32
  1609.2 20.6 %collective-permute-start.105 = (bf16[2,192,512]{2,1,0:T(8,128)(2,1)S(1)}, bf16[2,192,512]{2,1,0:T(8,128)(2,1)S(1)}, u32[]{:S(2)}, u32[]{:S(2)}) collective-permute-start(bf16[2,192,512]{2,1,0:T(8,128)(2,1)S(1)} %get-tuple-element.166), channel_id=1, source_target_pairs={{0,24},{4,28},{8,16},{12,20},{16,8},{20,12},{24,0},{28,4},{32,56},... | collective-permute-start | bytes 1179656 | tf_op jit(solution)/shard_map/ppermute | solution.py:32
  1612.8 24.7 %collective-permute-start.54 = (bf16[128,2048]{0,1:T(8,128)(2,1)S(1)}, bf16[128,2048]{0,1:T(8,128)(2,1)S(1)}, u32[]{:S(2)}, u32[]{:S(2)}) collective-permute-start(bf16[128,2048]{0,1:T(8,128)(2,1)S(1)} %get-tuple-element.160), channel_id=1, source_target_pairs={{0,8},{4,12},{8,0},{12,4},{16,24},{20,28},{24,16},{28,20},{32,40},... | collective-permute-start | bytes 1572872 | tf_op jit(solution)/shard_map/ppermute | solution.py:32
  1617.8 31.9 %collective-permute-start.55 = (bf16[128,2048]{0,1:T(8,128)(2,1)S(1)}, bf16[128,2048]{0,1:T(8,128)(2,1)S(1)}, u32[]{:S(2)}, u32[]{:S(2)}) collective-permute-start(bf16[128,2048]{0,1:T(8,128)(2,1)S(1)} %get-tuple-element.162), channel_id=1, source_target_pairs={{0,16},{4,20},{8,24},{12,28},{16,0},{20,4},{24,8},{28,12},{32,48},... | collective-permute-start | bytes 1572872 | tf_op jit(solution)/shard_map/ppermute | solution.py:32
  1627.5 25.6 %collective-permute-start.56 = (bf16[128,2048]{0,1:T(8,128)(2,1)S(1)}, bf16[128,2048]{0,1:T(8,128)(2,1)S(1)}, u32[]{:S(2)}, u32[]{:S(2)}) collective-permute-start(bf16[128,2048]{0,1:T(8,128)(2,1)S(1)} %get-tuple-element.161), channel_id=1, source_target_pairs={{0,24},{4,28},{8,16},{12,20},{16,8},{20,12},{24,0},{28,4},{32,56},... | collective-permute-start | bytes 1572872 | tf_op jit(solution)/shard_map/ppermute | solution.py:32
  1630.9 54.8 %collective-permute-start.106 = (bf16[4,192,512]{2,1,0:T(8,128)(2,1)S(1)}, bf16[4,192,512]{2,1,0:T(8,128)(2,1)S(1)}, u32[]{:S(2)}, u32[]{:S(2)}) collective-permute-start(bf16[4,192,512]{2,1,0:T(8,128)(2,1)S(1)} %get-tuple-element.163), channel_id=1, source_target_pairs={{0,4},{4,0},{8,12},{12,8},{16,20},{20,16},{24,28},{28,24},{32,36},... | collective-permute-start | bytes 2359304 | tf_op jit(solution)/shard_map/ppermute | solution.py:32
  1654.0 23.8 %collective-permute-start.58 = (bf16[32,2048]{0,1:T(8,128)(2,1)S(1)}, bf16[32,2048]{0,1:T(8,128)(2,1)S(1)}, u32[]{:S(2)}, u32[]{:S(2)}) collective-permute-start(bf16[32,2048]{0,1:T(8,128)(2,1)S(1)} %get-tuple-element.198), channel_id=1, source_target_pairs={{0,2},{1,3},{2,0},{3,1},{4,6},{5,7},{6,4},{7,5},{8,10},{9,11},{10,... | collective-permute-start | bytes 393224 | tf_op jit(solution)/shard_map/ppermute | solution.py:36
  1656.3 24.1 %collective-permute-start.59 = (bf16[32,2048]{0,1:T(8,128)(2,1)S(1)}, bf16[32,2048]{0,1:T(8,128)(2,1)S(1)}, u32[]{:S(2)}, u32[]{:S(2)}) collective-permute-start(bf16[32,2048]{0,1:T(8,128)(2,1)S(1)} %get-tuple-element.197), channel_id=1, source_target_pairs={{0,3},{1,2},{2,1},{3,0},{4,7},{5,6},{6,5},{7,4},{8,11},{9,10},{10,... | collective-permute-start | bytes 393224 | tf_op jit(solution)/shard_map/ppermute | solution.py:36
  1680.7 67.7 %collective-permute-start.60 = (bf16[32,2048]{0,1:T(8,128)(2,1)S(1)}, bf16[32,2048]{0,1:T(8,128)(2,1)}, u32[]{:S(2)}, u32[]{:S(2)}) collective-permute-start(bf16[32,2048]{0,1:T(8,128)(2,1)S(1)} %add_convert_fusion.6), channel_id=1, source_target_pairs={{0,1},{1,0},{2,3},{3,2},{4,5},{5,4},{6,7},{7,6},{8,9},{9,8},{10,11... | collective-permute-start | bytes 393224 | tf_op jit(solution)/shard_map/ppermute | solution.py:36
  1680.8 73.4 %collective-permute-start.61 = (bf16[32,2048]{0,1:T(8,128)(2,1)S(1)}, bf16[32,2048]{0,1:T(8,128)(2,1)}, u32[]{:S(2)}, u32[]{:S(2)}) collective-permute-start(bf16[32,2048]{0,1:T(8,128)(2,1)S(1)} %add_convert_fusion.6), channel_id=1, source_target_pairs={{0,2},{1,3},{2,0},{3,1},{4,6},{5,7},{6,4},{7,5},{8,10},{9,11},{10,... | collective-permute-start | bytes 393224 | tf_op jit(solution)/shard_map/ppermute | solution.py:36
  1684.6 75.3 %collective-permute-start.62 = (bf16[32,2048]{0,1:T(8,128)(2,1)S(1)}, bf16[32,2048]{0,1:T(8,128)(2,1)S(1)}, u32[]{:S(2)}, u32[]{:S(2)}) collective-permute-start(bf16[32,2048]{0,1:T(8,128)(2,1)S(1)} %add_convert_fusion.6), channel_id=1, source_target_pairs={{0,3},{1,2},{2,1},{3,0},{4,7},{5,6},{6,5},{7,4},{8,11},{9,10},{10,... | collective-permute-start | bytes 393224 | tf_op jit(solution)/shard_map/ppermute | solution.py:36
  1905.9 21.4 %collective-permute-start.89 = (bf16[4,32,2176]{2,1,0:T(8,128)(2,1)}, bf16[4,32,2176]{2,1,0:T(8,128)(2,1)}, u32[]{:S(2)}, u32[]{:S(2)}) collective-permute-start(bf16[4,32,2176]{2,1,0:T(8,128)(2,1)} %get-tuple-element.122), channel_id=1, source_target_pairs={{0,16},{4,20},{8,24},{12,28},{16,0},{20,4},{24,8},{28,12},{32,48},... | collective-permute-start | bytes 1671176 | tf_op jit(solution)/shard_map/ppermute | solution.py:32
  1908.7 21.2 %collective-permute-start.90 = (bf16[4,32,2176]{2,1,0:T(8,128)(2,1)S(1)}, bf16[4,32,2176]{2,1,0:T(8,128)(2,1)}, u32[]{:S(2)}, u32[]{:S(2)}) collective-permute-start(bf16[4,32,2176]{2,1,0:T(8,128)(2,1)S(1)} %get-tuple-element.121), channel_id=1, source_target_pairs={{0,24},{4,28},{8,16},{12,20},{16,8},{20,12},{24,0},{28,4},{32,56},... | collective-permute-start | bytes 1671176 | tf_op jit(solution)/shard_map/ppermute | solution.py:32
  1911.9 18.0 collective-permute-start.94
  1913.7 20.6 %collective-permute-start.95 = (bf16[4,32,2176]{2,1,0:T(8,128)(2,1)}, bf16[4,32,2176]{2,1,0:T(8,128)(2,1)}, u32[]{:S(2)}, u32[]{:S(2)}) collective-permute-start(bf16[4,32,2176]{2,1,0:T(8,128)(2,1)} %get-tuple-element.118), channel_id=1, source_target_pairs={{0,32},{4,36},{8,40},{12,44},{16,48},{20,52},{24,56},{28,60},{32,0... | collective-permute-start | bytes 1671176 | tf_op jit(solution)/shard_map/ppermute | solution.py:32
  1920.4 17.4 collective-permute-start.96
  (152 other events, 3779.4 us)

commit v2 on v1

v2 whole, which is shorter than its diff:
```python
import math

import jax
import jax.numpy as jnp
from jax import lax
from jax.experimental import pallas as pl
from jax.experimental.pallas import tpu as pltpu
from jax.sharding import Mesh
from jax.sharding import PartitionSpec as P

NOPE = 128
ROPE = 64
VD = 128
R = 512
E = 8
FF_PAD = 384
SH_PAD = 128
HEADS = 4

epsilon = 1e-06
rope_base = 50000.0
route_scale = 2.446
bf16 = jnp.bfloat16
f32 = jnp.float32

PLANE = ("yl", "yh", "x", "c")
YS = ("yl", "yh")


def mask(ky=0, kx=0, kc=0):
    return (ky & 1) * 16 + (ky >> 1) * 8 + kx * 2 + kc


def swap(values, ky=0, kx=0, kc=0):
    bits = mask(ky, kx, kc)
    return lax.ppermute(values, PLANE, [(i, i ^ bits) for i in range(32)])


def swap_z(values, k):
    return lax.ppermute(values, "z", [(i, i ^ k) for i in range(4)])


def total(parts, dtype=bf16):
    out = parts[0].astype(f32)
    for part in parts[1:]:
        out = out + part.astype(f32)
    return out.astype(dtype)


def nn(left, right):
    return jnp.dot(left, right, preferred_element_type=f32)


def nt(left, right):
    return lax.dot_general(left, right, (((1,), (1,)), ((), ())), preferred_element_type=f32)


def tn(left, right):
    return lax.dot_general(left, right, (((0,), (0,)), ((), ())), preferred_element_type=f32)


def lanes(shape):
    return lax.broadcasted_iota(jnp.int32, shape, 1)


def high_low(values):
    high = values.astype(bf16)
    return high, (values - high.astype(f32)).astype(bf16)


def start_all(copies, sem):
    for source, destination in copies:
        pltpu.make_async_copy(source, destination, sem).start()


def wait_for(ref, sem):
    pltpu.make_async_copy(ref, ref, sem).wait()


def call(kernel, outs, ins, scratch, macs=0, vmem=60, after=()):
    count, late = len(ins), len(after)
    body = kernel
    if late:

        def body(*refs):
            kernel(*refs[:count], *refs[count + late :])

    moved = sum(array.size * array.dtype.itemsize for array, _ in ins)
    moved += sum(math.prod(shape) * jnp.dtype(dtype).itemsize for shape, dtype, _ in outs)
    spaces = {"s": pltpu.SMEM, "v": pltpu.VMEM, "a": pl.ANY}
    return pl.pallas_call(
        body,
        out_shape=[jax.ShapeDtypeStruct(shape, dtype) for shape, dtype, _ in outs],
        in_specs=[pl.BlockSpec(memory_space=spaces[space]) for _, space in ins]
        + [pl.BlockSpec(memory_space=pl.ANY)] * late,
        out_specs=[pl.BlockSpec(memory_space=spaces[space]) for _, _, space in outs],
        scratch_shapes=scratch,
        compiler_params=pltpu.CompilerParams(vmem_limit_bytes=vmem << 20),
        cost_estimate=pl.CostEstimate(flops=4 * macs, bytes_accessed=moved, transcendentals=0),
    )(*[array for array, _ in ins], *after)


def exchange(blocks, axes):
    return lax.all_to_all(blocks, axes, 0, 0, tiled=True)


def gather(copies, axes, after):
    own = hold(exchange(copies, axes), *after)
    return [own, swap(own, kc=1)]


def pair_copies(parts, core, target, columns=None):
    if columns is not None:
        parts = [part.at[:, :, columns] for part in parts]
    return [(parts[0], target.at[:, core]), (parts[1], target.at[:, 1 - core])]


def hold(values, *after):
    def kernel(*refs):
        pass

    return pl.pallas_call(
        kernel,
        out_shape=jax.ShapeDtypeStruct(values.shape, values.dtype),
        in_specs=[pl.BlockSpec(memory_space=pl.ANY)] * (1 + len(after)),
        out_specs=pl.BlockSpec(memory_space=pl.ANY),
        input_output_aliases={0: 0},
    )(values, *after)


def tie(values, *after):
    late = sum(jnp.abs(lax.slice(one, (0,) * one.ndim, (1,) * one.ndim).reshape(()).astype(f32)) for one in after)
    return values + jnp.where(late > 3e38, 1.0, 0.0).astype(values.dtype)


def pack_attention(w_query, w_latent, attn_gain, moe_gain, latent_gain, router_t, out_t, w_expand):
    db = w_query.shape[0]
    query = w_query.shape[1]
    late = w_latent.shape[1]
    out = out_t.shape[1]
    per_head = NOPE + ROPE

    def kernel(q, lat, ag, mg, lg, rt, ot, ex, a, b):
        plain = [q[:, h * per_head : h * per_head + NOPE] for h in range(HEADS)]
        front = [q[:, h * per_head + NOPE : h * per_head + NOPE + ROPE // 2] for h in range(HEADS)]
        back = [q[:, h * per_head + NOPE + ROPE // 2 : (h + 1) * per_head] for h in range(HEADS)]
        rb = lg.shape[1]
        small = jnp.concatenate(
            [
                ag[...].astype(f32),
                mg[...].astype(f32),
                jnp.concatenate([lg[...].astype(f32), jnp.zeros((1, db - rb), f32)], axis=1),
                jnp.zeros((5, db), f32),
                rt[...].astype(f32),
            ]
            + ([jnp.zeros((db - 16, db), f32)] if db > 16 else []),
            axis=0,
        ).astype(bf16)
        one = jnp.concatenate(plain + front + back + [lat[...], small], axis=1)
        for n in range(16):
            a[n] = one
        width = ex.shape[1] // HEADS
        expand = jnp.concatenate([ex[:, h * width : (h + 1) * width] for h in range(HEADS)], axis=0)
        b[...] = jnp.concatenate([ot[...], expand], axis=1)

    one, two = query + late + db, out + w_expand.shape[1] // HEADS
    ins = [w_query, w_latent, attn_gain[None], moe_gain[None], latent_gain[None], router_t, out_t, w_expand]
    return call(
        kernel,
        [((16, db, one), bf16, "v"), ((db, two), bf16, "v")],
        [(array, "v") for array in ins],
        [],
    )


def pack_experts(info, gate, up, down_t, shared_gate, shared_up, shared_down_t, router):
    count, db, ff = gate.shape
    sh = shared_gate.shape[1] // count
    wide = FF_PAD + SH_PAD

    def kernel(info, g, u, d, sg, su, sd, rt, keep, send, packed, sem):
        fill = FF_PAD - ff - count
        for n, (routed, shared) in enumerate(((g, sg), (u, su), (d, sd))):
            extra = rt[...] if n == 0 else jnp.zeros((db, count), bf16)
            for e in range(count):
                packed[e, n] = jnp.concatenate(
                    [
                        routed[e],
                        extra,
                        jnp.zeros((db, fill), bf16),
                        shared[:, e * sh : (e + 1) * sh],
                        jnp.zeros((db, SH_PAD - sh), bf16),
                    ],
                    axis=1,
                )
        copies = []
        for kx in range(4):
            copies.append((packed.at[info[2] ^ (kx * 2)], keep.at[kx], sem.at[0]))
            copies.append((packed.at[info[2] ^ (kx * 2 + 1)], send.at[kx], sem.at[1]))
        for source, destination, which in copies:
            pltpu.make_async_copy(source, destination, which).start()
        wait_for(keep, sem.at[0])
        wait_for(send, sem.at[1])

    ins = [gate, up, down_t, shared_gate, shared_up, shared_down_t, router]
    return call(
        kernel,
        [((4, 3, db, wide), bf16, "a")] * 2,
        [(info, "s")] + [(array, "v") for array in ins],
        [pltpu.VMEM((count, 3, db, wide), bf16), pltpu.SemaphoreType.DMA((2,))],
    )


def project(info, tokens, cos4, sin4, parts, after):
    rows, width = tokens.shape
    db = width // 32
    rb = R // 32
    query = HEADS * (NOPE + ROPE)
    tile = ROPE + db
    half = ROPE // 2
    columns = query + R + tile

    def kernel(info, tok, cos, sin, *refs):
        ins, refs = refs[: len(parts)], refs[len(parts) :]
        hidden, q_nope, q_rope, keys, latent_out, small, gain_row, pairs, sem = refs
        start_all(pair_copies(ins, info[1] % 2, pairs), sem)
        x = tok[...].astype(f32)
        inverse = lax.rsqrt(jnp.mean(x * x, axis=-1, keepdims=True) + epsilon)
        unit = x * inverse
        wait_for(pairs, sem)
        weights = pairs.reshape(32, db, columns)
        lane = lanes((16, tile))
        tiles = []
        for t in range(16):
            even = weights[2 * t, 0:16, columns - tile :].astype(f32)
            odd = weights[2 * t + 1, 0:16, columns - tile :].astype(f32)
            tiles.append(jnp.where(lane < db, pltpu.roll(even, tile - db, 1), odd))
        table = jnp.concatenate(tiles, axis=1)
        small[...] = table.astype(bf16)
        lane = lanes((1, tile))
        per = tile // rb
        pieces = []
        for t in range(32 // per):
            piece = jnp.zeros((1, tile), f32)
            for i in range(per):
                row = weights[t * per + i, 0:16, columns - tile :].astype(f32)[2:3]
                piece = jnp.where(lane // rb == i, pltpu.roll(row, (i * rb + tile - db) % tile, 1), piece)
            pieces.append(piece)
        gain_latent = jnp.concatenate(pieces, axis=1)
        gain_row[...] = gain_latent
        low = (unit * table[0:1]).astype(bf16)
        hidden[...] = low
        raw = nn(low, weights[:, :, :query].reshape(width, query))
        q_nope[...] = raw[:, : HEADS * NOPE].astype(bf16)
        front = raw[:, HEADS * NOPE : HEADS * NOPE + tile]
        back = raw[:, HEADS * NOPE + tile :]
        turned_front = front * cos[...] - back * sin[...]
        turned_back = back * cos[...] + front * sin[...]
        lane = lanes((rows, tile))
        for h in range(HEADS):
            head = jnp.where(
                lane < half,
                pltpu.roll(turned_front, (tile - h * half) % tile, 1),
                jnp.where(lane < ROPE, pltpu.roll(turned_back, (tile - h * half + half) % tile, 1), 0.0),
            )
            q_rope[h * rows : (h + 1) * rows] = head.astype(bf16)
        late = nn(low, weights[:, :, query:].reshape(width, R + tile))
        latent_out[...] = late
        plain = late[:, :R]
        inverse = lax.rsqrt(jnp.mean(plain * plain, axis=-1, keepdims=True) + epsilon)
        key = jnp.concatenate(
            [plain * inverse * gain_latent, turn(late[:, R:], cos[...], sin[...])], axis=1
        ).astype(bf16)
        for n in range(8):
            keys[n] = key

    return call(
        kernel,
        [
            ((rows, width), bf16, "v"),
            ((rows, HEADS * NOPE), bf16, "v"),
            ((HEADS * rows, tile), bf16, "v"),
            ((8, rows, R + tile), bf16, "v"),
            ((rows, R + tile), f32, "v"),
            ((16, width), bf16, "v"),
            ((1, R), f32, "v"),
        ],
        [(info, "s"), (tokens, "v"), (cos4, "v"), (sin4, "v")] + [(part, "a") for part in parts],
        [pltpu.VMEM((16, 2, db, columns), bf16), pltpu.SemaphoreType.DMA(())],
        macs=rows * width * columns,
        after=after,
    )


def turn(values, cosine, sine_part):
    width = values.shape[1]
    half = ROPE // 2
    lane = lanes(values.shape)
    swapped = jnp.where(lane < half, -pltpu.roll(values, width - half, 1), pltpu.roll(values, half, 1))
    return jnp.where(lane < ROPE, values * cosine + swapped * sine_part, 0.0)


def put_quarters(values, targets, z):
    quarter = values.shape[0] // 4
    for n in range(4):
        for k in range(4):

            @pl.when(z ^ k == n)
            def _(n=n, k=k):
                targets[k][0] = values[n * quarter : (n + 1) * quarter]


def visible(info, shape, row_count):
    place = lax.broadcasted_iota(jnp.int32, shape, 0) + info[1] * row_count
    key = lax.broadcasted_iota(jnp.int32, shape, 1)
    end0 = info[4]
    end1 = info[4] + info[5]
    row_doc = (place >= end0).astype(jnp.int32) + (place >= end1).astype(jnp.int32)
    key_doc = (key >= end0).astype(jnp.int32) + (key >= end1).astype(jnp.int32)
    return (row_doc == key_doc) & (key <= place)


def attend(info, q_nope, q_rope, key_parts, pack, after):
    rows = q_nope.shape[0]
    db = pack.shape[1]
    width = 32 * db
    tile = q_rope.shape[1]
    out = HEADS * VD
    keys = 16 * rows
    quarter = rows // 4
    rb = R // 32

    def kernel(info, qn, qr, *refs):
        key_ins, refs = refs[:2], refs[2:]
        pack_in, refs = refs[0], refs[1:]
        probs, cat, mixture, head_out, result, key_rows, weights, expand, sem = refs
        start_all(pair_copies(key_ins, info[1] % 2, key_rows), sem.at[0])
        start_all([(pack_in, weights)], sem.at[1])
        wait_for(weights, sem.at[1])
        for h in range(HEADS):
            expand[h] = weights[:, h * rb : (h + 1) * rb, out:].reshape(R, NOPE + VD)
        for h in range(HEADS):
            own = slice(h * rows, (h + 1) * rows)
            cat[own, :R] = nt(qn[:, h * NOPE : (h + 1) * NOPE], expand[h, :, :NOPE]).astype(bf16)
            cat[own, R:] = qr[own]
        wait_for(key_rows, sem.at[0])
        flat = key_rows[...].reshape(keys, R + tile)
        seen = visible(info, (rows, keys), rows)
        scale = (NOPE + ROPE) ** (-0.5)
        for h in range(HEADS):
            own = slice(h * rows, (h + 1) * rows)
            scores = jnp.where(seen, scale * nt(cat[own], flat), -1e30)
            weight = jnp.exp(scores - jnp.max(scores, axis=-1, keepdims=True))
            prob = (weight / jnp.sum(weight, axis=-1, keepdims=True)).astype(bf16)
            probs[own] = prob
            mixed = nn(prob, flat[:, :R]).astype(bf16)
            mixture[own] = mixed
            head_out[:, h * VD : (h + 1) * VD] = nn(mixed, expand[h, :, NOPE:]).astype(bf16)
        summed = nt(head_out[...], weights[:, :, :out].reshape(width, out)).astype(bf16)
        result[...] = summed.reshape(4, quarter, width)

    return call(
        kernel,
        [
            ((HEADS * rows, keys), bf16, "v"),
            ((HEADS * rows, R + tile), bf16, "v"),
            ((HEADS * rows, R), bf16, "v"),
            ((rows, out), bf16, "v"),
        ]
        + [((4, quarter, width), bf16, "v")],
        [(info, "s"), (q_nope, "v"), (q_rope, "v")]
        + [(part, "a") for part in key_parts + [pack]],
        [
            pltpu.VMEM((8, 2, rows, R + tile), bf16),
            pltpu.VMEM((32, db, out + NOPE + VD), bf16),
            pltpu.VMEM((HEADS, R, NOPE + VD), bf16),
            pltpu.SemaphoreType.DMA((2,)),
        ],
        macs=HEADS * rows * keys * (2 * R + tile) * 2,
        after=after,
    )


def quarter_norm(info, parts, tokens, small, after):
    _, quarter, width = parts.shape

    def kernel(info, came, tok, table, attention, normed):
        summed = came[0].astype(f32) + came[1].astype(f32) + came[2].astype(f32) + came[3].astype(f32)
        low = summed.astype(bf16)
        attention[0] = low
        middle = tok[info[3]].astype(f32) + low.astype(f32)
        inverse = lax.rsqrt(jnp.mean(middle * middle, axis=-1, keepdims=True) + epsilon)
        rows = (middle * inverse * table[1:2].astype(f32)).astype(bf16)
        for n in range(16):
            normed[n] = rows

    return call(
        kernel,
        [((1, quarter, width), bf16, "v"), ((16, quarter, width), bf16, "v")],
        [(info, "s"), (parts, "v"), (tokens.reshape(4, quarter, width), "v"), (small, "v")],
        [],
        after=after,
    )


def expert_copies(parts, me, targets):
    copies = []
    for ky, part in enumerate(parts):
        for i in range(8):
            for n, target in enumerate(targets):
                copies.append((part.at[i, n], target.at[me ^ mask(ky, i // 2, i % 2)]))
    return copies


def expert_rows(info, normed_parts, cots, weights, ff):
    _, quarter, width = normed_parts[0].shape
    extra = cots.shape[-1] - width
    db, wide = weights[0].shape[-2:]
    count = 32 * quarter
    step = count // 4
    lane0 = FF_PAD - extra

    def kernel(info, *refs):
        nref, refs = refs[:2], refs[2:]
        cref, wref, refs = refs[0], refs[1:5], refs[5:]
        act_out, gate_out, up_out, keep, send, x, g, wg, wu, wd, result, sem = refs
        start_all(expert_copies(wref, info[0], (wg, wu, wd)), sem.at[0])
        start_all([(cref.at[:, info[1] % 2], g.at[0]), (cref.at[:, 1 - info[1] % 2], g.at[1])], sem.at[1])
        start_all([(nref[0], x.at[0]), (nref[1], x.at[1])], sem.at[2])
        for ref in (wg, wu, wd):
            wait_for(ref, sem.at[0])
        wait_for(g, sem.at[1])
        wait_for(x, sem.at[2])
        tile_lane = lanes((step, extra))
        lane = lanes((step, wide))
        half = step // quarter

        def body(i, carry):
            own = pl.ds(pl.multiple_of(i * step, step), step)
            core, at = i // 2, (i % 2) * half
            rows = x[core, pl.ds(at, half)].reshape(step, width)
            cot = g[core, pl.ds(at // 4, half // 4)].reshape(step, width + extra)
            gate_weight = wg[...].reshape(width, wide)
            up_weight = wu[...].reshape(width, wide)
            down_weight = wd[...].reshape(width, wide)
            gate_pre = nn(rows, gate_weight)
            up_pre = nn(rows, up_weight)
            back = nn(cot[:, :width], down_weight)
            router = jax.nn.sigmoid(gate_pre[:, lane0:FF_PAD])
            weighted = router * cot[:, width:].astype(f32)
            gates = route_scale * weighted / jnp.sum(weighted, axis=1, keepdims=True)
            gate = jnp.sum(jnp.where(tile_lane == ff - lane0 + info[2], gates, 0.0), axis=1, keepdims=True)
            gate_row = jnp.where(lane < FF_PAD, gate, 1.0)
            sig = jax.nn.sigmoid(gate_pre)
            silu = gate_pre * sig
            act = silu * up_pre
            own_grad = jnp.sum(jnp.where(lane < FF_PAD, act * back, 0.0), axis=1, keepdims=True)
            act_low = (gate_row * act).astype(bf16)
            grad_act = gate_row * back
            grad_gate = (grad_act * up_pre * (sig * (1.0 + gate_pre * (1.0 - sig)))).astype(bf16)
            grad_up = (grad_act * silu).astype(bf16)
            act_out[own] = act_low
            gate_out[own] = grad_gate
            up_out[own] = grad_up
            result[own, :width] = nt(act_low, down_weight).astype(bf16)
            result[own, width : 2 * width] = (nt(grad_gate, gate_weight) + nt(grad_up, up_weight)).astype(bf16)
            high = own_grad.astype(bf16).astype(f32)
            result[own, 2 * width :] = (
                jnp.where(tile_lane == 8 + info[2], high, 0.0)
                + jnp.where(tile_lane == 24 + info[2], own_grad - high, 0.0)
            ).astype(bf16)
            return carry

        lax.fori_loop(0, 4, body, 0)
        for core, target in enumerate((keep, send)):
            pltpu.make_async_copy(result.at[pl.ds(core * count // 2, count // 2)], target, sem.at[3 + core]).start()
        for core, target in enumerate((keep, send)):
            wait_for(target, sem.at[3 + core])

    return call(
        kernel,
        [((count, wide), bf16, "v")] * 3
        + [((count // 2, 2 * width + extra), bf16, "a")] * 2,
        [(info, "s")] + [(part, "a") for part in normed_parts + [cots] + weights],
        [
            pltpu.VMEM((2, 16, quarter, width), bf16),
            pltpu.VMEM((2, 4, 4, quarter, width + extra), bf16),
            pltpu.VMEM((32, db, wide), bf16),
            pltpu.VMEM((32, db, wide), bf16),
            pltpu.VMEM((32, db, wide), bf16),
            pltpu.VMEM((count, 2 * width + extra), bf16),
            pltpu.SemaphoreType.DMA((5,)),
        ],
        macs=6 * count * width * wide,
    )


def expert_weights(info, normed_parts, cots, act, grad_gate, grad_up, after):
    _, quarter, width = normed_parts[0].shape
    extra = cots.shape[-1] - width
    count, wide = act.shape
    db = width // 32
    step = width // 8
    blocks = step // db

    def kernel(info, *refs):
        nref, refs = refs[:2], refs[2:]
        cref, refs = refs[0], refs[1:]
        a, gg, gu, *results, x, g, grads, sem = refs
        start_all([(cref.at[:, info[1] % 2], g.at[0]), (cref.at[:, 1 - info[1] % 2], g.at[1])], sem.at[0])
        start_all([(nref[0], x.at[0]), (nref[1], x.at[1])], sem.at[1])
        wait_for(g, sem.at[0])
        wait_for(x, sem.at[1])

        def body(i, carry):
            cols = pl.ds(pl.multiple_of(i * step, step), step)
            rows = x[:, :, :, cols].reshape(count, step)
            cot = g[:, :, :, :, cols].reshape(count, step)
            own = pl.ds(i * blocks, blocks)
            grads[own, 0] = tn(rows, gg[...]).astype(bf16).reshape(blocks, db, wide)
            grads[own, 1] = tn(rows, gu[...]).astype(bf16).reshape(blocks, db, wide)
            grads[own, 2] = tn(cot, a[...]).astype(bf16).reshape(blocks, db, wide)
            return carry

        lax.fori_loop(0, 8, body, 0)
        for ky in range(4):
            for kx in range(4):
                for kc in (0, 1):
                    pltpu.make_async_copy(
                        grads.at[info[0] ^ mask(ky, kx, kc)], results[ky].at[kx, kc], sem.at[2]
                    ).start()
        for result in results:
            wait_for(result, sem.at[2])

    return call(
        kernel,
        [((4, 2, 3, db, wide), bf16, "a")] * 4,
        [(info, "s")]
        + [(part, "a") for part in normed_parts + [cots]]
        + [(act, "v"), (grad_gate, "v"), (grad_up, "v")],
        [
            pltpu.VMEM((2, 16, quarter, width), bf16),
            pltpu.VMEM((2, 4, 4, quarter, width + extra), bf16),
            pltpu.VMEM((32, 3, db, wide), bf16),
            pltpu.SemaphoreType.DMA((3,)),
        ],
        macs=3 * count * width * wide,
        after=after,
    )


def quarter_copies(parts, z, target, columns=None):
    if columns is None:
        return [(part.at[0], target.at[z ^ k]) for k, part in enumerate(parts)]
    return [(part.at[0, :, columns], target.at[z ^ k]) for k, part in enumerate(parts)]


def attend_back(
    info, tokens, cotangent, picked, att_parts, grad_parts, small, head_out, mixture, probs, cat, q_nope, hidden,
    key_parts, pack2, parts1, cos4, sin4, after,
):
    rows, width = tokens.shape
    quarter = rows // 4
    db = width // 32
    rb = R // 32
    tile = cat.shape[1] - R
    out = HEADS * VD
    keys = 16 * rows
    query = HEADS * (NOPE + ROPE)
    half = ROPE // 2
    extra = grad_parts[0].shape[-1] - 2 * width
    scale = (NOPE + ROPE) ** (-0.5)
    late = out + NOPE + VD

    def kernel(info, tok, cotan, pick, table, ho, mix, pr, ca, qn, hid, cos, sin, *refs):
        att_in, refs = refs[:4], refs[4:]
        grad_in, refs = refs[:4], refs[4:]
        key_in, refs = refs[:2], refs[2:]
        in2, refs = refs[0], refs[1:]
        in1, refs = refs[: len(parts1)], refs[len(parts1) :]
        (
            grad_middle, small_grads, key_keep, key_send, hid0, hid1, hid2, hid3, keep, send,
            att, arrived, key_rows, w2, w1, expand, grad_mix, grad_scores, key_grads, weight_grads, grad_q, sem,
        ) = refs
        start_all(quarter_copies(grad_in, info[3], arrived, pl.ds(width, width + extra)), sem.at[0])
        start_all(quarter_copies(att_in, info[3], att), sem.at[1])
        start_all([(in2, w2)], sem.at[2])
        start_all(pair_copies(key_in, info[1] % 2, key_rows), sem.at[3])
        columns = pl.ds(0, query)
        start_all(pair_copies([one.at[:, :, columns] for one in in1], info[1] % 2, w1), sem.at[4])
        wait_for(arrived, sem.at[0])
        wait_for(att, sem.at[1])
        middle = tok[...].astype(f32) + att[...].reshape(rows, width).astype(f32)
        inverse = lax.rsqrt(jnp.mean(middle * middle, axis=-1, keepdims=True) + epsilon)
        unit = middle * inverse
        gain = table[1:2].astype(f32)
        normed = (unit * gain).astype(bf16)
        came = arrived[...].reshape(rows, width + extra)
        sig = jax.nn.sigmoid(nt(normed, table[...]))
        chosen = pick[...]
        weighted = sig * chosen
        gate_total = jnp.sum(weighted, axis=1, keepdims=True)
        gates = route_scale * weighted / gate_total
        grad_gates = came[:, width : width + 16].astype(f32) + came[:, width + 16 : width + 32].astype(f32)
        grad_weighted = (route_scale * grad_gates - jnp.sum(grad_gates * gates, axis=1, keepdims=True)) / gate_total
        grad_logits = grad_weighted * chosen * sig * (1.0 - sig)
        high, low = high_low(grad_logits)
        grads = tn(high, normed) + tn(low, normed)
        grad_normed = came[:, :width].astype(f32) + nn(high, table[...]) + nn(low, table[...])
        scaled = grad_normed * gain
        grad_mid = cotan[...].astype(f32) + inverse * (
            scaled - unit * jnp.mean(scaled * unit, axis=-1, keepdims=True)
        )
        d_gain = jnp.sum(grad_normed * unit, axis=0, keepdims=True)
        row16 = lax.broadcasted_iota(jnp.int32, (16, width), 0)
        small_grads[...] = jnp.where(row16 >= 8, grads, jnp.where(row16 == 1, d_gain, 0.0))
        grad_middle[...] = grad_mid
        grad_att = grad_mid.astype(bf16)
        wait_for(w2, sem.at[2])
        for h in range(HEADS):
            expand[h] = w2[:, h * rb : (h + 1) * rb, out:].reshape(R, NOPE + VD)
        grad_heads = nn(grad_att, w2[:, :, :out].reshape(width, out)).astype(bf16)
        weight_grads[:, :, :, :out] = tn(grad_att, ho[...]).astype(bf16).reshape(16, 2, db, out)
        for h in range(HEADS):
            own = slice(h * rows, (h + 1) * rows)
            mine = grad_heads[:, h * VD : (h + 1) * VD]
            weight_grads[:, :, h * rb : (h + 1) * rb, out + NOPE : late] = (
                tn(mix[own], mine).astype(bf16).reshape(16, 2, rb, VD)
            )
            grad_mix[own] = nt(mine, expand[h, :, NOPE:]).astype(bf16)
        wait_for(key_rows, sem.at[3])
        flat = key_rows[...].reshape(keys, R + tile)
        lane = lanes((rows, tile))
        front = jnp.zeros((rows, tile), f32)
        back = jnp.zeros((rows, tile), f32)
        for h in range(HEADS):
            own = slice(h * rows, (h + 1) * rows)
            grad_prob = nt(grad_mix[own], flat[:, :R])
            prob = pr[own].astype(f32)
            inner = jnp.sum(prob * grad_prob, axis=-1, keepdims=True)
            grad_score = (prob * (grad_prob - inner)).astype(bf16)
            grad_scores[own] = grad_score
            grad_cat = scale * nn(grad_score, flat)
            grad_abs = grad_cat[:, :R].astype(bf16)
            weight_grads[:, :, h * rb : (h + 1) * rb, out : out + NOPE] = (
                tn(grad_abs, qn[:, h * NOPE : (h + 1) * NOPE]).astype(bf16).reshape(16, 2, rb, NOPE)
            )
            grad_q[:, h * NOPE : (h + 1) * NOPE] = nn(grad_abs, expand[h, :, :NOPE]).astype(bf16)
            turned = grad_cat[:, R:]
            inside = (lane >= h * half) & (lane < (h + 1) * half)
            front = jnp.where(inside, pltpu.roll(turned, (h * half) % tile, 1), front)
            back = jnp.where(inside, pltpu.roll(turned, (h * half + tile - half) % tile, 1), back)
        grad_q[:, HEADS * NOPE : HEADS * NOPE + tile] = (front * cos[...] + back * sin[...]).astype(bf16)
        grad_q[:, HEADS * NOPE + tile :] = (back * cos[...] - front * sin[...]).astype(bf16)
        chunk = keys // 4
        for n in range(4):
            cols = slice(n * chunk, (n + 1) * chunk)
            part = scale * tn(grad_scores[:, cols], ca[...])
            latent = part[:, :R] + tn(pr[:, cols], grad_mix[...])
            own = slice(n * 2, (n + 1) * 2)
            key_grads[own, :, :, :R] = latent.astype(bf16).reshape(2, 2, rows, R)
            key_grads[own, :, :, R:] = part[:, R:].astype(bf16).reshape(2, 2, rows, tile)
        core = info[1] % 2
        pltpu.make_async_copy(key_grads.at[:, core], key_keep, sem.at[5]).start()
        pltpu.make_async_copy(key_grads.at[:, 1 - core], key_send, sem.at[6]).start()
        wait_for(w1, sem.at[4])
        wq = w1[...].reshape(width, query)
        summed = nt(grad_q[...], wq).astype(bf16)
        put_quarters(summed, (hid0, hid1, hid2, hid3), info[3])
        weight_grads[:, :, :, late:] = tn(hid[...], grad_q[...]).astype(bf16).reshape(16, 2, db, query)
        pltpu.make_async_copy(weight_grads.at[:, core], keep, sem.at[7]).start()
        pltpu.make_async_copy(weight_grads.at[:, 1 - core], send, sem.at[8]).start()
        for n, ref in enumerate((key_keep, key_send, keep, send)):
            wait_for(ref, sem.at[5 + n])

    vmem_ins = [tokens, cotangent, picked, small, head_out, mixture, probs, cat, q_nope, hidden, cos4, sin4]
    return call(
        kernel,
        [
            ((rows, width), f32, "v"),
            ((16, width), f32, "v"),
            ((8, rows, R + tile), bf16, "a"),
            ((8, rows, R + tile), bf16, "a"),
            ((1, quarter, width), bf16, "v"),
            ((1, quarter, width), bf16, "v"),
            ((1, quarter, width), bf16, "v"),
            ((1, quarter, width), bf16, "v"),
            ((16, db, late + query), bf16, "a"),
            ((16, db, late + query), bf16, "a"),
        ],
        [(info, "s")]
        + [(array, "v") for array in vmem_ins]
        + [(part, "a") for part in att_parts + grad_parts + key_parts + [pack2] + parts1],
        [
            pltpu.VMEM((4, quarter, width), bf16),
            pltpu.VMEM((4, quarter, width + extra), bf16),
            pltpu.VMEM((8, 2, rows, R + tile), bf16),
            pltpu.VMEM((32, db, late), bf16),
            pltpu.VMEM((16, 2, db, query), bf16),
            pltpu.VMEM((HEADS, R, NOPE + VD), bf16),
            pltpu.VMEM((HEADS * rows, R), bf16),
            pltpu.VMEM((HEADS * rows, keys), bf16),
            pltpu.VMEM((8, 2, rows, R + tile), bf16),
            pltpu.VMEM((16, 2, db, late + query), bf16),
            pltpu.VMEM((rows, query), bf16),
            pltpu.SemaphoreType.DMA((9,)),
        ],
        macs=HEADS * rows * keys * (4 * R + 2 * tile) * 2,
        after=after,
    )


def finish(
    info, tokens, grad_middle, hidden, latent, gain_latent, small, small_grads, key_parts, hidden_parts, att_parts,
    sum_parts, parts1, cos4, sin4, after,
):
    rows, width = tokens.shape
    quarter = rows // 4
    db = width // 32
    rb = R // 32
    tile = latent.shape[1] - R
    query = HEADS * (NOPE + ROPE)

    def kernel(info, tok, gm, hid, lat, gl, table, sg, cos, sin, *refs):
        key_in, refs = refs[:4], refs[4:]
        hid_in, refs = refs[:4], refs[4:]
        att_in, refs = refs[:4], refs[4:]
        sum_in, refs = refs[:4], refs[4:]
        in1, refs = refs[: len(parts1)], refs[len(parts1) :]
        output, d_tokens, keep, send, own_keys, part, att, sums, w1, grads, sem = refs
        start_all(quarter_copies(key_in, info[3], own_keys), sem.at[6])
        start_all(pair_copies(in1, info[1] % 2, w1, pl.ds(query, R + tile)), sem.at[0])
        start_all(quarter_copies(hid_in, info[3], part), sem.at[1])
        start_all(quarter_copies(att_in, info[3], att), sem.at[2])
        start_all(quarter_copies(sum_in, info[3], sums, pl.ds(0, width)), sem.at[3])
        wait_for(own_keys, sem.at[6])
        own = own_keys[...].reshape(rows, R + tile)
        plain = lat[:, :R]
        inverse = lax.rsqrt(jnp.mean(plain * plain, axis=-1, keepdims=True) + epsilon)
        unit = plain * inverse
        grad_y = own[:, :R]
        scaled = grad_y * gl[...]
        d_gain_latent = jnp.sum(grad_y * unit, axis=0, keepdims=True)
        grad_in = inverse * (scaled - unit * jnp.mean(scaled * unit, axis=-1, keepdims=True))
        grad_latent = jnp.concatenate([grad_in, turn(own[:, R:], cos[...], -sin[...])], axis=1).astype(bf16)
        d_latent = tn(hid[...], grad_latent).astype(bf16)
        grads[...] = d_latent.reshape(16, 2, db, R + tile)
        wait_for(w1, sem.at[0])
        wait_for(part, sem.at[1])
        x = tok[...].astype(f32)
        inverse = lax.rsqrt(jnp.mean(x * x, axis=-1, keepdims=True) + epsilon)
        unit = x * inverse
        grad_hidden = part[...].reshape(rows, width).astype(f32) + nt(
            grad_latent, w1[...].reshape(width, R + tile)
        )
        scaled = grad_hidden * table[0:1].astype(f32)
        d_tokens[...] = gm[...] + inverse * (scaled - unit * jnp.mean(scaled * unit, axis=-1, keepdims=True))
        d_gain = jnp.sum(grad_hidden * unit, axis=0, keepdims=True)
        row16 = lax.broadcasted_iota(jnp.int32, (16, width), 0)
        every = jnp.where(row16 == 0, d_gain, sg[...])
        lane = lanes((16, tile))
        row = lax.broadcasted_iota(jnp.int32, (16, tile), 0)
        per = tile // rb
        for j in range(32):
            t = j // 2
            values = every[:, t * tile : (t + 1) * tile]
            if j % 2 == 0:
                values = pltpu.roll(values, db, 1)
            gains = d_gain_latent[:, (j // per) * tile : (j // per + 1) * tile]
            gains = pltpu.roll(gains, (db + tile - (j % per) * rb) % tile, 1)
            values = jnp.where(row == 2, jnp.where(lane < db + rb, gains, 0.0), values)
            before = grads[j // 2, j % 2, 0:16, R:].astype(f32)
            grads[j // 2, j % 2, 0:16, R:] = jnp.where(lane < db, before, values).astype(bf16)
        core = info[1] % 2
        pltpu.make_async_copy(grads.at[:, core], keep, sem.at[4]).start()
        pltpu.make_async_copy(grads.at[:, 1 - core], send, sem.at[5]).start()
        wait_for(att, sem.at[2])
        wait_for(sums, sem.at[3])
        middle = x + att[...].reshape(rows, width).astype(f32)
        output[...] = (middle + sums[...].reshape(rows, width).astype(f32)).astype(bf16)
        wait_for(keep, sem.at[4])
        wait_for(send, sem.at[5])

    vmem_ins = [tokens, grad_middle, hidden, latent, gain_latent, small, small_grads, cos4, sin4]
    return call(
        kernel,
        [
            ((rows, width), bf16, "v"),
            ((rows, width), f32, "v"),
            ((16, db, R + tile), bf16, "a"),
            ((16, db, R + tile), bf16, "a"),
        ],
        [(info, "s")]
        + [(array, "v") for array in vmem_ins]
        + [(part, "a") for part in key_parts + hidden_parts + att_parts + sum_parts + parts1],
        [
            pltpu.VMEM((4, quarter, R + tile), f32),
            pltpu.VMEM((4, quarter, width), bf16),
            pltpu.VMEM((4, quarter, width), bf16),
            pltpu.VMEM((4, quarter, width), bf16),
            pltpu.VMEM((16, 2, db, R + tile), bf16),
            pltpu.VMEM((16, 2, db, R + tile), bf16),
            pltpu.SemaphoreType.DMA((7,)),
        ],
        macs=4 * rows * width * (R + tile),
        after=after,
    )


def unpack_experts(info, own, other, ff, sh):
    _, _, db, wide = other.shape

    def kernel(info, a0, a1, a2, a3, b, gate, up, down, sg, su, sd, slots, sem):
        for kx, a in enumerate((a0, a1, a2, a3)):
            pltpu.make_async_copy(a.at[0], slots.at[info[2] ^ (kx * 2)], sem).start()
            pltpu.make_async_copy(b.at[kx], slots.at[info[2] ^ (kx * 2 + 1)], sem).start()
        wait_for(slots, sem)
        for n, (routed, shared) in enumerate(((gate, sg), (up, su), (down, sd))):
            for e in range(8):
                routed[e] = slots[e, n, :, :ff].astype(f32)
            shared[...] = jnp.concatenate(
                [slots[e, n, :, FF_PAD : FF_PAD + sh].astype(f32) for e in range(8)], axis=1
            )

    return call(
        kernel,
        [((8, db, ff), f32, "v")] * 3 + [((db, 8 * sh), f32, "v")] * 3,
        [(info, "s")] + [(part, "a") for part in own] + [(other, "a")],
        [pltpu.VMEM((8, 3, db, wide), bf16), pltpu.SemaphoreType.DMA(())],
    )


def unpack_attention(grads):
    db, _ = grads.shape
    rb = R // 32
    out = HEADS * VD
    late = out + NOPE + VD
    per_head, half = NOPE + ROPE, ROPE // 2

    def kernel(g, d_out, d_expand, d_query):
        d_out[...] = g[:, :out].astype(f32)
        for h in range(HEADS):
            d_expand[:, h * (NOPE + VD) : (h + 1) * (NOPE + VD)] = g[h * rb : (h + 1) * rb, out:late].astype(f32)
            plain = g[:, late + h * NOPE : late + (h + 1) * NOPE].astype(f32)
            front = late + HEADS * NOPE + h * half
            back = front + HEADS * half
            d_query[:, h * per_head : (h + 1) * per_head] = jnp.concatenate(
                [plain, g[:, front : front + half].astype(f32), g[:, back : back + half].astype(f32)], axis=1
            )

    return call(
        kernel,
        [
            ((db, out), f32, "v"),
            ((rb, HEADS * (NOPE + VD)), f32, "v"),
            ((db, HEADS * per_head), f32, "v"),
        ],
        [(grads, "v")],
        [],
    )


def shards(
    tokens,
    lengths,
    routes,
    cotangent,
    attn_gain,
    w_query,
    w_latent,
    latent_gain,
    w_expand,
    w_out,
    moe_gain,
    w_router,
    w_gate,
    w_up,
    w_down,
    shared_gate,
    shared_up,
    shared_down,
):
    me = lax.axis_index(PLANE)
    place = me % 16
    member = me % 8
    z = lax.axis_index("z")
    rows, width = tokens.shape
    quarter = rows // 4
    db = width // 32
    rb = R // 32
    ff, sh = w_gate.shape[2], shared_gate.shape[1] // 8
    tile = ROPE + db
    query = HEADS * (NOPE + ROPE)
    half = ROPE // 2
    extra = min(128, FF_PAD)
    wide = FF_PAD + SH_PAD
    info = jnp.concatenate([jnp.stack([me, place, member, z]).astype(jnp.int32), lengths[0]])

    one, two = pack_attention(
        w_query, w_latent, attn_gain, moe_gain, latent_gain, w_router.T, w_out.T, w_expand
    )
    pack2 = lax.all_gather(two, PLANE, axis=0)
    keep, send = pack_experts(
        info, w_gate, w_up, jnp.swapaxes(w_down, 1, 2), shared_gate, shared_up, shared_down.T, w_router
    )
    came = swap(send, kc=1)
    by_x = [jnp.stack([keep[k], came[k]]) for k in range(4)]
    parts1 = gather(one, ("yl", "yh", "x"), by_x)
    by_x = [by_x[0]] + [swap(hold(by_x[k], parts1[0]), kx=k) for k in (1, 2, 3)]
    mine = jnp.concatenate(by_x)
    weights = [mine] + [swap(mine, ky=k) for k in (1, 2, 3)]

    position = place * rows + jnp.arange(rows, dtype=jnp.int32)
    ends = jnp.stack([lengths[0, 0], lengths[0, 0] + lengths[0, 1]])
    start = jnp.where(position >= ends[1], ends[1], jnp.where(position >= ends[0], ends[0], 0))
    frequency = rope_base ** (-jnp.arange(half, dtype=f32) / half)
    angles = (position - start).astype(f32)[:, None] * jnp.tile(frequency, 2 * HEADS * half // ROPE)[None, :]
    cos4, sin4 = jnp.cos(angles), jnp.sin(angles)
    picked = jnp.sum(
        (routes[:, :, None] == jnp.arange(16, dtype=jnp.int32)[None, None, :] - 8).astype(f32), axis=1
    )
    lane_pick = jnp.sum(
        (routes[:, :, None] == jnp.arange(extra, dtype=jnp.int32)[None, None, :] - (ff - FF_PAD + extra)), axis=1
    ).astype(bf16)

    hidden, q_nope, q_rope, keys, latent, small, gain_latent = project(info, tokens, cos4, sin4, parts1, ())
    key_parts = gather(keys, ("yh", "x"), (mine,))
    cots = tie(jnp.concatenate([cotangent, lane_pick], axis=1), key_parts[0])
    cots = lax.all_gather(cots, ("x", "c"), axis=0).reshape(4, 2, 4, quarter, width + extra)
    probs, cat, mixture, head_out, attention = attend(info, q_nope, q_rope, key_parts, pack2, ())
    attention = hold(exchange(attention, "z"), weights[1], weights[3])
    own_attention, normed = quarter_norm(info, attention, tokens, small, ())
    normed_parts = gather(normed, ("x", "z"), (weights[2],))
    att_parts = [own_attention] + [swap_z(own_attention, k) for k in (1, 2, 3)]

    act, grad_gate, grad_up, keep, send = expert_rows(
        info, normed_parts, cots, weights, ff
    )
    def collect(values):
        return jnp.sum(values.astype(f32), axis=0, keepdims=True).astype(bf16)

    both = total([keep, swap(send, kc=1)])
    d_experts = expert_weights(info, normed_parts, cots, act, grad_gate, grad_up, (both,))
    both = collect(hold(exchange(both.reshape(16, quarter, -1), ("x", "z")), d_experts[0]))
    d_from_y = [swap(d_experts[k], ky=k) for k in (1, 2, 3)]
    sum_parts = [both] + [swap_z(both, k) for k in (1, 2, 3)]

    grad_middle, small_grads, key_keep, key_send, *hidden_part, keep, send = attend_back(
        info, tokens, cotangent, picked, att_parts, sum_parts, small, head_out, mixture, probs, cat, q_nope,
        hidden, key_parts, pack2, parts1, cos4, sin4, (d_from_y[0], d_from_y[2]),
    )
    key_send = hold(key_send, d_from_y[1])
    grad_keys = total([key_keep, swap(key_send, kc=1)]).reshape(32, quarter, R + tile)
    send = hold(send, grad_keys)
    most = total([keep, swap(send, kc=1)])
    most = lax.psum_scatter(most, ("yl", "yh", "x"), scatter_dimension=0)
    grad_keys = exchange(grad_keys, ("yh", "x", "z"))
    grad_hidden = total([hidden_part[0]] + [swap_z(hidden_part[k], k) for k in (1, 2, 3)])
    hidden_parts = [grad_hidden] + [swap_z(grad_hidden, k) for k in (1, 2, 3)]
    grad_keys = jnp.sum(grad_keys.astype(f32), axis=0, keepdims=True)
    grad_key_parts = [grad_keys] + [swap_z(grad_keys, k) for k in (1, 2, 3)]
    d_mine = [total([part[k] for part in [d_experts[0]] + d_from_y]) for k in range(4)]
    d_mine = [d_mine[0]] + [swap(hold(d_mine[k], grad_keys), kx=k) for k in (1, 2, 3)]

    output, d_tokens, keep, send = finish(
        info, tokens, grad_middle, hidden, latent, gain_latent, small, small_grads, grad_key_parts, hidden_parts,
        att_parts, sum_parts, parts1, cos4, sin4, (),
    )
    rest = total([keep, swap(send, kc=1)])
    rest = lax.all_to_all(rest, ("yl", "yh", "x"), 0, 0, tiled=True)
    d_other = swap(jnp.stack([part[1] for part in d_mine]), kc=1)
    d_routed = unpack_experts(info, d_mine, d_other, ff, sh)
    d_out, d_expand, d_query = unpack_attention(most)
    rest = jnp.sum(rest.astype(f32), axis=0)

    aux = rest[:16, R + ROPE :]
    return (
        output,
        d_tokens,
        aux[0],
        d_query,
        rest[:, : R + ROPE],
        aux[2, :rb],
        d_expand,
        d_out.T,
        aux[1],
        aux[8:16].T,
        d_routed[0],
        d_routed[1],
        jnp.swapaxes(d_routed[2], 1, 2),
        d_routed[3],
        d_routed[4],
        d_routed[5].T,
    )


def solution(mesh):
    rows = P(PLANE, None)
    split = P(PLANE, "z")
    vector = P(PLANE)
    turned = P("z", PLANE)
    expert_rows = P(None, PLANE, "z")
    expert_columns = P(None, "z", PLANE)
    fine = Mesh(mesh.devices.reshape(2, 2, 4, 2, 4), ("yl", "yh", "x", "c", "z"))
    return jax.shard_map(
        shards,
        mesh=fine,
        in_specs=(
            rows,
            P("yl", None),
            rows,
            rows,
            vector,
            split,
            rows,
            vector,
            split,
            turned,
            vector,
            rows,
            expert_rows,
            expert_rows,
            expert_columns,
            split,
            split,
            turned,
        ),
        out_specs=(
            rows,
            rows,
            vector,
            split,
            rows,
            vector,
            split,
            turned,
            vector,
            rows,
            expert_rows,
            expert_rows,
            expert_columns,
            split,
            split,
            turned,
        ),
        check_vma=False,
    )
```

time: 1980 us -> 523 us (0.26)
  Pallas kernels: 1190 us -> 105 us
  local copies, waits for them, and re-layouts: 259 us -> 21.4 us
  matrix products: 82.8 us -> 0 us
  starting transfers between devices: 142 us -> 99.4 us
  other arithmetic: 60.5 us -> 24.1 us
    pallas_call x9 -> x24, Pallas kernels: 1190 us -> 105 us  [the longest x11 105 us: call(): pl.pallas_call(body, out_shape=[jax.ShapeDtypeStruct(shape, dtype) for sh...]
    dynamic_update_slice x16 -> x0, local copies, waits for them, and re-layouts: 92.2 us -> none  [gather_z(): out = lax.dynamic_update_slice_in_dim(out, piece, (z ^ k) * rows, 0)]
    all_to_all x0 -> x7, waiting for transfers between devices: none -> 85.9 us  [the longest x6 72.3 us: exchange(): return lax.all_to_all(blocks, axes, 0, 0, tiled=True)]
    dot_general x33 -> x0, matrix products: 75.8 us -> none  [the longest x8 14.9 us: dot(): return jnp.dot(left, right, preferred_element_type=f32)]
    ppermute x80 -> x21, starting transfers between devices: 95 us -> 22.8 us  [swap(): return lax.ppermute(values, PLANE, [(i, i ^ bits) for i in range(32)])]
    ppermute x27 -> x15, waiting for transfers between devices: 83.7 us -> 29.5 us  [swap_z(): return lax.ppermute(values, 'z', [(i, i ^ k) for i in range(4)])]
    all_to_all x0 -> x7, starting transfers between devices: none -> 52.7 us  [the longest x6 45.8 us: exchange(): return lax.all_to_all(blocks, axes, 0, 0, tiled=True)]
    slice x10 -> x6, local copies, waits for them, and re-layouts: 27.2 us -> 1.93 us  [the longest x1 1.29 us: tie(): lax.slice(one, (0,) * one.ndim, (1,) * one.ndim).reshape(()).astype(f32)]
  transfers between devices with their start and end apart: 107 -> 46, of which waited for: 45 -> 28; matrix products, arithmetic and copies ran while one was open for 17% -> 5% of each run, Pallas kernels for 60% -> 15%
where the time goes in v2:
time: 523 us; the launch traced here: 513 us
  waiting for transfers between devices  247 us (47%)
  Pallas kernels  105 us (20%)
  starting transfers between devices  99.4 us (19%)
  other arithmetic  24.1 us (5%)
  local copies, waits for them, and re-layouts  21.4 us (4%)
  between operations  16.8 us (3%)
    ppermute x21, waiting for transfers between devices, swap(): return lax.ppermute(values, PLANE, [(i, i ^ bits) for i in range(32)])  131 us
    pallas_call x11, Pallas kernels, call(): pl.pallas_call(body, out_shape=[jax.ShapeDtypeStruct(shape, dtype) for sh...  105 us
    all_to_all x6, waiting for transfers between devices, exchange(): return lax.all_to_all(blocks, axes, 0, 0, tiled=True)  72.3 us
    all_to_all x6, starting transfers between devices, exchange(): return lax.all_to_all(blocks, axes, 0, 0, tiled=True)  45.8 us
    ppermute x15, waiting for transfers between devices, swap_z(): return lax.ppermute(values, 'z', [(i, i ^ k) for i in range(4)])  29.5 us
    ppermute x15, starting transfers between devices, swap_z(): return lax.ppermute(values, 'z', [(i, i ^ k) for i in range(4)])  23.8 us
    ppermute x21, starting transfers between devices, swap(): return lax.ppermute(values, PLANE, [(i, i ^ bits) for i in range(32)])  22.8 us
    unnamed x93, local copies, waits for them, and re-layouts  16.2 us
  transfers between devices with their start and end apart: 46, of which 28 were waited for; matrix products, arithmetic and copies ran while one was open for 5% of the time, Pallas kernels for 15%

profile of v2, /device:TPU:0, one launch (start us, length us, event | category | flops | bytes accessed | tf_op | source)
XLA Modules:
  0.0 513.1 jit_solution(16301665859524609126)
XLA Ops:
  7.2 2.8 shard_map.297
  10.0 7.3 %all-to-all-start = ((bf16[16,64,1408]{2,1,0:T(8,128)(2,1)}), bf16[16,64,1408]{2,1,0:T(8,128)(2,1)S(1)}, u32[]{:S(2)}, u32[]{:S(2)}) async-start(bf16[16,64,1408]{2,1,0:T(8,128)(2,1)} %get-tuple-element.66), calls=%async_computation | async-start | bytes 5767168 | tf_op jit(solution)/shard_map/all_to_all | solution.py:104
  19.4 2.7 shard_map.298
  22.2 2.0 constant_dynamic-update-slice_fusion.4
  27.4 34.5 %all-to-all-done.refs_0_ = bf16[16,64,1408]{2,1,0:T(8,128)(2,1)S(1)} async-done(((bf16[16,64,1408]{2,1,0:T(8,128)(2,1)}), bf16[16,64,1408]{2,1,0:T(8,128)(2,1)S(1)}, u32[]{:S(2)}, u32[]{:S(2)}) %all-to-all-start) | async-done | bytes 2883616 | tf_op jit(solution)/shard_map/all_to_all | solution.py:104
  61.9 1.6 copy-done
  67.1 2.2 collective-permute-done.1.refs_1_.refs_25_.refs_17_
  69.3 1.5 copy-done.1
  70.8 6.3 %shard_map.300 = (bf16[128,2048]{1,0:T(8,128)(2,1)}, bf16[128,512]{1,0:T(8,128)(2,1)}, bf16[512,128]{1,0:T(8,128)(2,1)}, bf16[8,128,640]{2,1,0:T(8,128)(2,1)}, f...) custom-call(s32[7]{0:T(128)} %concatenate.21.info.refs_0_, bf16[128,2048]{1,0:T(8,128)(2,1)} %tok.3, ...), custom_call_target="tpu_custom_call" | custom-call | flops 1476395008 | bytes 8914972 | tf_op jit(solution)/shard_map/pallas_call | solution.py:91
  77.1 4.1 all-to-all-start.1
  81.3 2.0 collective-permute-start.2
  83.3 2.7 collective-permute-start.3
  86.4 25.8 %collective-permute-done.2 = bf16[2,3,64,512]{3,2,1,0:T(8,128)(2,1)S(1)} collective-permute-done((bf16[2,3,64,512]{3,2,1,0:T(8,128)(2,1)}, bf16[2,3,64,512]{3,2,1,0:T(8,128)(2,1)S(1)}, u32[]{:S(2)}, u32[]{:S(2)}) %collective-permute-start.2) | collective-permute-done | bytes 393248 | tf_op jit(solution)/shard_map/ppermute | solution.py:36
  112.2 6.9 %collective-permute-done.3 = bf16[2,3,64,512]{3,2,1,0:T(8,128)(2,1)} collective-permute-done((bf16[2,3,64,512]{3,2,1,0:T(8,128)(2,1)}, bf16[2,3,64,512]{3,2,1,0:T(8,128)(2,1)}, u32[]{:S(2)}, u32[]{:S(2)}) %collective-permute-start.3) | collective-permute-done | bytes 393248 | tf_op jit(solution)/shard_map/ppermute | solution.py:36
  125.4 3.0 collective-permute-start.6
  129.1 12.5 %shard_map.305 = (bf16[512,2048]{1,0:T(8,128)(2,1)}, bf16[512,640]{1,0:T(8,128)(2,1)}, bf16[512,512]{1,0:T(8,128)(2,1)}, bf16[128,512]{1,0:T(8,128)(2,1)}, bf16[4,32,2048]{2,1,0:T(8,128)(2,1)}) custom-call(s32[7]{0:T(128)} %concatenate.21.info.refs_0_, bf16[128,512]{1,0:T(8,128)(2,1)} %get-tuple-element.70.qn.refs_9_, ...), custom_call_target="tpu_custom_call" | custom-call | flops 9663676416 | bytes 9961500 | tf_op jit(solution)/shard_map/pallas_call | solution.py:91
  141.6 5.6 %all-to-all-start.2 = ((bf16[4,32,2048]{2,1,0:T(8,128)(2,1)}), bf16[4,32,2048]{2,1,0:T(8,128)(2,1)S(1)}, u32[]{:S(2)}, u32[]{:S(2)}) async-start(bf16[4,32,2048]{2,1,0:T(8,128)(2,1)} %get-tuple-element.79), calls=%async_computation.2 | async-start | bytes 1048576 | tf_op jit(solution)/shard_map/all_to_all | solution.py:104
  147.3 16.3 %collective-permute-done.6.refs_1_.refs_4_ = bf16[8,3,64,512]{3,2,1,0:T(8,128)(2,1)S(1)} collective-permute-done((bf16[8,3,64,512]{3,2,1,0:T(8,128)(2,1)}, bf16[8,3,64,512]{3,2,1,0:T(8,128)(2,1)S(1)}, u32[]{:S(2)}, u32[]{:S(2)}) %collective-permute-start.6) | collective-permute-done | bytes 1572896 | tf_op jit(solution)/shard_map/ppermute | solution.py:36
  163.6 2.8 collective-permute-done.7.refs_2_.refs_6_
  167.2 2.8 shard_map.307
  170.0 6.4 %all-to-all-start.3 = ((bf16[16,32,2048]{2,1,0:T(8,128)(2,1)}), bf16[16,32,2048]{2,1,0:T(8,128)(2,1)S(1)}, u32[]{:S(2)}, u32[]{:S(2)}) async-start(bf16[16,32,2048]{2,1,0:T(8,128)(2,1)} %get-tuple-element.81), calls=%async_computation.3 | async-start | bytes 4194304 | tf_op jit(solution)/shard_map/all_to_all | solution.py:104
  176.5 3.0 collective-permute-start.11
  179.4 34.7 %collective-permute-done.11.refs_1_.refs_5_ = bf16[8,3,64,512]{3,2,1,0:T(8,128)(2,1)} collective-permute-done((bf16[8,3,64,512]{3,2,1,0:T(8,128)(2,1)}, bf16[8,3,64,512]{3,2,1,0:T(8,128)(2,1)}, u32[]{:S(2)}, u32[]{:S(2)}) %collective-permute-start.11) | collective-permute-done | bytes 1572896 | tf_op jit(solution)/shard_map/ppermute | solution.py:36
  215.5 4.4 collective-permute-done.12.refs_1_.refs_2_
  221.3 25.7 %shard_map.309 = (bf16[1024,512]{1,0:T(8,128)(2,1)}, bf16[1024,512]{1,0:T(8,128)(2,1)}, bf16[1024,512]{1,0:T(8,128)(2,1)}, bf16[512,4224]{1,0:T(8,128)(2,1)}, bf16[512,4224]{1,0:T(8,128)(2,1)}) custom-call(s32[7]{0:T(128)} %concatenate.21.info.refs_0_, bf16[16,32,2048]{2,1,0:T(8,128)(2,1)} %shard_map.308.refs_0_.refs_1_, bf16[16,32,2048]{2,1,0:T(8,128)(2,1)} %copy-done.40, ...), custom_call_target="tpu_custom_call" | custom-call | flops 25769803776 | bytes 26738716 | tf_op jit(solution)/shard_map/pallas_call | solution.py:91
  247.2 7.4 %collective-permute-done.13 = bf16[512,4224]{1,0:T(8,128)(2,1)S(1)} collective-permute-done((bf16[512,4224]{1,0:T(8,128)(2,1)}, bf16[512,4224]{1,0:T(8,128)(2,1)S(1)}, u32[]{:S(2)}, u32[]{:S(2)}) %collective-permute-start.13) | collective-permute-done | bytes 4325408 | tf_op jit(solution)/shard_map/ppermute | solution.py:36
  254.6 5.4 %add_convert_fusion.refs_7_ = bf16[512,4224]{1,0:T(8,128)(2,1)} fusion(bf16[512,4224]{1,0:T(8,128)(2,1)S(1)} %collective-permute-done.13, bf16[512,4224]{1,0:T(8,128)(2,1)} %get-tuple-element.82), kind=kLoop, calls=%fused_computation | loop fusion | flops 8650752 | bytes 12976128 | tf_op jit(solution)/shard_map/convert_element_type | solution.py:47
  260.0 6.9 %all-to-all-start.4 = ((bf16[16,32,4224]{2,1,0:T(8,128)(2,1)}), bf16[16,32,4224]{2,1,0:T(8,128)(2,1)}, u32[]{:S(2)}, u32[]{:S(2)}) async-start(bf16[16,32,4224]{2,1,0:T(8,128)(2,1)} %bitcast.47), calls=%async_computation.4 | async-start | bytes 8650752 | tf_op jit(solution)/shard_map/all_to_all | solution.py:104
  266.9 16.3 %shard_map.310 = (bf16[4,2,3,64,512]{4,3,2,1,0:T(8,128)(2,1)}, bf16[4,2,3,64,512]{4,3,2,1,0:T(8,128)(2,1)}, bf16[4,2,3,64,512]{4,3,2,1,0:T(8,128)(2,1)}, bf16[4,2,3,64,512]{4,3,2,1,0:T(8,128)(2,1)}) custom-call(s32[7]{0:T(128)} %concatenate.21.info.refs_0_, bf16[16,32,2048]{2,1,0:T(8,128)(2,1)} %shard_map.308.refs_0_.refs_1_, ...), custom_call_target="tpu_custom_call" | custom-call | flops 12884901888 | bytes 18087964 | tf_op jit(solution)/shard_map/pallas_call | solution.py:91
  284.4 2.2 collective-permute-start.18
  286.5 3.1 collective-permute-start.10
  291.2 35.7 %all-to-all-done.4.refs_0_ = bf16[16,32,4224]{2,1,0:T(8,128)(2,1)} async-done(((bf16[16,32,4224]{2,1,0:T(8,128)(2,1)}), bf16[16,32,4224]{2,1,0:T(8,128)(2,1)}, u32[]{:S(2)}, u32[]{:S(2)}) %all-to-all-start.4) | async-done | bytes 4325408 | tf_op jit(solution)/shard_map/all_to_all | solution.py:104
  327.0 2.9 reduce_sum.50
  329.9 1.9 collective-permute-start.14
  333.0 1.7 collective-permute-start.16
  335.5 2.9 collective-permute-start.19
  339.5 4.8 collective-permute-done.15.refs_19_.refs_14_
  344.3 2.6 collective-permute-done.16.refs_20_.refs_15_
  347.0 21.8 %shard_map.312 = (f32[128,2048]{1,0:T(8,128)}, f32[16,2048]{1,0:T(8,128)}, bf16[8,128,640]{2,1,0:T(8,128)(2,1)}, bf16[8,128,640]{2,1,0:T(8,128)(2,1)}, bf16[1,32...) custom-call(s32[7]{0:T(128)} %concatenate.21.info.refs_0_, ...), custom_call_target="tpu_custom_call" | custom-call | flops 19327352832 | bytes 29073436 | tf_op jit(solution)/shard_map/pallas_call | solution.py:91
  368.7 3.6 collective-permute-done.19.refs_1_
  373.7 3.2 collective-permute-done.20
  378.6 5.7 %collective-permute-done.31 = bf16[16,64,1536]{2,1,0:T(8,128)(2,1)S(1)} collective-permute-done((bf16[16,64,1536]{2,1,0:T(8,128)(2,1)}, bf16[16,64,1536]{2,1,0:T(8,128)(2,1)S(1)}, u32[]{:S(2)}, u32[]{:S(2)}) %collective-permute-start.31) | collective-permute-done | bytes 3145760 | tf_op jit(solution)/shard_map/ppermute | solution.py:36
  384.3 2.6 add_convert_fusion.1
  387.0 15.4 %all-to-all-start.5 = ((bf16[32,32,640]{2,1,0:T(8,128)(2,1)}), bf16[32,32,640]{2,1,0:T(8,128)(2,1)S(1)}, u32[]{:S(2)}, u32[]{:S(2)}) async-start(bf16[32,32,640]{2,1,0:T(8,128)(2,1)} %bitcast.22.refs_1_), calls=%async_computation.5 | async-start | bytes 2621440 | tf_op jit(solution)/shard_map/all_to_all | solution.py:104
  402.5 1.9 collective-permute-start.24
  404.3 2.7 collective-permute-start.25
  407.2 11.1 %collective-permute-done.24 = bf16[1,32,2048]{2,1,0:T(8,128)(2,1)S(1)} collective-permute-done((bf16[1,32,2048]{2,1,0:T(8,128)(2,1)S(1)}, bf16[1,32,2048]{2,1,0:T(8,128)(2,1)S(1)}, u32[]{:S(2)}, u32[]{:S(2)}) %collective-permute-start.24) | collective-permute-done | bytes 131104 | tf_op jit(solution)/shard_map/ppermute | solution.py:40
  418.4 3.3 collective-permute-done.25
  421.6 2.0 collective-permute-done.26
  423.8 4.2 collective-permute-start.28
  428.5 2.1 all-to-all-done.5
  432.1 2.4 collective-permute-start.22
  436.1 2.0 collective-permute-done.22.refs_2_
  438.0 2.1 collective-permute-done.23.refs_3_
  440.7 8.1 %shard_map.314 = (bf16[128,2048]{1,0:T(8,128)(2,1)}, f32[128,2048]{1,0:T(8,128)}, bf16[16,64,640]{2,1,0:T(8,128)(2,1)}, bf16[16,64,640]{2,1,0:T(8,128)(2,1)}) custom-call(s32[7]{0:T(128)} %concatenate.21.info.refs_0_, bf16[128,2048]{1,0:T(8,128)(2,1)} %tok.3, f32[128,2048]{1,0:T(8,128)} %get-tuple-element.90.gm, ...), custom_call_target="tpu_custom_call" | custom-call | flops 2684354560 | bytes 15173660 | tf_op jit(solution)/shard_map/pallas_call | solution.py:91
  449.0 3.8 fusion.2
  452.7 3.2 collective-permute-start.34
  456.9 2.8 add_convert_fusion.2
  459.7 6.9 %all-to-all-start.6 = ((bf16[16,64,640]{2,1,0:T(8,128)(2,1)}), bf16[16,64,640]{2,1,0:T(8,128)(2,1)S(1)}, u32[]{:S(2)}, u32[]{:S(2)}) async-start(bf16[16,64,640]{2,1,0:T(8,128)(2,1)} %add_convert_fusion.2), calls=%async_computation.6 | async-start | bytes 2621440 | tf_op jit(solution)/shard_map/all_to_all | solution.py:970
  466.6 14.4 %collective-permute-done.34.a3 = bf16[2,3,64,512]{3,2,1,0:T(8,128)(2,1)S(1)} collective-permute-done((bf16[2,3,64,512]{3,2,1,0:T(8,128)(2,1)}, bf16[2,3,64,512]{3,2,1,0:T(8,128)(2,1)S(1)}, u32[]{:S(2)}, u32[]{:S(2)}) %collective-permute-start.34) | collective-permute-done | bytes 393248 | tf_op jit(solution)/shard_map/ppermute | solution.py:36
  481.7 2.3 collective-permute-done.35.b
  484.9 3.8 shard_map.320
  488.7 13.6 %all-to-all-done.6 = bf16[16,64,640]{2,1,0:T(8,128)(2,1)S(1)} async-done(((bf16[16,64,640]{2,1,0:T(8,128)(2,1)}), bf16[16,64,640]{2,1,0:T(8,128)(2,1)S(1)}, u32[]{:S(2)}, u32[]{:S(2)}) %all-to-all-start.6) | async-done | bytes 1310752 | tf_op jit(solution)/shard_map/all_to_all | solution.py:970
  504.4 1.8 shard_map.316
  (183 shorter events, 36.3 us)
Async XLA Ops:
  10.0 8.0 %copy-start.38 = (bf16[64,8]{0,1:T(8,128)(2,1)S(1)}, bf16[64,8]{0,1:T(8,128)(2,1)}, u32[]{:S(2)}) copy-start(bf16[64,8]{0,1:T(8,128)(2,1)} %param.29) | copy-start | bytes 3076
  10.0 8.7 %copy-start.39 = (s32[1,3]{1,0:T(1,128)S(1)}, s32[1,3]{1,0:T(1,128)}, u32[]{:S(2)}) copy-start(s32[1,3]{1,0:T(1,128)} %param.19) | copy-start | bytes 40
  10.0 51.8 %all-to-all-start = ((bf16[16,64,1408]{2,1,0:T(8,128)(2,1)}), bf16[16,64,1408]{2,1,0:T(8,128)(2,1)S(1)}, u32[]{:S(2)}, u32[]{:S(2)}) async-start(bf16[16,64,1408]{2,1,0:T(8,128)(2,1)} %get-tuple-element.66), calls=%async_computation | async-start | bytes 5767168 | tf_op jit(solution)/shard_map/all_to_all | solution.py:104
  17.3 111.8 %all-gather.6.cloned.1.call-start = ((), (), s32[]{:S(2)}) async-start(), calls=%async_computation.10 | async-start | bytes 3244032 | tf_op jit(solution)/shard_map/all_gather | solution.py:902
  22.1 2.6 collective-permute-start
  63.5 5.8 %collective-permute-start.1 = (bf16[16,64,1408]{2,1,0:T(8,128)(2,1)}, bf16[16,64,1408]{2,1,0:T(8,128)(2,1)S(1)}, u32[]{:S(2)}, u32[]{:S(2)}) collective-permute-start(bf16[16,64,1408]{2,1,0:T(8,128)(2,1)} %shard_map.299.refs_0_.refs_1_.refs_24_.refs_16_), channel_id=1, source_target_pairs={{0,4},{4,0},{8,12},{12,8},{16,20},{20,16},{24,28},{28,24},{32,36},... | collective-permute-start | bytes 8650760 | tf_op jit(solution)/shard_map/ppermute | solution.py:36
  77.1 43.1 %all-to-all-start.1 = ((bf16[8,128,640]{2,1,0:T(8,128)(2,1)}), bf16[8,128,640]{2,1,0:T(8,128)(2,1)S(1)}, u32[]{:S(2)}, u32[]{:S(2)}) async-start(bf16[8,128,640]{2,1,0:T(8,128)(2,1)} %get-tuple-element.72), calls=%async_computation.1 | async-start | bytes 2621440 | tf_op jit(solution)/shard_map/all_to_all | solution.py:104
  81.3 138.6 %all-gather.4.cloned.1.call-start = ((), (), s32[]{:S(2)}) async-start(), calls=%async_computation.8 | async-start | bytes 5013504 | tf_op jit(solution)/shard_map/all_gather | solution.py:929
  81.3 30.9 %collective-permute-start.2 = (bf16[2,3,64,512]{3,2,1,0:T(8,128)(2,1)}, bf16[2,3,64,512]{3,2,1,0:T(8,128)(2,1)S(1)}, u32[]{:S(2)}, u32[]{:S(2)}) collective-permute-start(bf16[2,3,64,512]{3,2,1,0:T(8,128)(2,1)} %shard_map.301), channel_id=1, source_target_pairs={{0,8},{4,12},{8,0},{12,4},{16,24},{20,28},{24,16},{28,20},{32,40},... | collective-permute-start | bytes 1179656 | tf_op jit(solution)/shard_map/ppermute | solution.py:36
  83.3 35.8 %collective-permute-start.3 = (bf16[2,3,64,512]{3,2,1,0:T(8,128)(2,1)}, bf16[2,3,64,512]{3,2,1,0:T(8,128)(2,1)}, u32[]{:S(2)}, u32[]{:S(2)}) collective-permute-start(bf16[2,3,64,512]{3,2,1,0:T(8,128)(2,1)} %shard_map.302), channel_id=1, source_target_pairs={{0,16},{4,20},{8,24},{12,28},{16,0},{20,4},{24,8},{28,12},{32,48},... | collective-permute-start | bytes 1179656 | tf_op jit(solution)/shard_map/ppermute | solution.py:36
  86.2 26.0 %copy-start.12 = (bf16[8,3,64,512]{3,2,1,0:T(8,128)(2,1)S(1)}, bf16[8,3,64,512]{3,2,1,0:T(8,128)(2,1)}, u32[]{:S(2)}) copy-start(bf16[8,3,64,512]{3,2,1,0:T(8,128)(2,1)} %get-tuple-element.120) | copy-start | bytes 4718596
  86.2 34.0 %collective-permute-start.4 = (bf16[2,3,64,512]{3,2,1,0:T(8,128)(2,1)}, bf16[2,3,64,512]{3,2,1,0:T(8,128)(2,1)S(1)}, u32[]{:S(2)}, u32[]{:S(2)}) collective-permute-start(bf16[2,3,64,512]{3,2,1,0:T(8,128)(2,1)} %shard_map.303), channel_id=1, source_target_pairs={{0,24},{4,28},{8,16},{12,20},{16,8},{20,12},{24,0},{28,4},{32,56},... | collective-permute-start | bytes 1179656 | tf_op jit(solution)/shard_map/ppermute | solution.py:36
  125.3 3.8 collective-permute-start.5
  125.4 38.2 %collective-permute-start.6 = (bf16[8,3,64,512]{3,2,1,0:T(8,128)(2,1)}, bf16[8,3,64,512]{3,2,1,0:T(8,128)(2,1)S(1)}, u32[]{:S(2)}, u32[]{:S(2)}) collective-permute-start(bf16[8,3,64,512]{3,2,1,0:T(8,128)(2,1)} %copy-done.13), channel_id=1, source_target_pairs={{0,64},{4,68},{8,72},{12,76},{16,80},{20,84},{24,88},{28,92},{32,9... | collective-permute-start | bytes 4718600 | tf_op jit(solution)/shard_map/ppermute | solution.py:36
  128.4 38.0 %collective-permute-start.7 = (bf16[8,3,64,512]{3,2,1,0:T(8,128)(2,1)}, bf16[8,3,64,512]{3,2,1,0:T(8,128)(2,1)}, u32[]{:S(2)}, u32[]{:S(2)}) collective-permute-start(bf16[8,3,64,512]{3,2,1,0:T(8,128)(2,1)} %copy-done.13), channel_id=1, source_target_pairs={{0,96},{4,100},{8,104},{12,108},{16,112},{20,116},{24,120},{28,124... | collective-permute-start | bytes 4718600 | tf_op jit(solution)/shard_map/ppermute | solution.py:36
  141.6 24.8 %all-to-all-start.2 = ((bf16[4,32,2048]{2,1,0:T(8,128)(2,1)}), bf16[4,32,2048]{2,1,0:T(8,128)(2,1)S(1)}, u32[]{:S(2)}, u32[]{:S(2)}) async-start(bf16[4,32,2048]{2,1,0:T(8,128)(2,1)} %get-tuple-element.79), calls=%async_computation.2 | async-start | bytes 1048576 | tf_op jit(solution)/shard_map/all_to_all | solution.py:104
  170.0 44.1 %all-to-all-start.3 = ((bf16[16,32,2048]{2,1,0:T(8,128)(2,1)}), bf16[16,32,2048]{2,1,0:T(8,128)(2,1)S(1)}, u32[]{:S(2)}, u32[]{:S(2)}) async-start(bf16[16,32,2048]{2,1,0:T(8,128)(2,1)} %get-tuple-element.81), calls=%async_computation.3 | async-start | bytes 4194304 | tf_op jit(solution)/shard_map/all_to_all | solution.py:104
  176.5 37.7 %collective-permute-start.11 = (bf16[8,3,64,512]{3,2,1,0:T(8,128)(2,1)}, bf16[8,3,64,512]{3,2,1,0:T(8,128)(2,1)}, u32[]{:S(2)}, u32[]{:S(2)}) collective-permute-start(bf16[8,3,64,512]{3,2,1,0:T(8,128)(2,1)} %copy-done.13), channel_id=1, source_target_pairs={{0,32},{4,36},{8,40},{12,44},{16,48},{20,52},{24,56},{28,60},{32,0... | collective-permute-start | bytes 4718600 | tf_op jit(solution)/shard_map/ppermute | solution.py:36
  215.5 4.4 collective-permute-start.12
  247.0 7.6 %collective-permute-start.13 = (bf16[512,4224]{1,0:T(8,128)(2,1)}, bf16[512,4224]{1,0:T(8,128)(2,1)S(1)}, u32[]{:S(2)}, u32[]{:S(2)}) collective-permute-start(bf16[512,4224]{1,0:T(8,128)(2,1)} %get-tuple-element.83), channel_id=1, source_target_pairs={{0,4},{4,0},{8,12},{12,8},{16,20},{20,16},{24,28},{28,24},{32,36},... | collective-permute-start | bytes 12976136 | tf_op jit(solution)/shard_map/ppermute | solution.py:36
  260.0 67.0 %all-to-all-start.4 = ((bf16[16,32,4224]{2,1,0:T(8,128)(2,1)}), bf16[16,32,4224]{2,1,0:T(8,128)(2,1)}, u32[]{:S(2)}, u32[]{:S(2)}) async-start(bf16[16,32,4224]{2,1,0:T(8,128)(2,1)} %bitcast.47), calls=%async_computation.4 | async-start | bytes 8650752 | tf_op jit(solution)/shard_map/all_to_all | solution.py:104
  266.9 237.5 %reduce-scatter.2.cloned.1.call-start = ((), (), s32[]{:S(2)}) async-start(), calls=%async_computation.9 | async-start | bytes 3342336 | tf_op jit(solution)/shard_map/reduce_scatter | solution.py:956
  266.9 19.6 %copy-start.26 = (bf16[1,32,2048]{2,1,0:T(8,128)(2,1)S(1)}, bf16[1,32,2048]{2,1,0:T(8,128)(2,1)}, u32[]{:S(2)}) copy-start(bf16[1,32,2048]{2,1,0:T(8,128)(2,1)} %get-tuple-element.80.refs_13_.refs_8_) | copy-start | bytes 393220
  283.3 52.2 %collective-permute-start.17 = (bf16[4,2,3,64,512]{4,3,2,1,0:T(8,128)(2,1)}, bf16[4,2,3,64,512]{4,3,2,1,0:T(8,128)(2,1)S(1)}, u32[]{:S(2)}, u32[]{:S(2)}) collective-permute-start(bf16[4,2,3,64,512]{4,3,2,1,0:T(8,128)(2,1)} %get-tuple-element.88), channel_id=1, source_target_pairs={{0,64},{4,68},{8,72},{12,76},{16,80},{20,84},{24,88},{28,92},{32,9... | collective-permute-start | bytes 4718600 | tf_op jit(solution)/shard_map/ppermute | solution.py:36
  284.4 54.0 %collective-permute-start.18 = (bf16[4,2,3,64,512]{4,3,2,1,0:T(8,128)(2,1)}, bf16[4,2,3,64,512]{4,3,2,1,0:T(8,128)(2,1)}, u32[]{:S(2)}, u32[]{:S(2)}) collective-permute-start(bf16[4,2,3,64,512]{4,3,2,1,0:T(8,128)(2,1)} %get-tuple-element.89), channel_id=1, source_target_pairs={{0,96},{4,100},{8,104},{12,108},{16,112},{20,116},{24,120},{28,124... | collective-permute-start | bytes 4718600 | tf_op jit(solution)/shard_map/ppermute | solution.py:36
  286.5 43.3 %collective-permute-start.10 = (bf16[1,32,2048]{2,1,0:T(8,128)(2,1)S(1)}, bf16[1,32,2048]{2,1,0:T(8,128)(2,1)S(1)}, u32[]{:S(2)}, u32[]{:S(2)}) collective-permute-start(bf16[1,32,2048]{2,1,0:T(8,128)(2,1)S(1)} %copy-done.26), channel_id=1, source_target_pairs={{0,3},{1,2},{2,1},{3,0},{4,7},{5,6},{6,5},{7,4},{8,11},{9,10},{10,... | collective-permute-start | bytes 393224 | tf_op jit(solution)/shard_map/ppermute | solution.py:40
  289.6 42.1 %collective-permute-start.8 = (bf16[1,32,2048]{2,1,0:T(8,128)(2,1)S(1)}, bf16[1,32,2048]{2,1,0:T(8,128)(2,1)S(1)}, u32[]{:S(2)}, u32[]{:S(2)}) collective-permute-start(bf16[1,32,2048]{2,1,0:T(8,128)(2,1)S(1)} %copy-done.26), channel_id=1, source_target_pairs={{0,1},{1,0},{2,3},{3,2},{4,5},{5,4},{6,7},{7,6},{8,9},{9,8},{10,11... | collective-permute-start | bytes 393224 | tf_op jit(solution)/shard_map/ppermute | solution.py:40
  289.8 43.2 %collective-permute-start.9 = (bf16[1,32,2048]{2,1,0:T(8,128)(2,1)S(1)}, bf16[1,32,2048]{2,1,0:T(8,128)(2,1)S(1)}, u32[]{:S(2)}, u32[]{:S(2)}) collective-permute-start(bf16[1,32,2048]{2,1,0:T(8,128)(2,1)S(1)} %copy-done.26), channel_id=1, source_target_pairs={{0,2},{1,3},{2,0},{3,1},{4,6},{5,7},{6,4},{7,5},{8,10},{9,11},{10,... | collective-permute-start | bytes 393224 | tf_op jit(solution)/shard_map/ppermute | solution.py:40
  329.9 17.1 %copy-start.18 = (bf16[32,4224]{1,0:T(8,128)(2,1)}, bf16[32,4224]{1,0:T(8,128)(2,1)S(1)}, u32[]{:S(2)}) copy-start(bf16[32,4224]{1,0:T(8,128)(2,1)S(1)} %reduce_sum.50) | copy-start | bytes 811012
  329.9 5.6 %copy-start.27 = (bf16[1,32,2048]{2,1,0:T(8,128)(2,1)}, bf16[1,32,2048]{2,1,0:T(8,128)(2,1)S(1)}, u32[]{:S(2)}) copy-start(bf16[1,32,2048]{2,1,0:T(8,128)(2,1)S(1)} %collective-permute-done.10.refs_16_.refs_11_) | copy-start | bytes 393220
  329.9 9.6 %collective-permute-start.14 = (bf16[1,32,4224]{2,1,0:T(8,128)(2,1)S(1)}, bf16[1,32,4224]{2,1,0:T(8,128)(2,1)}, u32[]{:S(2)}, u32[]{:S(2)}) collective-permute-start(bf16[1,32,4224]{2,1,0:T(8,128)(2,1)S(1)} %bitcast.57), channel_id=1, source_target_pairs={{0,1},{1,0},{2,3},{3,2},{4,5},{5,4},{6,7},{7,6},{8,9},{9,8},{10,11... | collective-permute-start | bytes 811016 | tf_op jit(solution)/shard_map/ppermute | solution.py:40
  331.8 12.6 %collective-permute-start.15 = (bf16[1,32,4224]{2,1,0:T(8,128)(2,1)S(1)}, bf16[1,32,4224]{2,1,0:T(8,128)(2,1)}, u32[]{:S(2)}, u32[]{:S(2)}) collective-permute-start(bf16[1,32,4224]{2,1,0:T(8,128)(2,1)S(1)} %bitcast.58), channel_id=1, source_target_pairs={{0,2},{1,3},{2,0},{3,1},{4,6},{5,7},{6,4},{7,5},{8,10},{9,11},{10,... | collective-permute-start | bytes 811016 | tf_op jit(solution)/shard_map/ppermute | solution.py:40
  333.0 13.9 %collective-permute-start.16 = (bf16[1,32,4224]{2,1,0:T(8,128)(2,1)S(1)}, bf16[1,32,4224]{2,1,0:T(8,128)(2,1)}, u32[]{:S(2)}, u32[]{:S(2)}) collective-permute-start(bf16[1,32,4224]{2,1,0:T(8,128)(2,1)S(1)} %bitcast.59), channel_id=1, source_target_pairs={{0,3},{1,2},{2,1},{3,0},{4,7},{5,6},{6,5},{7,4},{8,11},{9,10},{10,... | collective-permute-start | bytes 811016 | tf_op jit(solution)/shard_map/ppermute | solution.py:40
  335.5 11.4 %copy-start.15 = (bf16[4,2,3,64,512]{4,3,2,1,0:T(8,128)(2,1)}, bf16[4,2,3,64,512]{4,3,2,1,0:T(8,128)(2,1)S(1)}, u32[]{:S(2)}) copy-start(bf16[4,2,3,64,512]{4,3,2,1,0:T(8,128)(2,1)S(1)} %collective-permute-done.17.refs_26_) | copy-start | bytes 4718596
  335.5 36.8 %collective-permute-start.19 = (bf16[4,2,3,64,512]{4,3,2,1,0:T(8,128)(2,1)}, bf16[4,2,3,64,512]{4,3,2,1,0:T(8,128)(2,1)S(1)}, u32[]{:S(2)}, u32[]{:S(2)}) collective-permute-start(bf16[4,2,3,64,512]{4,3,2,1,0:T(8,128)(2,1)} %get-tuple-element.96), channel_id=1, source_target_pairs={{0,32},{4,36},{8,40},{12,44},{16,48},{20,52},{24,56},{28,60},{32,0... | collective-permute-start | bytes 4718600 | tf_op jit(solution)/shard_map/ppermute | solution.py:36
  373.5 3.5 collective-permute-start.20
  378.4 5.9 %copy-start.9 = (bf16[16,64,1536]{2,1,0:T(8,128)(2,1)S(1)}, bf16[16,64,1536]{2,1,0:T(8,128)(2,1)}, u32[]{:S(2)}) copy-start(bf16[16,64,1536]{2,1,0:T(8,128)(2,1)} %get-tuple-element.105) | copy-start | bytes 9437188
  378.4 5.9 %collective-permute-start.31 = (bf16[16,64,1536]{2,1,0:T(8,128)(2,1)}, bf16[16,64,1536]{2,1,0:T(8,128)(2,1)S(1)}, u32[]{:S(2)}, u32[]{:S(2)}) collective-permute-start(bf16[16,64,1536]{2,1,0:T(8,128)(2,1)} %shard_map.315), channel_id=1, source_target_pairs={{0,4},{4,0},{8,12},{12,8},{16,20},{20,16},{24,28},{28,24},{32,36},... | collective-permute-start | bytes 9437192 | tf_op jit(solution)/shard_map/ppermute | solution.py:36
  387.0 15.5 %copy-start.43 = (bf16[1,32,2048]{2,1,0:T(8,128)(2,1)S(1)}, bf16[1,32,2048]{2,1,0:T(8,128)(2,1)}, u32[]{:S(2)}) copy-start(bf16[1,32,2048]{2,1,0:T(8,128)(2,1)} %get-tuple-element.98) | copy-start | bytes 393220
  387.0 17.4 %copy-start.42 = (bf16[1,32,2048]{2,1,0:T(8,128)(2,1)S(1)}, bf16[1,32,2048]{2,1,0:T(8,128)(2,1)}, u32[]{:S(2)}) copy-start(bf16[1,32,2048]{2,1,0:T(8,128)(2,1)} %get-tuple-element.99) | copy-start | bytes 393220
  387.0 20.0 %copy-start.41 = (bf16[1,32,2048]{2,1,0:T(8,128)(2,1)S(1)}, bf16[1,32,2048]{2,1,0:T(8,128)(2,1)}, u32[]{:S(2)}) copy-start(bf16[1,32,2048]{2,1,0:T(8,128)(2,1)} %get-tuple-element.100) | copy-start | bytes 393220
  387.0 36.7 %copy-start.33 = (bf16[1,32,2048]{2,1,0:T(8,128)(2,1)S(1)}, bf16[1,32,2048]{2,1,0:T(8,128)(2,1)}, u32[]{:S(2)}) copy-start(bf16[1,32,2048]{2,1,0:T(8,128)(2,1)} %get-tuple-element.97) | copy-start | bytes 393220
  387.0 43.6 %all-to-all-start.5 = ((bf16[32,32,640]{2,1,0:T(8,128)(2,1)}), bf16[32,32,640]{2,1,0:T(8,128)(2,1)S(1)}, u32[]{:S(2)}, u32[]{:S(2)}) async-start(bf16[32,32,640]{2,1,0:T(8,128)(2,1)} %bitcast.22.refs_1_), calls=%async_computation.5 | async-start | bytes 2621440 | tf_op jit(solution)/shard_map/all_to_all | solution.py:104
  402.5 15.9 %collective-permute-start.24 = (bf16[1,32,2048]{2,1,0:T(8,128)(2,1)S(1)}, bf16[1,32,2048]{2,1,0:T(8,128)(2,1)S(1)}, u32[]{:S(2)}, u32[]{:S(2)}) collective-permute-start(bf16[1,32,2048]{2,1,0:T(8,128)(2,1)S(1)} %copy-done.43), channel_id=1, source_target_pairs={{0,1},{1,0},{2,3},{3,2},{4,5},{5,4},{6,7},{7,6},{8,9},{9,8},{10,11... | collective-permute-start | bytes 393224 | tf_op jit(solution)/shard_map/ppermute | solution.py:40
  404.3 17.3 %collective-permute-start.25 = (bf16[1,32,2048]{2,1,0:T(8,128)(2,1)S(1)}, bf16[1,32,2048]{2,1,0:T(8,128)(2,1)S(1)}, u32[]{:S(2)}, u32[]{:S(2)}) collective-permute-start(bf16[1,32,2048]{2,1,0:T(8,128)(2,1)S(1)} %copy-done.42), channel_id=1, source_target_pairs={{0,2},{1,3},{2,0},{3,1},{4,6},{5,7},{6,4},{7,5},{8,10},{9,11},{10,... | collective-permute-start | bytes 393224 | tf_op jit(solution)/shard_map/ppermute | solution.py:40
  407.0 16.7 %collective-permute-start.26 = (bf16[1,32,2048]{2,1,0:T(8,128)(2,1)S(1)}, bf16[1,32,2048]{2,1,0:T(8,128)(2,1)S(1)}, u32[]{:S(2)}, u32[]{:S(2)}) collective-permute-start(bf16[1,32,2048]{2,1,0:T(8,128)(2,1)S(1)} %copy-done.41), channel_id=1, source_target_pairs={{0,3},{1,2},{2,1},{3,0},{4,7},{5,6},{6,5},{7,4},{8,11},{9,10},{10,... | collective-permute-start | bytes 393224 | tf_op jit(solution)/shard_map/ppermute | solution.py:40
  423.7 16.4 %copy-start.23 = (bf16[1,32,2048]{2,1,0:T(8,128)(2,1)}, bf16[1,32,2048]{2,1,0:T(8,128)(2,1)S(1)}, u32[]{:S(2)}) copy-start(bf16[1,32,2048]{2,1,0:T(8,128)(2,1)S(1)} %add_convert_fusion.8.refs_4_) | copy-start | bytes 393220
  423.8 10.7 %collective-permute-start.27 = (bf16[1,32,2048]{2,1,0:T(8,128)(2,1)S(1)}, bf16[1,32,2048]{2,1,0:T(8,128)(2,1)S(1)}, u32[]{:S(2)}, u32[]{:S(2)}) collective-permute-start(bf16[1,32,2048]{2,1,0:T(8,128)(2,1)S(1)} %add_convert_fusion.8.refs_4_), channel_id=1, source_target_pairs={{0,1},{1,0},{2,3},{3,2},{4,5},{5,4},{6,7},{7,6},{8,9},{9,8},{10,11... | collective-permute-start | bytes 393224 | tf_op jit(solution)/shard_map/ppermute | solution.py:40
  423.8 11.8 %collective-permute-start.28 = (bf16[1,32,2048]{2,1,0:T(8,128)(2,1)S(1)}, bf16[1,32,2048]{2,1,0:T(8,128)(2,1)S(1)}, u32[]{:S(2)}, u32[]{:S(2)}) collective-permute-start(bf16[1,32,2048]{2,1,0:T(8,128)(2,1)S(1)} %add_convert_fusion.8.refs_4_), channel_id=1, source_target_pairs={{0,2},{1,3},{2,0},{3,1},{4,6},{5,7},{6,4},{7,5},{8,10},{9,11},{10,... | collective-permute-start | bytes 393224 | tf_op jit(solution)/shard_map/ppermute | solution.py:40
  428.0 8.0 %collective-permute-start.29 = (bf16[1,32,2048]{2,1,0:T(8,128)(2,1)S(1)}, bf16[1,32,2048]{2,1,0:T(8,128)(2,1)S(1)}, u32[]{:S(2)}, u32[]{:S(2)}) collective-permute-start(bf16[1,32,2048]{2,1,0:T(8,128)(2,1)S(1)} %add_convert_fusion.8.refs_4_), channel_id=1, source_target_pairs={{0,3},{1,2},{2,1},{3,0},{4,7},{5,6},{6,5},{7,4},{8,11},{9,10},{10,... | collective-permute-start | bytes 393224 | tf_op jit(solution)/shard_map/ppermute | solution.py:40
  430.8 9.3 %copy-start.11 = (f32[32,640]{1,0:T(8,128)}, f32[32,640]{1,0:T(8,128)S(1)}, u32[]{:S(2)}) copy-start(f32[32,640]{1,0:T(8,128)S(1)} %convert_reduce_fusion.1) | copy-start | bytes 245764
  430.8 5.2 %collective-permute-start.21 = (f32[1,32,640]{2,1,0:T(8,128)S(1)}, f32[1,32,640]{2,1,0:T(8,128)S(1)}, u32[]{:S(2)}, u32[]{:S(2)}) collective-permute-start(f32[1,32,640]{2,1,0:T(8,128)S(1)} %bitcast.50), channel_id=1, source_target_pairs={{0,1},{1,0},{2,3},{3,2},{4,5},{5,4},{6,7},{7,6},{8,9},{9,8},{10,11... | collective-permute-start | bytes 245768 | tf_op jit(solution)/shard_map/ppermute | solution.py:40
  432.1 5.9 %collective-permute-start.22 = (f32[1,32,640]{2,1,0:T(8,128)S(1)}, f32[1,32,640]{2,1,0:T(8,128)S(1)}, u32[]{:S(2)}, u32[]{:S(2)}) collective-permute-start(f32[1,32,640]{2,1,0:T(8,128)S(1)} %bitcast.51), channel_id=1, source_target_pairs={{0,2},{1,3},{2,0},{3,1},{4,6},{5,7},{6,4},{7,5},{8,10},{9,11},{10,... | collective-permute-start | bytes 245768 | tf_op jit(solution)/shard_map/ppermute | solution.py:40
  434.5 5.7 %copy-start.30 = (bf16[1,32,2048]{2,1,0:T(8,128)(2,1)}, bf16[1,32,2048]{2,1,0:T(8,128)(2,1)S(1)}, u32[]{:S(2)}) copy-start(bf16[1,32,2048]{2,1,0:T(8,128)(2,1)S(1)} %collective-permute-done.27.refs_5_) | copy-start | bytes 393220
  434.5 5.7 %collective-permute-start.23 = (f32[1,32,640]{2,1,0:T(8,128)S(1)}, f32[1,32,640]{2,1,0:T(8,128)S(1)}, u32[]{:S(2)}, u32[]{:S(2)}) collective-permute-start(f32[1,32,640]{2,1,0:T(8,128)S(1)} %bitcast.52), channel_id=1, source_target_pairs={{0,3},{1,2},{2,1},{3,0},{4,7},{5,6},{6,5},{7,4},{8,11},{9,10},{10,... | collective-permute-start | bytes 245768 | tf_op jit(solution)/shard_map/ppermute | solution.py:40
  440.7 8.2 %copy-start.3 = (bf16[4,2,3,64,512]{4,3,2,1,0:T(8,128)(2,1)S(1)}, bf16[4,2,3,64,512]{4,3,2,1,0:T(8,128)(2,1)}, u32[]{:S(2)}) copy-start(bf16[4,2,3,64,512]{4,3,2,1,0:T(8,128)(2,1)} %get-tuple-element.87.refs_1_) | copy-start | bytes 4718596
  440.7 8.2 %copy-start.5 = (bf16[4,2,3,64,512]{4,3,2,1,0:T(8,128)(2,1)S(1)}, bf16[4,2,3,64,512]{4,3,2,1,0:T(8,128)(2,1)}, u32[]{:S(2)}) copy-start(bf16[4,2,3,64,512]{4,3,2,1,0:T(8,128)(2,1)} %copy-done.4) | copy-start | bytes 4718596
  448.9 8.1 %collective-permute-start.30 = (bf16[16,64,640]{2,1,0:T(8,128)(2,1)}, bf16[16,64,640]{2,1,0:T(8,128)(2,1)}, u32[]{:S(2)}, u32[]{:S(2)}) collective-permute-start(bf16[16,64,640]{2,1,0:T(8,128)(2,1)} %get-tuple-element.104), channel_id=1, source_target_pairs={{0,4},{4,0},{8,12},{12,8},{16,20},{20,16},{24,28},{28,24},{32,36},... | collective-permute-start | bytes 3932168 | tf_op jit(solution)/shard_map/ppermute | solution.py:36
  452.7 13.9 %copy-start.10 = (bf16[1,2,3,64,512]{4,3,2,1,0:T(8,128)(2,1)}, bf16[1,2,3,64,512]{4,3,2,1,0:T(8,128)(2,1)S(1)}, u32[]{:S(2)}) copy-start(bf16[1,2,3,64,512]{4,3,2,1,0:T(8,128)(2,1)S(1)} %get-tuple-element.119) | copy-start | bytes 1179652
  452.7 28.3 %collective-permute-start.34 = (bf16[2,3,64,512]{3,2,1,0:T(8,128)(2,1)}, bf16[2,3,64,512]{3,2,1,0:T(8,128)(2,1)S(1)}, u32[]{:S(2)}, u32[]{:S(2)}) collective-permute-start(bf16[2,3,64,512]{3,2,1,0:T(8,128)(2,1)} %shard_map.319), channel_id=1, source_target_pairs={{0,24},{4,28},{8,16},{12,20},{16,8},{20,12},{24,0},{28,4},{32,56},... | collective-permute-start | bytes 1179656 | tf_op jit(solution)/shard_map/ppermute | solution.py:36
  455.9 25.2 %collective-permute-start.33 = (bf16[2,3,64,512]{3,2,1,0:T(8,128)(2,1)}, bf16[2,3,64,512]{3,2,1,0:T(8,128)(2,1)S(1)}, u32[]{:S(2)}, u32[]{:S(2)}) collective-permute-start(bf16[2,3,64,512]{3,2,1,0:T(8,128)(2,1)} %shard_map.318), channel_id=1, source_target_pairs={{0,16},{4,20},{8,24},{12,28},{16,0},{20,4},{24,8},{28,12},{32,48},... | collective-permute-start | bytes 1179656 | tf_op jit(solution)/shard_map/ppermute | solution.py:36
  456.6 24.8 %collective-permute-start.32 = (bf16[2,3,64,512]{3,2,1,0:T(8,128)(2,1)}, bf16[2,3,64,512]{3,2,1,0:T(8,128)(2,1)S(1)}, u32[]{:S(2)}, u32[]{:S(2)}) collective-permute-start(bf16[2,3,64,512]{3,2,1,0:T(8,128)(2,1)} %shard_map.317), channel_id=1, source_target_pairs={{0,8},{4,12},{8,0},{12,4},{16,24},{20,28},{24,16},{28,20},{32,40},... | collective-permute-start | bytes 1179656 | tf_op jit(solution)/shard_map/ppermute | solution.py:36
  459.7 42.6 %all-to-all-start.6 = ((bf16[16,64,640]{2,1,0:T(8,128)(2,1)}), bf16[16,64,640]{2,1,0:T(8,128)(2,1)S(1)}, u32[]{:S(2)}, u32[]{:S(2)}) async-start(bf16[16,64,640]{2,1,0:T(8,128)(2,1)} %add_convert_fusion.2), calls=%async_computation.6 | async-start | bytes 2621440 | tf_op jit(solution)/shard_map/all_to_all | solution.py:970
  481.6 2.4 collective-permute-start.35
  (26 other events, 64.7 us)
Sparse Core Ops, SparseCore 0:
  20.4 88.8 all-gather.5
  125.4 36.4 all-gather.3
  387.1 112.8 reduce-scatter.1
